TPU v7x, 32 devices: a whole 2x2x4 slice. The times are simulated.
32 devices in a mesh: section: 4 (over z), dp: 8 (over y, x, core).
Axes of the slice: x: 2, y: 2, z: 4, core: 2. Of those that a mesh axis runs over, the one named last changes fastest.
Arguments:
- master: float32 [4, 2560, 2560], P('section', 'dp'), may hold values from -0.125 to 0.125
- first_moment: float32 [4, 2560, 2560], P('section', 'dp'), may hold values from -3 to 3
- second_moment: float32 [4, 2560, 2560], P('section', 'dp'), may hold values from 0.1 to 4
- inputs_own: bfloat16 [4, 4, 1024, 2560], P('section', None, 'dp'), may hold values from -6 to 6
- inputs_arriving: bfloat16 [4, 4, 1024, 2560], P('section', None, 'dp'), may hold values from -6 to 6
- grads_own: bfloat16 [4, 4, 1024, 2560], P('section', None, 'dp'), may hold values from -0.1875 to 0.1875
- windows_own: int32 [4, 1024, 2560], P('section', 'dp'), may hold values from 0 to 15
- windows_arriving: int32 [4, 1024, 2560], P('section', 'dp'), may hold values from 0 to 15
- next_inputs: bfloat16 [4, 256, 2560], P('section', 'dp'), may hold values from -6 to 6
Outputs:
- fresh_params: float32 [4, 2560, 2560], P('section', 'dp')
- fresh_first: float32 [4, 2560, 2560], P('section', 'dp')
- fresh_second: float32 [4, 2560, 2560], P('section', 'dp')
- next_currents: bfloat16 [4, 256, 2560], P('section', 'dp')
Inputs may be any that keep to these rules, and one draw needn't show every extreme that they name: `windows_own`: bit t of an entry is the surrogate derivative of spikes_t by v_t for timestep t. `windows_arriving`: bit t of an entry is the surrogate derivative of spikes_t by v_t for timestep t.
All inputs are finite; a program needn't handle non-finite values.
Results may differ from a plain program's by a relative error of at most 0.008.
Values may be sent and summed in bfloat16 or wider, within the bound.
No kernel may reach another device: no remote copies, remote signals or barrier semaphores. Data moves between devices by JAX's collectives and lax.ppermute only.
A program may use at most 128 MiB of HBM per device.

v0:
```python
import jax
import jax.numpy as jnp
from jax import lax
from jax.sharding import PartitionSpec as P

LEAK_RATE = 0.5
LEARN_RATE = 0.002
FIRST_DECAY = 0.9
SECOND_DECAY = 0.95
EPSILON = 1e-08
WEIGHT_DECAY = 0.1
FIRST_CORRECTION = 1.0 - 0.9**10
SECOND_CORRECTION = 1.0 - 0.95**10


def passed_along(shard, axis, by):
    count = lax.axis_size(axis)
    pairs = [(i, i + by) for i in range(count) if 0 <= i + by < count]
    return lax.ppermute(shard, axis, pairs)


def membrane_grads(gradients, windows):
    carried = jnp.zeros(gradients.shape[1:], jnp.float32)
    results = []
    for moment in reversed(range(gradients.shape[0])):
        window = jnp.bitwise_and(jnp.right_shift(windows, moment), 1).astype(jnp.float32)
        carried = window * gradients[moment].astype(jnp.float32) + LEAK_RATE * carried
        results = [carried] + results
    return jnp.stack(results).astype(jnp.bfloat16)


def shards(
    master,
    first_moment,
    second_moment,
    inputs_own,
    inputs_arriving,
    grads_own,
    windows_own,
    windows_arriving,
    next_inputs,
):
    params = master[0]
    timesteps, tok_rows, features = (grads_own.shape[1], grads_own.shape[2], grads_own.shape[3])
    flat_rows = timesteps * tok_rows
    membrane_own = membrane_grads(grads_own[0], windows_own[0]).reshape(flat_rows, features)
    through = lax.dot_general(
        membrane_own,
        lax.all_gather(params.astype(jnp.bfloat16), "dp", axis=0, tiled=True),
        (((1,), (1,)), ((), ())),
        preferred_element_type=jnp.float32,
    )
    outgoing = (grads_own[0].reshape(flat_rows, features).astype(jnp.float32) + through).astype(
        jnp.bfloat16
    )
    received = passed_along(outgoing.reshape(timesteps, tok_rows, features), "section", -1)
    membrane_arriving = membrane_grads(received, windows_arriving[0]).reshape(flat_rows, features)
    acts_own = inputs_own[0].reshape(flat_rows, features)
    acts_arriving = inputs_arriving[0].reshape(flat_rows, features)
    contract = (((0,), (0,)), ((), ()))
    partial_value = lax.dot_general(
        acts_own, membrane_own, contract, preferred_element_type=jnp.float32
    )
    gradient = lax.psum_scatter(
        (
            partial_value
            + lax.dot_general(
                acts_arriving, membrane_arriving, contract, preferred_element_type=jnp.float32
            )
        ).astype(jnp.bfloat16),
        "dp",
        scatter_dimension=0,
        tiled=True,
    ).astype(jnp.float32)
    fresh_first = FIRST_DECAY * first_moment[0] + (1.0 - FIRST_DECAY) * gradient
    fresh_second = SECOND_DECAY * second_moment[0] + (1.0 - SECOND_DECAY) * gradient * gradient
    direction = (
        fresh_first / FIRST_CORRECTION / (jnp.sqrt(fresh_second / SECOND_CORRECTION) + EPSILON)
    )
    fresh_params = params - LEARN_RATE * (direction + WEIGHT_DECAY * params)
    fresh_weights = fresh_params.astype(jnp.bfloat16)
    upcoming = next_inputs[0]
    currents = jnp.dot(
        upcoming,
        lax.all_gather(fresh_weights, "dp", axis=0, tiled=True),
        preferred_element_type=jnp.float32,
    )
    next_currents = currents.astype(jnp.bfloat16)
    return (fresh_params[None], fresh_first[None], fresh_second[None], next_currents[None])


def solution(mesh):
    return jax.shard_map(
        shards,
        mesh=mesh,
        in_specs=(
            P("section", "dp", None),
            P("section", "dp", None),
            P("section", "dp", None),
            P("section", None, "dp", None),
            P("section", None, "dp", None),
            P("section", None, "dp", None),
            P("section", "dp", None),
            P("section", "dp", None),
            P("section", "dp", None),
        ),
        out_specs=(
            P("section", "dp", None),
            P("section", "dp", None),
            P("section", "dp", None),
            P("section", "dp", None),
        ),
        check_vma=False,
    )
```

profile of v0, /device:TPU:0, one launch (start us, length us, event | category | flops | bytes accessed | tf_op | source)
XLA Modules:
  0.0 393.0 jit_solution(8821370254945144514)
XLA Ops:
  7.2 0.0 copy-start
  7.2 0.0 all-gather.3.cloned.1.call-start
  7.2 3.4 bitcast_convert_fusion
  10.6 0.0 all-gather.3.cloned.1.call-update
  10.7 0.0 reduce-scatter.4.cloned.1.call-start
  10.7 3.2 fusion.11
  13.9 1.8 maximum_convert_fusion
  15.8 72.1 %all-gather.3.cloned.1.call-done = bf16[2560,2560]{1,0:T(8,128)(2,1)} async-done(((bf16[320,2560]{1,0:T(8,128)(2,1)}), bf16[2560,2560]{1,0:T(8,128)(2,1)}) %all-gather.3.cloned.1.call-update) | async-done | bytes 13107216 | tf_op jit(solution)/shard_map/all_gather | solution.py:49
  87.9 0.0 copy-start.2
  87.9 13.9 %fusion.1 = bf16[512,2560]{1,0:T(8,128)(2,1)} fusion(bf16[512,2560]{1,0:T(8,128)(2,1)} %bitcast.80, bf16[512,2560]{1,0:T(8,128)(2,1)} %bitcast.81, bf16[2560,2560]{1,0:T(8,128)(2,1)} %all-gather.3.cloned.1.call-done), kind=kOutput, calls=%fused_computation.4 | convolution fusion | flops 6714818560 | bytes 20971520 | tf_op jit(solution)/shard_map/dot_general | solution.py:47
  101.8 1.5 collective-permute-start
  103.2 0.0 copy-done
  103.2 0.0 copy-done.2
  103.2 0.0 copy-start.3
  103.3 12.5 %fusion.17 = f32[2560,2560]{1,0:T(8,128)} fusion(bf16[512,2560]{1,0:T(8,128)(2,1)S(1)} %bitcast.82, bf16[512,2560]{1,0:T(8,128)(2,1)S(1)} %bitcast.78), kind=kOutput, calls=%fused_computation.35 | convolution fusion | flops 6710886400 | bytes 31457280 | tf_op jit(solution)/shard_map/dot_general | solution.py:61
  115.7 47.1 %collective-permute-done = bf16[4,128,2560]{2,1,0:T(8,128)(2,1)S(1)} collective-permute-done((bf16[4,128,2560]{2,1,0:T(8,128)(2,1)}, bf16[4,128,2560]{2,1,0:T(8,128)(2,1)S(1)}, u32[]{:S(2)}, u32[]{:S(2)}) %collective-permute-start) | collective-permute-done | bytes 2621472 | tf_op jit(solution)/shard_map/ppermute | solution.py:19
  162.9 0.0 copy-done.3
  162.9 1.2 add_convert_fusion.1
  164.0 1.8 pad_maximum_fusion
  165.9 16.4 %fusion = bf16[2560,2560]{0,1:T(8,128)(2,1)} fusion(f32[2560,2560]{1,0:T(8,128)} %fusion.17, bf16[512,2560]{1,0:T(8,128)(2,1)} %bitcast.83, bf16[512,2560]{1,0:T(8,128)(2,1)} %bitcast.84), kind=kOutput, calls=%fused_computation.1 | convolution fusion | flops 6723993600 | bytes 44564480 | tf_op jit(solution)/shard_map/dot_general | solution.py:67
  182.3 17.7 %copy.20 = bf16[2560,2560]{1,0:T(8,128)(2,1)} copy(bf16[2560,2560]{0,1:T(8,128)(2,1)} %fusion) | data formatting | bytes 26214400
  200.0 0.0 reduce-scatter.4.cloned.1.call-update
  200.0 0.0 copy-start.4
  200.0 0.3 all-gather.5.cloned.1.call-start
  200.3 94.1 %reduce-scatter.4.cloned.1.call-done = bf16[320,2560]{1,0:T(8,128)(2,1)} async-done(((bf16[2560,2560]{1,0:T(8,128)(2,1)}), bf16[320,2560]{1,0:T(8,128)(2,1)}) %reduce-scatter.4.cloned.1.call-update) | async-done | bytes 1638416 | tf_op jit(solution)/shard_map/reduce_scatter | solution.py:64
  294.4 9.7 %fusion.16 = (bf16[320,2560]{1,0:T(8,128)(2,1)}, f32[320,2560]{1,0:T(8,128)}, f32[1,320,2560]{2,1,0:T(8,128)}, f32[1,320,2560]{2,1,0:T(8,128)}) fusion(f32[1,320,2560]{2,1,0:T(8,128)} %param.11, bf16[320,2560]{1,0:T(8,128)(2,1)} %reduce-scatter.4.cloned.1.call-done, f32[1,320,2560]{2,1,0:T(8,128)} %param.10, f32[1,320,2560]{2,1,0:T(8,128)} %param.9), kind=kLoop, calls=%fused_computation.34 | loop fusion | flops 13926400 | bytes 22937600 | tf_op jit(solution)/shard_map/convert_element_type | solution.py:81
  304.1 0.0 all-gather.5.cloned.1.call-update
  304.1 74.5 %all-gather.5.cloned.1.call-done = bf16[2560,2560]{1,0:T(8,128)(2,1)} async-done(((bf16[320,2560]{1,0:T(8,128)(2,1)}), bf16[2560,2560]{1,0:T(8,128)(2,1)}) %all-gather.5.cloned.1.call-update) | async-done | bytes 13107216 | tf_op jit(solution)/shard_map/all_gather | solution.py:85
  378.6 0.0 copy-done.4
  378.6 0.0 copy-start.1
  378.6 7.9 %fusion.2 = bf16[1,32,2560]{2,1,0:T(8,128)(2,1)} fusion(bf16[2560,2560]{1,0:T(8,128)(2,1)} %all-gather.5.cloned.1.call-done, bf16[1,32,2560]{2,1,0:T(8,128)(2,1)S(1)} %copy-done.4), kind=kOutput, calls=%fused_computation.8 | convolution fusion | flops 419512320 | bytes 13434880 | tf_op jit(solution)/shard_map/dot_general | solution.py:83
  386.4 0.0 copy-done.1
Async XLA Ops:
  7.2 96.1 %copy-start = (bf16[1,4,128,2560]{3,2,1,0:T(8,128)(2,1)S(1)}, bf16[1,4,128,2560]{3,2,1,0:T(8,128)(2,1)}, u32[]{:S(2)}) copy-start(bf16[1,4,128,2560]{3,2,1,0:T(8,128)(2,1)} %param.12) | copy-start | bytes 7864324
  7.2 80.7 %all-gather.3.cloned.1.call-start = ((), (), s32[]{:S(2)}) async-start(), calls=%async_computation.1 | async-start | bytes 14745600 | tf_op jit(solution)/shard_map/all_gather | solution.py:49
  10.7 283.7 %reduce-scatter.4.cloned.1.call-start = ((), (), s32[]{:S(2)}) async-start(), calls=%async_computation.3 | async-start | bytes 14745600 | tf_op jit(solution)/shard_map/reduce_scatter | solution.py:64
  87.9 15.4 %copy-start.2 = (bf16[4,128,2560]{2,1,0:T(8,128)(2,1)S(1)}, bf16[4,128,2560]{2,1,0:T(8,128)(2,1)}, u32[]{:S(2)}) copy-start(bf16[4,128,2560]{2,1,0:T(8,128)(2,1)} %maximum_convert_fusion) | copy-start | bytes 7864324
  101.8 61.1 %collective-permute-start = (bf16[4,128,2560]{2,1,0:T(8,128)(2,1)}, bf16[4,128,2560]{2,1,0:T(8,128)(2,1)S(1)}, u32[]{:S(2)}, u32[]{:S(2)}) collective-permute-start(bf16[4,128,2560]{2,1,0:T(8,128)(2,1)} %bitcast.85), channel_id=1, source_target_pairs={{8,0},{16,8},{24,16},{9,1},{17,9},{25,17},{10,2},{18,10},{26,18},{... | collective-permute-start | bytes 7864328 | tf_op jit(solution)/shard_map/ppermute | solution.py:19
  103.2 59.6 %copy-start.3 = (s32[1,128,2560]{2,1,0:T(8,128)S(1)}, s32[1,128,2560]{2,1,0:T(8,128)}, u32[]{:S(2)}) copy-start(s32[1,128,2560]{2,1,0:T(8,128)} %param.16) | copy-start | bytes 3932164
  200.0 178.6 %copy-start.4 = (bf16[1,32,2560]{2,1,0:T(8,128)(2,1)S(1)}, bf16[1,32,2560]{2,1,0:T(8,128)(2,1)}, u32[]{:S(2)}) copy-start(bf16[1,32,2560]{2,1,0:T(8,128)(2,1)} %param.17) | copy-start | bytes 491524
  200.0 178.6 %all-gather.5.cloned.1.call-start = ((), (), s32[]{:S(2)}) async-start(), calls=%async_computation.2 | async-start | bytes 14745600 | tf_op jit(solution)/shard_map/all_gather | solution.py:85
  378.6 7.9 %copy-start.1 = (bf16[1,4,128,2560]{3,2,1,0:T(8,128)(2,1)S(1)}, bf16[1,4,128,2560]{3,2,1,0:T(8,128)(2,1)}, u32[]{:S(2)}) copy-start(bf16[1,4,128,2560]{3,2,1,0:T(8,128)(2,1)} %param.12) | copy-start | bytes 7864324
Sparse Core Ops, SparseCore 0:
  10.8 77.0 all-gather.2
  200.1 94.2 reduce-scatter.3
  304.2 74.3 all-gather.4
where the time goes:
time: 394 us; the launch traced here: 393 us
  waiting for transfers between devices  288 us (73%)
  matrix products  50.7 us (13%)
  other arithmetic  21.1 us (5%)
  local copies, waits for them, and re-layouts  17.7 us (4%)
  between operations  13.8 us (4%)
    reduce_scatter x1, waiting for transfers between devices, shards(): lax.psum_scatter((partial_value + lax.dot_general(acts_arriving, membrane...  94.1 us
    all_gather x1, waiting for transfers between devices, shards(): lax.all_gather(fresh_weights, 'dp', axis=0, tiled=True)  74.5 us
    all_gather x1, waiting for transfers between devices, shards(): lax.all_gather(params.astype(jnp.bfloat16), 'dp', axis=0, tiled=True)  72.1 us
    ppermute x1, waiting for transfers between devices, passed_along(): return lax.ppermute(shard, axis, pairs)  47.1 us
    unnamed x11, local copies, waits for them, and re-layouts  17.7 us
    dot_general x1, matrix products, shards(): lax.dot_general(acts_arriving, membrane_arriving, contract, preferred_ele...  16.4 us
    dot_general x1, matrix products, shards(): lax.dot_general(membrane_own, lax.all_gather(params.astype(jnp.bfloat16),...  13.9 us
    dot_general x1, matrix products, shards(): lax.dot_general(acts_own, membrane_own, contract, preferred_element_type=...  12.5 us
  transfers between devices with their start and end apart: 4, of which 4 were waited for; matrix products, arithmetic and copies ran while one was open for 4% of the time, Pallas kernels for 0%

commit v1 on v0

v1 whole, which is shorter than its diff:
```python
import functools

import jax
import jax.numpy as jnp
from jax import lax
from jax.experimental import pallas as pl
from jax.experimental.pallas import tpu as pltpu
from jax.sharding import PartitionSpec as P

LEAK_RATE = 0.5
LEARN_RATE = 0.002
FIRST_DECAY = 0.9
SECOND_DECAY = 0.95
EPSILON = 1e-08
WEIGHT_DECAY = 0.1
FIRST_CORRECTION = 1.0 - 0.9**10
SECOND_CORRECTION = 1.0 - 0.95**10

LANES = 128
PARTS = 8
CHIPS = 4
BF16 = jnp.bfloat16
F32 = jnp.float32


def passed_along(shard, axis, by):
    count = lax.axis_size(axis)
    pairs = [(i, i + by) for i in range(count) if 0 <= i + by < count]
    return lax.ppermute(shard, axis, pairs)


def swapped(shard, bit):
    return lax.ppermute(shard, "dp", [(i, i ^ bit) for i in range(PARTS)])


def over_core(shard):
    return swapped(shard, 1)


def over_x(shard):
    return swapped(shard, 2)


def over_y(shard):
    return swapped(shard, 4)


def cost(flops, *arrays):
    moved = sum(a.size * a.dtype.itemsize for a in arrays)
    return pl.CostEstimate(flops=int(flops), bytes_accessed=int(moved), transcendentals=0)


def adam(params, first, second, gradient):
    fresh_first = FIRST_DECAY * first + (1.0 - FIRST_DECAY) * gradient
    fresh_second = SECOND_DECAY * second + (1.0 - SECOND_DECAY) * gradient * gradient
    direction = (
        fresh_first / FIRST_CORRECTION / (jnp.sqrt(fresh_second / SECOND_CORRECTION) + EPSILON)
    )
    fresh_params = params - LEARN_RATE * (direction + WEIGHT_DECAY * params)
    return fresh_params, fresh_first, fresh_second


def prepare_kernel(where, grads, own, arriving, membrane_t, grads_t, arriving_t):
    steps, rows = grads.shape[0], grads.shape[1]
    window = own[...].T
    arriving_t[...] = arriving[...].T
    carried = jnp.zeros(window.shape, F32)
    for moment in reversed(range(steps)):
        now = grads[moment].astype(F32).T
        lanes = pl.ds(moment * rows, rows)
        grads_t[:, lanes] = now.astype(BF16)
        bit = jnp.bitwise_and(jnp.right_shift(window, moment), 1).astype(F32)
        carried = bit * now + LEAK_RATE * carried
        membrane_t[:, lanes] = carried.astype(BF16)


def prepare(where, grads, own, arriving):
    steps, rows, features = grads.shape
    block = 256
    tokens = steps * rows
    outs = (
        jax.ShapeDtypeStruct((features, tokens), BF16),
        jax.ShapeDtypeStruct((features, tokens), BF16),
        jax.ShapeDtypeStruct((features, rows), jnp.int32),
    )
    return pl.pallas_call(
        prepare_kernel,
        out_shape=outs,
        grid_spec=pltpu.PrefetchScalarGridSpec(
            num_scalar_prefetch=1,
            grid=(features // block,),
            in_specs=[
                pl.BlockSpec((steps, rows, block), lambda i, s: (0, 0, i)),
                pl.BlockSpec((rows, block), lambda i, s: (0, i)),
                pl.BlockSpec((rows, block), lambda i, s: (0, i)),
            ],
            out_specs=[
                pl.BlockSpec((block, tokens), lambda i, s: (i, 0)),
                pl.BlockSpec((block, tokens), lambda i, s: (i, 0)),
                pl.BlockSpec((block, rows), lambda i, s: (i, 0)),
            ],
        ),
        cost_estimate=cost(0, grads, grads, grads, own, arriving, arriving),
        compiler_params=pltpu.CompilerParams(vmem_limit_bytes=16 << 20),
        name="prepare",
    )(where, grads, own, arriving)


def column_block(s, relative, begin, width, rows):
    chip = jnp.bitwise_xor(s[0], relative)
    at = jnp.where(s[1] == 0, begin, 2 * rows - begin - width)
    return (chip * (2 * rows) + at) // width


def through_kernel(splits, pieces, where, *refs):
    weights = refs[: sum(splits)]
    refs = refs[sum(splits) :]
    mine, sibling = refs[:2]
    grads = refs[2 : 2 + 2 * len(pieces)]
    out, total = refs[2 + 2 * len(pieces) :]
    step = pl.program_id(0)
    tokens = mine.shape[1]
    rows = jnp.concatenate([w[...] for w in weights], axis=0)

    @pl.when(step == 0)
    def _():
        total[...] = jnp.zeros_like(total)

    for side, held in enumerate((mine, sibling)):
        lanes = pl.ds(side * tokens, tokens)
        total[:, lanes] += jnp.dot(rows, held[...], preferred_element_type=F32)

    @pl.when(step == pl.num_programs(0) - 1)
    def _():
        at = 0
        for index, (_, _, width) in enumerate(pieces):
            for side in range(2):
                lanes = pl.ds(side * tokens, tokens)
                value = total[pl.ds(at, width), lanes] + grads[2 * index + side][...].astype(F32)
                out[pl.ds(at, width), lanes] = value.astype(BF16)
            at += width


def through(where, pieces, weights, membranes, grads_t, rows):
    features, tokens = membranes[0].shape
    count = sum(p[2] for p in pieces)
    chunk = 512 if features % 512 == 0 else features
    flat = [w for group in weights for w in group]
    out = jax.ShapeDtypeStruct((count, 2 * tokens), BF16)
    specs = [pl.BlockSpec((w.shape[0], chunk), lambda i, s: (0, i)) for w in flat]
    specs += [pl.BlockSpec((chunk, tokens), lambda i, s: (i, 0))] * 2
    grad_operands = []
    for relative, begin, width in pieces:
        for side in range(2):
            specs.append(
                pl.BlockSpec(
                    (width, tokens),
                    functools.partial(
                        lambda i, s, r, b, w: (column_block(s, r, b, w, rows), 0),
                        r=relative,
                        b=begin,
                        w=width,
                    ),
                )
            )
            grad_operands.append(grads_t[side])
    return pl.pallas_call(
        functools.partial(through_kernel, [len(g) for g in weights], pieces),
        out_shape=out,
        grid_spec=pltpu.PrefetchScalarGridSpec(
            num_scalar_prefetch=1,
            grid=(features // chunk,),
            in_specs=specs,
            out_specs=pl.BlockSpec((count, 2 * tokens), lambda i, s: (0, 0)),
            scratch_shapes=[pltpu.VMEM((count, 2 * tokens), F32)],
        ),
        cost_estimate=cost(4 * count * features * tokens, *flat, *membranes, out, out),
        compiler_params=pltpu.CompilerParams(vmem_limit_bytes=24 << 20),
        name="through",
    )(where, *flat, *membranes, *grad_operands)


def partial_kernel(sources, width, where, *refs):
    own = refs[:8]
    windows = refs[8:16]
    arrived = refs[16 : 16 + len(set(a for a, _ in sources))]
    refs = refs[16 + len(arrived) :]
    acts = refs[:4]
    x_keep, x_send, y_keep, y_send, held_own, held_arriving = refs[4:]
    step = pl.program_id(0)
    tokens = own[0].shape[1]
    rows = windows[0].shape[1]

    @pl.when(step == 0)
    def _():
        for chip in range(CHIPS):
            for side in range(2):
                lanes = pl.ds(side * tokens, tokens)
                held_own[pl.ds(chip * width, width), lanes] = own[2 * chip + side][...]
        for relative in range(CHIPS):
            chip = jnp.bitwise_xor(where[0], relative)
            place = pl.ds(pl.multiple_of(chip * width, width), width)
            array, begin = sources[relative]
            for side in range(2):
                window = windows[2 * relative + side][...]
                carried = jnp.zeros(window.shape, F32)
                for moment in reversed(range(tokens // rows)):
                    lanes = pl.ds(side * tokens + moment * rows, rows)
                    now = arrived[array][pl.ds(begin, width), lanes].astype(F32)
                    bit = jnp.bitwise_and(jnp.right_shift(window, moment), 1).astype(F32)
                    carried = bit * now + LEAK_RATE * carried
                    held_arriving[place, lanes] = carried.astype(BF16)

    value = None
    for index, act in enumerate(acts):
        held = (held_own, held_own, held_arriving, held_arriving)[index]
        term = jnp.dot(
            held[:, pl.ds((index % 2) * tokens, tokens)],
            act[...],
            preferred_element_type=F32,
        )
        value = term if value is None else value + term
    value = value.astype(BF16)
    first, last = value[: 2 * width], value[2 * width :]

    @pl.when(jnp.logical_or(step == 0, step == 2))
    def _():
        x_send[0] = first

    @pl.when(jnp.logical_or(step == 1, step == 3))
    def _():
        x_keep[0] = first

    @pl.when(step < 2)
    def _():
        y_send[0] = last

    @pl.when(step >= 2)
    def _():
        y_keep[0] = last


def partials(where, begin, width, membranes, windows_t, arrived, sources, acts, rows):
    features, tokens = membranes[0].shape
    block = 2 * rows
    specs, operands = [], []
    for chip in range(CHIPS):
        for side in range(2):

            def index(i, s, chip=chip):
                return (column_block(s, jnp.bitwise_xor(s[0], chip), begin, width, rows), 0)

            specs.append(pl.BlockSpec((width, tokens), index))
            operands.append(membranes[side])
    for relative in range(CHIPS):
        for side in range(2):
            window = windows_t[side]

            def index(i, s, relative=relative):
                return (column_block(s, relative, begin, width, rows), 0)

            specs.append(pl.BlockSpec((width, window.shape[1]), index))
            operands.append(window)
    for array in arrived:
        specs.append(pl.BlockSpec(array.shape, lambda i, s: (0, 0)))
        operands.append(array)
    for act in acts:
        specs.append(
            pl.BlockSpec((tokens, block), lambda i, s: (0, jnp.bitwise_xor(s[0], 3 - i)))
        )
        operands.append(act)
    piece = jax.ShapeDtypeStruct((2, 2 * width, block), BF16)

    def out_spec(index):
        return pl.BlockSpec((1, 2 * width, block), lambda i, s: (index(i), 0, 0))

    return pl.pallas_call(
        functools.partial(partial_kernel, sources, width),
        out_shape=(piece,) * 4,
        grid_spec=pltpu.PrefetchScalarGridSpec(
            num_scalar_prefetch=1,
            grid=(CHIPS,),
            in_specs=specs,
            out_specs=[
                out_spec(lambda i: jnp.where(i < 3, 1, 0)),
                out_spec(lambda i: jnp.where(i < 2, 1, 0)),
                out_spec(lambda i: jnp.where(i < 3, 1, 0)),
                out_spec(lambda i: jnp.where(i < 1, 1, 0)),
            ],
            scratch_shapes=[pltpu.VMEM((CHIPS * width, 2 * tokens), BF16)] * 2,
        ),
        cost_estimate=cost(32 * width * tokens * features, *acts, piece, piece, piece, piece),
        compiler_params=pltpu.CompilerParams(vmem_limit_bytes=32 << 20),
        name="partials",
    )(where, *operands)


def gather_up_kernel(width, where, xk, xr, xs, yk, yr, ys, mine, other):
    rows = mine.shape[0]
    core = where[1]
    for chip in range(CHIPS):
        kept, received, summed = (xk, xr, xs) if chip < 2 else (yk, yr, ys)
        at = pl.ds((chip % 2) * width, width)
        value = (
            kept[0, at].astype(F32) + received[0, at].astype(F32) + summed[at].astype(F32)
        )
        if width < LANES:
            blank = jnp.zeros((LANES - width, value.shape[1]), F32)
            value = jnp.where(
                core == 0,
                jnp.concatenate([value, blank], axis=0),
                jnp.concatenate([blank, value], axis=0),
            )
        value = value.T.astype(BF16)
        lanes = pl.ds(chip * LANES, LANES)

        @pl.when(core == 0)
        def _(value=value, lanes=lanes):
            mine[:, lanes] = value[:rows]
            other[:, lanes] = value[rows:]

        @pl.when(core != 0)
        def _(value=value, lanes=lanes):
            mine[:, lanes] = value[rows:]
            other[:, lanes] = value[:rows]


def gather_up(where, width, kept_x, got_x, sum_x, kept_y, got_y, sum_y, rows):
    first = pl.BlockSpec((1, 2 * width, 2 * rows), lambda i, s: (0, 0, 0))
    whole = pl.BlockSpec((2 * width, 2 * rows), lambda i, s: (0, 0))
    out = jax.ShapeDtypeStruct((rows, CHIPS * LANES), BF16)
    spec = pl.BlockSpec(out.shape, lambda i, s: (0, 0))
    return pl.pallas_call(
        functools.partial(gather_up_kernel, width),
        out_shape=(out, out),
        grid_spec=pltpu.PrefetchScalarGridSpec(
            num_scalar_prefetch=1,
            grid=(1,),
            in_specs=[first, first, whole, first, first, whole],
            out_specs=[spec, spec],
        ),
        cost_estimate=cost(0, sum_x, sum_x, sum_x, sum_x, sum_x, sum_x, out, out),
        compiler_params=pltpu.CompilerParams(vmem_limit_bytes=24 << 20),
        name="gather_up",
    )(where, kept_x, got_x, sum_x, kept_y, got_y, sum_y)


def update_kernel(whole, where, mine, theirs, params, first, second, acts, *refs):
    fresh_params, fresh_first, fresh_second, currents = refs[-4:]
    if whole:
        own = pl.program_id(1) == where[1]
        gradient = jnp.where(own, mine[...].astype(F32), theirs[...].astype(F32))
    else:
        gradient = mine[...].astype(F32) + theirs[...].astype(F32)
    new = adam(params[...], first[...], second[...], gradient)
    fresh_params[...], fresh_first[...], fresh_second[...] = new
    currents[...] = jnp.dot(
        acts[...], new[0].astype(BF16), preferred_element_type=F32
    ).astype(BF16)


def update(where, begin, width, mine, theirs, state, acts, held):
    params = state[0]
    rows, features = params.shape
    per_chip = 2 * rows // LANES
    whole = width == LANES
    cores = 2 if whole else 1
    tile_of_core = [begin // LANES, (2 * rows - begin - width) // LANES]

    def tile(i, j, s):
        inside = jnp.where(j == 0, tile_of_core[0], tile_of_core[1])
        return (0, per_chip * i + inside)

    block = pl.BlockSpec((rows, LANES), tile)
    grads = pl.BlockSpec((rows, LANES), lambda i, j, s: (0, i))
    current_shape = jax.ShapeDtypeStruct((acts.shape[0], CHIPS * cores * LANES), BF16)
    operands = [where, mine, theirs, *state, acts]
    specs = [grads, grads, block, block, block, pl.BlockSpec(acts.shape, lambda i, j, s: (0, 0))]
    aliases = {}
    if held is not None:
        for index, array in enumerate(held):
            aliases[len(operands)] = index
            operands.append(array)
            specs.append(pl.BlockSpec(memory_space=pl.ANY))
    shape = jax.ShapeDtypeStruct((rows, features), F32)
    *fresh, currents = pl.pallas_call(
        functools.partial(update_kernel, whole),
        out_shape=(shape, shape, shape, current_shape),
        grid_spec=pltpu.PrefetchScalarGridSpec(
            num_scalar_prefetch=1,
            grid=(CHIPS, cores),
            in_specs=specs,
            out_specs=[
                block,
                block,
                block,
                pl.BlockSpec((acts.shape[0], LANES), lambda i, j, s: (0, cores * i + j)),
            ],
        ),
        input_output_aliases=aliases,
        cost_estimate=pl.CostEstimate(
            flops=2 * acts.size * CHIPS * cores * LANES,
            bytes_accessed=24 * rows * CHIPS * cores * LANES,
            transcendentals=0,
        ),
        compiler_params=pltpu.CompilerParams(vmem_limit_bytes=16 << 20),
        name="update",
    )(*operands)
    return fresh, currents


def columns_to_owners(tokens, device):
    count, features = tokens.shape
    width = features // PARTS
    cut = tokens.reshape(count, PARTS, width).transpose(1, 0, 2)
    cut = cut.reshape(2, 2, 2, count, width)
    for axis, bit in ((0, 4), (1, 2), (2, 1)):
        cut = jnp.where(jnp.bitwise_and(device, bit) != 0, jnp.flip(cut, axis), cut)
    held = cut.transpose(2, 0, 1, 3, 4)
    held = jnp.stack([held[0], over_core(held[1])])
    held = held.transpose(2, 0, 1, 3, 4)
    held = jnp.stack([held[0], over_x(held[1])])
    held = held.transpose(3 - 1, 0, 1, 3, 4)
    held = jnp.stack([held[0], over_y(held[1])])
    return held.reshape(PARTS * count, width)


def summed_to_owners(terms):
    rows, columns = terms.shape
    held = terms.reshape(CHIPS, 2, rows // PARTS, columns)

    def add(kept, got):
        return (kept.astype(F32) + got.astype(F32)).astype(BF16)

    held = add(held[:, 0], over_core(held[:, 1]))
    held = held.reshape(2, 2, rows // PARTS, columns)
    held = add(held[:, 0], over_x(held[:, 1]))
    return add(held[0], over_y(held[1]))


def relay_shards(
    master,
    first_moment,
    second_moment,
    inputs_own,
    inputs_arriving,
    grads_own,
    windows_own,
    windows_arriving,
    next_inputs,
):
    params = master[0]
    rows, features = params.shape
    steps, tok_rows = grads_own.shape[1], grads_own.shape[2]
    tokens = steps * tok_rows
    device = lax.axis_index("dp")
    core = jnp.bitwise_and(device, 1)
    where = jnp.stack([device // 2, core]).astype(jnp.int32)

    widths = [LANES] * (rows // LANES) + ([rows % LANES] if rows % LANES else [])
    begins = [sum(widths[:i]) for i in range(len(widths))]
    groups = list(zip(begins, widths))

    held = []
    for begin, width in groups:
        at = jnp.where(core == 0, begin, rows - begin - width)
        held.append(lax.dynamic_slice_in_dim(params, at, width, 0).astype(BF16))
    gathered = []
    for piece in held:
        half = piece.shape[0] // 2
        by_x, by_y = over_x(piece), over_y(piece)
        gathered.append(
            ((by_x,), (by_y,), (over_y(by_x[:half]), over_x(by_y[half:])))
        )

    membrane_t, grads_t, window_t = prepare(
        where, grads_own[0], windows_own[0], windows_arriving[0]
    )
    membranes = (membrane_t, over_core(membrane_t))
    grads_ts = (grads_t, over_core(grads_t))
    acts = []
    for array in (inputs_own, inputs_arriving):
        flat = array[0].reshape(tokens, features)
        acts += [flat, over_core(flat)]
    windows_t = (window_t, over_core(window_t))

    last = len(groups) - 1
    own_pieces = [(0, *groups[g]) for g in range(last)]
    own_arrived = passed_along(
        through(where, own_pieces, [(held[g],) for g in range(last)], membranes, grads_ts, rows),
        "section",
        -1,
    )
    arrived = []
    for g, (begin, width) in enumerate(groups):
        pieces = [(r, begin, width) for r in (1, 2, 3)]
        weights = list(gathered[g])
        if g == last:
            pieces = [(0, begin, width)] + pieces
            weights = [(held[g],)] + weights
        sent = through(where, pieces, weights, membranes, grads_ts, rows)
        got = passed_along(sent, "section", -1)
        if g == last:
            arrived.append(((got,), [(0, r * width) for r in range(CHIPS)]))
        else:
            arrived.append(
                ((own_arrived, got), [(0, begin)] + [(1, r * width) for r in range(3)])
            )

    acts_here = columns_to_owners(next_inputs[0], device)

    fresh = None
    state = (params, first_moment[0], second_moment[0])
    currents = []
    for g, (begin, width) in enumerate(groups):
        x_keep, x_send, y_keep, y_send = partials(
            where, begin, width, membranes, windows_t, *arrived[g], acts, rows
        )
        got_x, got_y = over_x(x_send), over_y(y_send)
        pass_y = (x_keep[1].astype(F32) + got_x[1].astype(F32)).astype(BF16)
        pass_x = (y_keep[1].astype(F32) + got_y[1].astype(F32)).astype(BF16)
        sum_x, sum_y = over_y(pass_y), over_x(pass_x)
        mine, other = gather_up(
            where, width, x_keep, got_x, sum_x, y_keep, got_y, sum_y, rows
        )
        fresh, current = update(
            where, begin, width, mine, over_core(other), state, acts_here, fresh
        )
        currents.append(current)

    early = summed_to_owners(jnp.concatenate(currents[:last], axis=1))
    late = summed_to_owners(currents[last])
    count = early.shape[0]
    tiles = [None] * (2 * rows // LANES)
    for g, (begin, width) in enumerate(groups):
        if g < last:
            size = CHIPS * 2 * LANES
            whole = early[:, g * size : (g + 1) * size].reshape(count, CHIPS, 2, LANES)
            tiles[begin // LANES] = whole[:, :, 0]
            tiles[(2 * rows - begin - width) // LANES] = whole[:, :, 1]
        else:
            tiles[begin // LANES] = late.reshape(count, CHIPS, LANES)
    next_currents = jnp.stack(tiles, axis=2).reshape(count, features)
    return (fresh[0][None], fresh[1][None], fresh[2][None], next_currents[None])


def membrane_grads(gradients, windows):
    carried = jnp.zeros(gradients.shape[1:], F32)
    results = []
    for moment in reversed(range(gradients.shape[0])):
        window = jnp.bitwise_and(jnp.right_shift(windows, moment), 1).astype(F32)
        carried = window * gradients[moment].astype(F32) + LEAK_RATE * carried
        results = [carried] + results
    return jnp.stack(results).astype(BF16)


def plain_shards(
    master,
    first_moment,
    second_moment,
    inputs_own,
    inputs_arriving,
    grads_own,
    windows_own,
    windows_arriving,
    next_inputs,
):
    params = master[0]
    timesteps, tok_rows, features = (grads_own.shape[1], grads_own.shape[2], grads_own.shape[3])
    flat_rows = timesteps * tok_rows
    membrane_own = membrane_grads(grads_own[0], windows_own[0]).reshape(flat_rows, features)
    weights = lax.all_gather(params.astype(BF16), "dp", axis=0, tiled=True)
    across = (((1,), (1,)), ((), ()))
    product = lax.dot_general(membrane_own, weights, across, preferred_element_type=F32)
    summed = grads_own[0].reshape(flat_rows, features).astype(F32) + product
    outgoing = summed.astype(BF16).reshape(timesteps, tok_rows, features)
    received = passed_along(outgoing, "section", -1)
    membrane_arriving = membrane_grads(received, windows_arriving[0]).reshape(flat_rows, features)
    contract = (((0,), (0,)), ((), ()))
    partial_value = lax.dot_general(
        inputs_own[0].reshape(flat_rows, features),
        membrane_own,
        contract,
        preferred_element_type=F32,
    ) + lax.dot_general(
        inputs_arriving[0].reshape(flat_rows, features),
        membrane_arriving,
        contract,
        preferred_element_type=F32,
    )
    gradient = lax.psum_scatter(
        partial_value.astype(BF16), "dp", scatter_dimension=0, tiled=True
    ).astype(F32)
    fresh_params, fresh_first, fresh_second = adam(
        params, first_moment[0], second_moment[0], gradient
    )
    gathered = lax.all_gather(fresh_params.astype(BF16), "dp", axis=0, tiled=True)
    currents = jnp.dot(next_inputs[0], gathered, preferred_element_type=F32)
    return (
        fresh_params[None],
        fresh_first[None],
        fresh_second[None],
        currents.astype(BF16)[None],
    )


def solution(mesh):
    rows = P("section", "dp", None)
    acts = P("section", None, "dp", None)
    return jax.shard_map(
        relay_shards if mesh.shape["dp"] == PARTS else plain_shards,
        mesh=mesh,
        in_specs=(rows, rows, rows, acts, acts, acts, rows, rows, rows),
        out_specs=(rows, rows, rows, rows),
        check_vma=False,
    )
```

time: 394 us -> 236 us (0.60)
  waiting for transfers between devices: 288 us -> 111 us
  Pallas kernels: 0 us -> 63.3 us
  matrix products: 50.7 us -> 0 us
  starting transfers between devices: 1.8 us -> 43.3 us
  other arithmetic: 21.1 us -> 1.98 us
  between operations: 13.8 us -> 1.27 us
    all_gather x2 -> x0, waiting for transfers between devices: 147 us -> none  [the longest x1 74.5 us: shards(): lax.all_gather(fresh_weights, 'dp', axis=0, tiled=True)]
    reduce_scatter x1 -> x0, waiting for transfers between devices: 94.1 us -> none  [shards(): lax.psum_scatter((partial_value + lax.dot_general(acts_arriving, membrane...]
    ppermute x0 -> x41, waiting for transfers between devices: none -> 83.6 us  [swapped(): return lax.ppermute(shard, 'dp', [(i, i ^ bit) for i in range(PARTS)])]
    pallas_call x0 -> x14, Pallas kernels: none -> 63.3 us  [the longest x3 26.1 us: partials(): pl.pallas_call(functools.partial(partial_kernel, sources, width), out_sha...]
    dot_general x4 -> x0, matrix products: 50.7 us -> none  [the longest x1 16.4 us: shards(): lax.dot_general(acts_arriving, membrane_arriving, contract, preferred_ele...]
    ppermute x0 -> x41, starting transfers between devices: none -> 37.9 us  [swapped(): return lax.ppermute(shard, 'dp', [(i, i ^ bit) for i in range(PARTS)])]
    ppermute x1 -> x4, waiting for transfers between devices: 47.1 us -> 27.3 us  [passed_along(): return lax.ppermute(shard, axis, pairs)]
    convert_element_type x3 -> x12, other arithmetic: 14.9 us -> 0.7 us  [the longest x6 0.29 us: add(): return (kept.astype(F32) + got.astype(F32)).astype(BF16)]
  transfers between devices with their start and end apart: 4 -> 45, of which waited for: 4 -> 19; matrix products, arithmetic and copies ran while one was open for 4% -> 3% of each run, Pallas kernels for 0% -> 26%
where the time goes in v1:
time: 236 us; the launch traced here: 235 us
  waiting for transfers between devices  111 us (47%)
  Pallas kernels  63.3 us (27%)
  starting transfers between devices  43.3 us (18%)
  local copies, waits for them, and re-layouts  14.5 us (6%)
    ppermute x41, waiting for transfers between devices, swapped(): return lax.ppermute(shard, 'dp', [(i, i ^ bit) for i in range(PARTS)])  83.6 us
    ppermute x41, starting transfers between devices, swapped(): return lax.ppermute(shard, 'dp', [(i, i ^ bit) for i in range(PARTS)])  37.9 us
    ppermute x4, waiting for transfers between devices, passed_along(): return lax.ppermute(shard, axis, pairs)  27.3 us
    pallas_call x3, Pallas kernels, partials(): pl.pallas_call(functools.partial(partial_kernel, sources, width), out_sha...  26.1 us
    pallas_call x4, Pallas kernels, through(): pl.pallas_call(functools.partial(through_kernel, [len(g) for g in weights...  16.3 us
    pallas_call x3, Pallas kernels, update(): pl.pallas_call(functools.partial(update_kernel, whole), out_shape=(shape,...  13.7 us
    unnamed x31, local copies, waits for them, and re-layouts  6.9 us
    ppermute x4, starting transfers between devices, passed_along(): return lax.ppermute(shard, axis, pairs)  5.35 us
  transfers between devices with their start and end apart: 45, of which 19 were waited for; matrix products, arithmetic and copies ran while one was open for 3% of the time, Pallas kernels for 26%

profile of v1, /device:TPU:0, one launch (start us, length us, event | category | flops | bytes accessed | tf_op | source)
XLA Modules:
  0.0 235.2 jit_solution(6705039651755925962)
XLA Ops:
  0.6 1.9 fusion.4.refs_0_
  2.5 2.9 %collective-permute-start.2 = (bf16[64,2560]{1,0:T(8,128)(2,1)}, bf16[64,2560]{1,0:T(8,128)(2,1)S(1)}, u32[]{:S(2)}, u32[]{:S(2)}) collective-permute-start(bf16[64,2560]{1,0:T(8,128)(2,1)} %fusion.4.refs_0_), channel_id=1, source_target_pairs={{0,2},{1,3},{2,0},{3,1},{4,6},{5,7},{6,4},{7,5},{8,10},{9,11},{10,... | collective-permute-start | bytes 983048 | tf_op jit(solution)/shard_map/ppermute | solution.py:33
  5.4 1.5 collective-permute-start.3
  8.9 1.8 fusion.2
  11.4 2.0 collective-permute-done.2.refs_1_
  13.4 2.4 %collective-permute-start.4 = (bf16[32,2560]{1,0:T(8,128)(2,1)S(1)}, bf16[32,2560]{1,0:T(8,128)(2,1)S(1)}, u32[]{:S(2)}, u32[]{:S(2)}) collective-permute-start(bf16[32,2560]{1,0:T(8,128)(2,1)S(1)} %slice.168), channel_id=1, source_target_pairs={{0,4},{1,5},{2,6},{3,7},{4,0},{5,1},{6,2},{7,3},{8,12},{9,13},{10,... | collective-permute-start | bytes 491528 | tf_op jit(solution)/shard_map/ppermute | solution.py:33
  15.9 1.7 copy-done.8
  20.3 3.5 %prepare.1 = (bf16[2560,512]{1,0:T(8,128)(2,1)S(1)}, bf16[2560,512]{1,0:T(8,128)(2,1)S(1)}, s32[2560,128]{1,0:T(8,128)S(1)}) custom-call(s32[2]{0:T(128)S(1)} %pad_add_fusion.where, bf16[4,128,2560]{2,1,0:T(8,128)(2,1)S(1)} %bitcast.133, s32[128,2560]{1,0:T(8,128)S(1)} %bitcast.134, s32[128,2560]{1,0:T(8,128)S(1)} %bitcast.135), custom_call_target="tpu_custom_call" | custom-call | bytes 11796480 | tf_op jit(solution)/shard_map/prepare/pallas_call | solution.py:86
  25.9 2.1 collective-permute-start.5
  28.0 4.2 %collective-permute-done.5.refs_4_ = bf16[32,2560]{1,0:T(8,128)(2,1)S(1)} collective-permute-done((bf16[32,2560]{1,0:T(8,128)(2,1)S(1)}, bf16[32,2560]{1,0:T(8,128)(2,1)S(1)}, u32[]{:S(2)}, u32[]{:S(2)}) %collective-permute-start.5) | collective-permute-done | bytes 163872 | tf_op jit(solution)/shard_map/ppermute | solution.py:33
  32.2 1.7 collective-permute-start.29
  35.4 6.6 %collective-permute-done.20.refs_1_ = bf16[128,2560]{1,0:T(8,128)(2,1)S(1)} collective-permute-done((bf16[128,2560]{1,0:T(8,128)(2,1)S(1)}, bf16[128,2560]{1,0:T(8,128)(2,1)S(1)}, u32[]{:S(2)}, u32[]{:S(2)}) %collective-permute-start.20) | collective-permute-done | bytes 655392 | tf_op jit(solution)/shard_map/ppermute | solution.py:33
  42.0 6.1 %collective-permute-done.29.refs_0_ = bf16[128,2560]{1,0:T(8,128)(2,1)S(1)} collective-permute-done((bf16[128,2560]{1,0:T(8,128)(2,1)S(1)}, bf16[128,2560]{1,0:T(8,128)(2,1)S(1)}, u32[]{:S(2)}, u32[]{:S(2)}) %collective-permute-start.29) | collective-permute-done | bytes 655392 | tf_op jit(solution)/shard_map/ppermute | solution.py:33
  48.1 7.1 %collective-permute-done.30.refs_1_ = bf16[128,2560]{1,0:T(8,128)(2,1)S(1)} collective-permute-done((bf16[128,2560]{1,0:T(8,128)(2,1)S(1)}, bf16[128,2560]{1,0:T(8,128)(2,1)S(1)}, u32[]{:S(2)}, u32[]{:S(2)}) %collective-permute-start.30) | collective-permute-done | bytes 655392 | tf_op jit(solution)/shard_map/ppermute | solution.py:33
  55.8 8.3 %collective-permute-done.21.refs_2_ = bf16[64,2560]{1,0:T(8,128)(2,1)S(1)} collective-permute-done((bf16[64,2560]{1,0:T(8,128)(2,1)S(1)}, bf16[64,2560]{1,0:T(8,128)(2,1)S(1)}, u32[]{:S(2)}, u32[]{:S(2)}) %collective-permute-start.21) | collective-permute-done | bytes 327712 | tf_op jit(solution)/shard_map/ppermute | solution.py:33
  64.0 2.0 collective-permute-start.22
  66.1 6.2 %collective-permute-done.22.refs_3_ = bf16[64,2560]{1,0:T(8,128)(2,1)S(1)} collective-permute-done((bf16[64,2560]{1,0:T(8,128)(2,1)S(1)}, bf16[64,2560]{1,0:T(8,128)(2,1)S(1)}, u32[]{:S(2)}, u32[]{:S(2)}) %collective-permute-start.22) | collective-permute-done | bytes 327712 | tf_op jit(solution)/shard_map/ppermute | solution.py:33
  73.0 1.7 collective-permute-start.32
  75.6 4.8 %through.4 = bf16[256,1024]{1,0:T(8,128)(2,1)S(1)} custom-call(s32[2]{0:T(128)S(1)} %pad_add_fusion.where, bf16[64,2560]{1,0:T(8,128)(2,1)} %fusion.4.refs_0_, bf16[64,2560]{1,0:T(8,128)(2,1)S(1)} %copy-done.12, bf16[64,2560]{1,0:T(8,128)(2,1)} %collective-permute-done.3.refs_2_, bf16[32,2560]{1,0:T(8,128)(2,1)S(1)} %collective-permute-done.4.refs_3_, ...), custom_call_target="tpu_custom_call" | custom-call | flops 1342177280 | bytes 7602176 | tf_op jit(solution)/shard_map/through/pallas_call | solution.py:167
  80.5 4.2 %through.6 = bf16[384,1024]{1,0:T(8,128)(2,1)S(1)} custom-call(s32[2]{0:T(128)S(1)} %pad_add_fusion.where, bf16[128,2560]{1,0:T(8,128)(2,1)S(1)} %collective-permute-done.19.refs_0_, bf16[128,2560]{1,0:T(8,128)(2,1)S(1)} %collective-permute-done.20.refs_1_, bf16[64,2560]{1,0:T(8,128)(2,1)S(1)} %collective-permute-done.21.refs_2_, ...), custom_call_target="tpu_custom_call" | custom-call | flops 2013265920 | bytes 8781824 | tf_op jit(solution)/shard_map/through/pallas_call | solution.py:167
  87.3 3.2 %through.5 = bf16[256,1024]{1,0:T(8,128)(2,1)S(1)} custom-call(s32[2]{0:T(128)S(1)} %pad_add_fusion.where, bf16[128,2560]{1,0:T(8,128)(2,1)S(1)} %get-tuple-element.71.refs_0_, bf16[128,2560]{1,0:T(8,128)(2,1)S(1)} %get-tuple-element.70.refs_1_, bf16[2560,512]{1,0:T(8,128)(2,1)S(1)} %get-tuple-element.37.refs_5_.refs_0_.refs_2_.refs_4_.refs_6_, ...), custom_call_target="tpu_custom_call" | custom-call | flops 1342177280 | bytes 7602176 | tf_op jit(solution)/shard_map/through/pallas_call | solution.py:167
  91.7 4.2 %through.7 = bf16[384,1024]{1,0:T(8,128)(2,1)S(1)} custom-call(s32[2]{0:T(128)S(1)} %pad_add_fusion.where, bf16[128,2560]{1,0:T(8,128)(2,1)S(1)} %collective-permute-done.29.refs_0_, bf16[128,2560]{1,0:T(8,128)(2,1)S(1)} %collective-permute-done.30.refs_1_, bf16[64,2560]{1,0:T(8,128)(2,1)S(1)} %collective-permute-done.31.refs_2_, ...), custom_call_target="tpu_custom_call" | custom-call | flops 2013265920 | bytes 8781824 | tf_op jit(solution)/shard_map/through/pallas_call | solution.py:167
  95.9 1.5 collective-permute-start.33
  97.8 3.5 %collective-permute-done.7.refs_16_ = bf16[256,1024]{1,0:T(8,128)(2,1)S(1)} collective-permute-done((bf16[256,1024]{1,0:T(8,128)(2,1)S(1)}, bf16[256,1024]{1,0:T(8,128)(2,1)S(1)}, u32[]{:S(2)}, u32[]{:S(2)}) %collective-permute-start.7) | collective-permute-done | bytes 524320 | tf_op jit(solution)/shard_map/ppermute | solution.py:29
  101.3 6.3 %partials.3 = (bf16[2,128,640]{2,1,0:T(8,128)(2,1)S(1)}, bf16[2,128,640]{2,1,0:T(8,128)(2,1)S(1)}, bf16[2,128,640]{2,1,0:T(8,128)(2,1)S(1)}, bf16[2,128,640]{2,1,0:T(8,128)(2,1)S(1)}) custom-call(s32[2]{0:T(128)S(1)} %pad_add_fusion.where, bf16[2560,512]{1,0:T(8,128)(2,1)S(1)} %get-tuple-element.37.refs_5_.refs_0_.refs_2_.refs_4_.refs_6_, ...), custom_call_target="tpu_custom_call" | custom-call | flops 2684354560 | bytes 11796480 | tf_op jit(solution)/shard_map/partials/pallas_call | solution.py:277
  108.0 21.5 %collective-permute-done.18.refs_16_ = bf16[256,1024]{1,0:T(8,128)(2,1)S(1)} collective-permute-done((bf16[256,1024]{1,0:T(8,128)(2,1)S(1)}, bf16[256,1024]{1,0:T(8,128)(2,1)S(1)}, u32[]{:S(2)}, u32[]{:S(2)}) %collective-permute-start.18) | collective-permute-done | bytes 524320 | tf_op jit(solution)/shard_map/ppermute | solution.py:29
  129.4 1.5 collective-permute-start.12
  130.9 1.7 copy-done.7
  132.6 9.9 %partials.4 = (bf16[2,256,640]{2,1,0:T(8,128)(2,1)S(1)}, bf16[2,256,640]{2,1,0:T(8,128)(2,1)S(1)}, bf16[2,256,640]{2,1,0:T(8,128)(2,1)S(1)}, bf16[2,256,640]{2,1,0:T(8,128)(2,1)S(1)}) custom-call(s32[2]{0:T(128)S(1)} %pad_add_fusion.where, bf16[2560,512]{1,0:T(8,128)(2,1)S(1)} %get-tuple-element.37.refs_5_.refs_0_.refs_2_.refs_4_.refs_6_, ...), custom_call_target="tpu_custom_call" | custom-call | flops 5368709120 | bytes 13107200 | tf_op jit(solution)/shard_map/partials/pallas_call | solution.py:277
  142.9 2.4 %collective-permute-done.33.refs_17_ = bf16[384,1024]{1,0:T(8,128)(2,1)S(1)} collective-permute-done((bf16[384,1024]{1,0:T(8,128)(2,1)S(1)}, bf16[384,1024]{1,0:T(8,128)(2,1)S(1)}, u32[]{:S(2)}, u32[]{:S(2)}) %collective-permute-start.33) | collective-permute-done | bytes 786464 | tf_op jit(solution)/shard_map/ppermute | solution.py:29
  145.3 1.5 collective-permute-start.26
  146.7 9.9 %partials.5 = (bf16[2,256,640]{2,1,0:T(8,128)(2,1)S(1)}, bf16[2,256,640]{2,1,0:T(8,128)(2,1)S(1)}, bf16[2,256,640]{2,1,0:T(8,128)(2,1)S(1)}, bf16[2,256,640]{2,1,0:T(8,128)(2,1)S(1)}) custom-call(s32[2]{0:T(128)S(1)} %pad_add_fusion.where, bf16[2560,512]{1,0:T(8,128)(2,1)S(1)} %get-tuple-element.37.refs_5_.refs_0_.refs_2_.refs_4_.refs_6_, ...), custom_call_target="tpu_custom_call" | custom-call | flops 5368709120 | bytes 13107200 | tf_op jit(solution)/shard_map/partials/pallas_call | solution.py:277
  157.8 5.1 %collective-permute-done.26.yr = bf16[2,256,640]{2,1,0:T(8,128)(2,1)S(1)} collective-permute-done((bf16[2,256,640]{2,1,0:T(8,128)(2,1)S(1)}, bf16[2,256,640]{2,1,0:T(8,128)(2,1)S(1)}, u32[]{:S(2)}, u32[]{:S(2)}) %collective-permute-start.26) | collective-permute-done | bytes 655392 | tf_op jit(solution)/shard_map/ppermute | solution.py:33
  164.5 7.7 %collective-permute-done.34.xr = bf16[2,256,640]{2,1,0:T(8,128)(2,1)S(1)} collective-permute-done((bf16[2,256,640]{2,1,0:T(8,128)(2,1)S(1)}, bf16[2,256,640]{2,1,0:T(8,128)(2,1)S(1)}, u32[]{:S(2)}, u32[]{:S(2)}) %collective-permute-start.34) | collective-permute-done | bytes 655392 | tf_op jit(solution)/shard_map/ppermute | solution.py:33
  172.8 4.1 %collective-permute-done.36.yr = bf16[2,256,640]{2,1,0:T(8,128)(2,1)S(1)} collective-permute-done((bf16[2,256,640]{2,1,0:T(8,128)(2,1)S(1)}, bf16[2,256,640]{2,1,0:T(8,128)(2,1)S(1)}, u32[]{:S(2)}, u32[]{:S(2)}) %collective-permute-start.36) | collective-permute-done | bytes 655392 | tf_op jit(solution)/shard_map/ppermute | solution.py:33
  177.1 1.8 collective-permute-start.35
  178.9 1.7 collective-permute-start.37
  181.1 12.3 %collective-permute-done.13.ys = bf16[128,640]{1,0:T(8,128)(2,1)S(1)} collective-permute-done((bf16[128,640]{1,0:T(8,128)(2,1)S(1)}, bf16[128,640]{1,0:T(8,128)(2,1)S(1)}, u32[]{:S(2)}, u32[]{:S(2)}) %collective-permute-start.13) | collective-permute-done | bytes 163872 | tf_op jit(solution)/shard_map/ppermute | solution.py:33
  197.9 1.5 collective-permute-start.17
  199.4 3.7 %collective-permute-done.17 = bf16[2,2,32,320]{3,2,1,0:T(8,128)(2,1)S(1)} collective-permute-done((bf16[2,2,32,320]{3,2,1,0:T(8,128)(2,1)S(1)}, bf16[2,2,32,320]{3,2,1,0:T(8,128)(2,1)S(1)}, u32[]{:S(2)}, u32[]{:S(2)}) %collective-permute-start.17) | collective-permute-done | bytes 81952 | tf_op jit(solution)/shard_map/ppermute | solution.py:33
  203.2 5.3 %update.3 = (f32[320,2560]{1,0:T(8,128)}, f32[320,2560]{1,0:T(8,128)}, f32[320,2560]{1,0:T(8,128)}, bf16[256,1024]{1,0:T(8,128)(2,1)S(1)}) custom-call(s32[2]{0:T(128)S(1)} %pad_add_fusion.where, bf16[320,512]{1,0:T(8,128)(2,1)S(1)} %get-tuple-element.56.mine, bf16[320,512]{1,0:T(8,128)(2,1)S(1)} %collective-permute-done.38.theirs, ...), custom_call_target="tpu_custom_call" | custom-call | flops 167772160 | bytes 7864320 | tf_op jit(solution)/shard_map/update/pallas_call | solution.py:386
  208.5 5.3 %update.4 = (f32[320,2560]{1,0:T(8,128)}, f32[320,2560]{1,0:T(8,128)}, f32[320,2560]{1,0:T(8,128)}, bf16[256,1024]{1,0:T(8,128)(2,1)S(1)}) custom-call(s32[2]{0:T(128)S(1)} %pad_add_fusion.where, bf16[320,512]{1,0:T(8,128)(2,1)S(1)} %get-tuple-element.50.mine, ...), custom_call_target="tpu_custom_call", output_to_operand_aliasing={{0}: (7, {}), {1}: (8, {}), {2}: (9, {})} | custom-call | flops 167772160 | bytes 7864320 | tf_op jit(solution)/shard_map/update/pallas_call | solution.py:386
  213.7 3.2 %update.5 = (f32[320,2560]{1,0:T(8,128)}, f32[320,2560]{1,0:T(8,128)}, f32[320,2560]{1,0:T(8,128)}, bf16[256,512]{1,0:T(8,128)(2,1)S(1)}) custom-call(s32[2]{0:T(128)S(1)} %pad_add_fusion.where, bf16[320,512]{1,0:T(8,128)(2,1)S(1)} %get-tuple-element.44.mine, ...), custom_call_target="tpu_custom_call", output_to_operand_aliasing={{0}: (7, {}), {1}: (8, {}), {2}: (9, {})} | custom-call | flops 83886080 | bytes 3932160 | tf_op jit(solution)/shard_map/update/pallas_call | solution.py:386
  220.7 2.4 %collective-permute-done.43 = bf16[2,32,512]{2,1,0:T(8,128)(2,1)S(1)} collective-permute-done((bf16[2,32,512]{2,1,0:T(8,128)(2,1)S(1)}, bf16[2,32,512]{2,1,0:T(8,128)(2,1)S(1)}, u32[]{:S(2)}, u32[]{:S(2)}) %collective-permute-start.43) | collective-permute-done | bytes 65568 | tf_op jit(solution)/shard_map/ppermute | solution.py:33
  223.1 1.5 collective-permute-start.44
  224.6 3.7 %collective-permute-done.40 = bf16[2,32,2048]{2,1,0:T(8,128)(2,1)S(1)} collective-permute-done((bf16[2,32,2048]{2,1,0:T(8,128)(2,1)S(1)}, bf16[2,32,2048]{2,1,0:T(8,128)(2,1)S(1)}, u32[]{:S(2)}, u32[]{:S(2)}) %collective-permute-start.40) | collective-permute-done | bytes 262176 | tf_op jit(solution)/shard_map/ppermute | solution.py:33
  228.4 1.5 collective-permute-start.41
  230.0 3.5 %collective-permute-done.41 = bf16[32,2048]{1,0:T(8,128)(2,1)S(1)} collective-permute-done((bf16[32,2048]{1,0:T(8,128)(2,1)S(1)}, bf16[32,2048]{1,0:T(8,128)(2,1)S(1)}, u32[]{:S(2)}, u32[]{:S(2)}) %collective-permute-start.41) | collective-permute-done | bytes 131104 | tf_op jit(solution)/shard_map/ppermute | solution.py:33
  (130 shorter events, 30.0 us)
Async XLA Ops:
  2.5 10.9 %collective-permute-start.2 = (bf16[64,2560]{1,0:T(8,128)(2,1)}, bf16[64,2560]{1,0:T(8,128)(2,1)S(1)}, u32[]{:S(2)}, u32[]{:S(2)}) collective-permute-start(bf16[64,2560]{1,0:T(8,128)(2,1)} %fusion.4.refs_0_), channel_id=1, source_target_pairs={{0,2},{1,3},{2,0},{3,1},{4,6},{5,7},{6,4},{7,5},{8,10},{9,11},{10,... | collective-permute-start | bytes 983048 | tf_op jit(solution)/shard_map/ppermute | solution.py:33
  5.4 19.0 %collective-permute-start.3 = (bf16[64,2560]{1,0:T(8,128)(2,1)}, bf16[64,2560]{1,0:T(8,128)(2,1)}, u32[]{:S(2)}, u32[]{:S(2)}) collective-permute-start(bf16[64,2560]{1,0:T(8,128)(2,1)} %fusion.4.refs_0_), channel_id=1, source_target_pairs={{0,4},{1,5},{2,6},{3,7},{4,0},{5,1},{6,2},{7,3},{8,12},{9,13},{10,... | collective-permute-start | bytes 983048 | tf_op jit(solution)/shard_map/ppermute | solution.py:33
  8.9 15.0 %collective-permute-start.15 = (bf16[2,2,32,320]{3,2,1,0:T(8,128)(2,1)}, bf16[2,2,32,320]{3,2,1,0:T(8,128)(2,1)}, u32[]{:S(2)}, u32[]{:S(2)}) collective-permute-start(bf16[2,2,32,320]{3,2,1,0:T(8,128)(2,1)} %get-tuple-element.77), channel_id=1, source_target_pairs={{0,1},{1,0},{2,3},{3,2},{4,5},{5,4},{6,7},{7,6},{8,9},{9,8},{10,11... | collective-permute-start | bytes 245768 | tf_op jit(solution)/shard_map/ppermute | solution.py:33
  10.8 23.1 %collective-permute-start.19 = (bf16[128,2560]{1,0:T(8,128)(2,1)S(1)}, bf16[128,2560]{1,0:T(8,128)(2,1)S(1)}, u32[]{:S(2)}, u32[]{:S(2)}) collective-permute-start(bf16[128,2560]{1,0:T(8,128)(2,1)S(1)} %get-tuple-element.70.refs_1_), channel_id=1, source_target_pairs={{0,2},{1,3},{2,0},{3,1},{4,6},{5,7},{6,4},{7,5},{8,10},{9,11},{10,... | collective-permute-start | bytes 1966088 | tf_op jit(solution)/shard_map/ppermute | solution.py:33
  13.4 12.5 %collective-permute-start.4 = (bf16[32,2560]{1,0:T(8,128)(2,1)S(1)}, bf16[32,2560]{1,0:T(8,128)(2,1)S(1)}, u32[]{:S(2)}, u32[]{:S(2)}) collective-permute-start(bf16[32,2560]{1,0:T(8,128)(2,1)S(1)} %slice.168), channel_id=1, source_target_pairs={{0,4},{1,5},{2,6},{3,7},{4,0},{5,1},{6,2},{7,3},{8,12},{9,13},{10,... | collective-permute-start | bytes 491528 | tf_op jit(solution)/shard_map/ppermute | solution.py:33
  23.8 50.9 %copy-start.13 = (bf16[1,2,2,32,320]{4,3,2,1,0:T(8,128)(2,1)S(1)}, bf16[1,2,2,32,320]{4,3,2,1,0:T(8,128)(2,1)}, u32[]{:S(2)}) copy-start(bf16[1,2,2,32,320]{4,3,2,1,0:T(8,128)(2,1)} %get-tuple-element.76) | copy-start | bytes 245764
  23.8 51.8 %copy-start.12 = (bf16[64,2560]{1,0:T(8,128)(2,1)S(1)}, bf16[64,2560]{1,0:T(8,128)(2,1)}, u32[]{:S(2)}) copy-start(bf16[64,2560]{1,0:T(8,128)(2,1)} %copy-done.11) | copy-start | bytes 983044
  23.8 48.5 %collective-permute-start = (bf16[2560,512]{1,0:T(8,128)(2,1)S(1)}, bf16[2560,512]{1,0:T(8,128)(2,1)S(1)}, u32[]{:S(2)}, u32[]{:S(2)}) collective-permute-start(bf16[2560,512]{1,0:T(8,128)(2,1)S(1)} %get-tuple-element.37.refs_5_.refs_0_.refs_2_.refs_4_.refs_6_), channel_id=1, source_target_pairs={{0,1},{1,0},{2,3},{3,2},{4,5},{5,4},{6,7},{7,6},{8,9},{9,8},{10,11... | collective-permute-start | bytes 7864328 | tf_op jit(solution)/shard_map/ppermute | solution.py:33
  23.9 49.0 %collective-permute-start.6 = (bf16[2560,512]{1,0:T(8,128)(2,1)S(1)}, bf16[2560,512]{1,0:T(8,128)(2,1)S(1)}, u32[]{:S(2)}, u32[]{:S(2)}) collective-permute-start(bf16[2560,512]{1,0:T(8,128)(2,1)S(1)} %get-tuple-element.39.refs_7_.refs_9_.refs_11_.refs_13_.refs_4_.refs_6_.refs_8_.refs_10_), channel_id=1, source_target_pairs={{0,1},{1,0},{2,3},{3,2},{4,5},{5,4},{6,7},{7,6},{8,9},{9,8},{10,11... | collective-permute-start | bytes 7864328 | tf_op jit(solution)/shard_map/ppermute | solution.py:33
  24.4 17.6 %collective-permute-start.20 = (bf16[128,2560]{1,0:T(8,128)(2,1)S(1)}, bf16[128,2560]{1,0:T(8,128)(2,1)S(1)}, u32[]{:S(2)}, u32[]{:S(2)}) collective-permute-start(bf16[128,2560]{1,0:T(8,128)(2,1)S(1)} %get-tuple-element.70.refs_1_), channel_id=1, source_target_pairs={{0,4},{1,5},{2,6},{3,7},{4,0},{5,1},{6,2},{7,3},{8,12},{9,13},{10,... | collective-permute-start | bytes 1966088 | tf_op jit(solution)/shard_map/ppermute | solution.py:33
  25.9 6.3 %collective-permute-start.5 = (bf16[32,2560]{1,0:T(8,128)(2,1)S(1)}, bf16[32,2560]{1,0:T(8,128)(2,1)S(1)}, u32[]{:S(2)}, u32[]{:S(2)}) collective-permute-start(bf16[32,2560]{1,0:T(8,128)(2,1)S(1)} %slice.169), channel_id=1, source_target_pairs={{0,2},{1,3},{2,0},{3,1},{4,6},{5,7},{6,4},{7,5},{8,10},{9,11},{10,... | collective-permute-start | bytes 491528 | tf_op jit(solution)/shard_map/ppermute | solution.py:33
  32.2 15.9 %collective-permute-start.29 = (bf16[128,2560]{1,0:T(8,128)(2,1)S(1)}, bf16[128,2560]{1,0:T(8,128)(2,1)S(1)}, u32[]{:S(2)}, u32[]{:S(2)}) collective-permute-start(bf16[128,2560]{1,0:T(8,128)(2,1)S(1)} %get-tuple-element.71.refs_0_), channel_id=1, source_target_pairs={{0,2},{1,3},{2,0},{3,1},{4,6},{5,7},{6,4},{7,5},{8,10},{9,11},{10,... | collective-permute-start | bytes 1966088 | tf_op jit(solution)/shard_map/ppermute | solution.py:33
  33.9 21.3 %collective-permute-start.30 = (bf16[128,2560]{1,0:T(8,128)(2,1)S(1)}, bf16[128,2560]{1,0:T(8,128)(2,1)S(1)}, u32[]{:S(2)}, u32[]{:S(2)}) collective-permute-start(bf16[128,2560]{1,0:T(8,128)(2,1)S(1)} %get-tuple-element.71.refs_0_), channel_id=1, source_target_pairs={{0,4},{1,5},{2,6},{3,7},{4,0},{5,1},{6,2},{7,3},{8,12},{9,13},{10,... | collective-permute-start | bytes 1966088 | tf_op jit(solution)/shard_map/ppermute | solution.py:33
  42.0 53.9 %collective-permute-start.8 = (bf16[512,2560]{1,0:T(8,128)(2,1)S(1)}, bf16[512,2560]{1,0:T(8,128)(2,1)S(1)}, u32[]{:S(2)}, u32[]{:S(2)}) collective-permute-start(bf16[512,2560]{1,0:T(8,128)(2,1)S(1)} %bitcast.122), channel_id=1, source_target_pairs={{0,1},{1,0},{2,3},{3,2},{4,5},{5,4},{6,7},{7,6},{8,9},{9,8},{10,11... | collective-permute-start | bytes 7864328 | tf_op jit(solution)/shard_map/ppermute | solution.py:33
  48.1 49.4 %collective-permute-start.9 = (bf16[512,2560]{1,0:T(8,128)(2,1)S(1)}, bf16[512,2560]{1,0:T(8,128)(2,1)S(1)}, u32[]{:S(2)}, u32[]{:S(2)}) collective-permute-start(bf16[512,2560]{1,0:T(8,128)(2,1)S(1)} %bitcast.126), channel_id=1, source_target_pairs={{0,1},{1,0},{2,3},{3,2},{4,5},{5,4},{6,7},{7,6},{8,9},{9,8},{10,11... | collective-permute-start | bytes 7864328 | tf_op jit(solution)/shard_map/ppermute | solution.py:33
  55.2 8.9 %collective-permute-start.21 = (bf16[64,2560]{1,0:T(8,128)(2,1)S(1)}, bf16[64,2560]{1,0:T(8,128)(2,1)S(1)}, u32[]{:S(2)}, u32[]{:S(2)}) collective-permute-start(bf16[64,2560]{1,0:T(8,128)(2,1)S(1)} %slice.178), channel_id=1, source_target_pairs={{0,4},{1,5},{2,6},{3,7},{4,0},{5,1},{6,2},{7,3},{8,12},{9,13},{10,... | collective-permute-start | bytes 983048 | tf_op jit(solution)/shard_map/ppermute | solution.py:33
  64.0 8.2 %collective-permute-start.22 = (bf16[64,2560]{1,0:T(8,128)(2,1)S(1)}, bf16[64,2560]{1,0:T(8,128)(2,1)S(1)}, u32[]{:S(2)}, u32[]{:S(2)}) collective-permute-start(bf16[64,2560]{1,0:T(8,128)(2,1)S(1)} %slice.179), channel_id=1, source_target_pairs={{0,2},{1,3},{2,0},{3,1},{4,6},{5,7},{6,4},{7,5},{8,10},{9,11},{10,... | collective-permute-start | bytes 983048 | tf_op jit(solution)/shard_map/ppermute | solution.py:33
  72.3 18.2 %collective-permute-start.1 = (s32[2560,128]{1,0:T(8,128)S(1)}, s32[2560,128]{1,0:T(8,128)S(1)}, u32[]{:S(2)}, u32[]{:S(2)}) collective-permute-start(s32[2560,128]{1,0:T(8,128)S(1)} %get-tuple-element.38.refs_8_.refs_10_.refs_12_.refs_14_), channel_id=1, source_target_pairs={{0,1},{1,0},{2,3},{3,2},{4,5},{5,4},{6,7},{7,6},{8,9},{9,8},{10,11... | collective-permute-start | bytes 3932168 | tf_op jit(solution)/shard_map/ppermute | solution.py:33
  72.3 12.3 %collective-permute-start.31 = (bf16[64,2560]{1,0:T(8,128)(2,1)S(1)}, bf16[64,2560]{1,0:T(8,128)(2,1)S(1)}, u32[]{:S(2)}, u32[]{:S(2)}) collective-permute-start(bf16[64,2560]{1,0:T(8,128)(2,1)S(1)} %slice.182), channel_id=1, source_target_pairs={{0,4},{1,5},{2,6},{3,7},{4,0},{5,1},{6,2},{7,3},{8,12},{9,13},{10,... | collective-permute-start | bytes 983048 | tf_op jit(solution)/shard_map/ppermute | solution.py:33
  73.0 13.0 %collective-permute-start.32 = (bf16[64,2560]{1,0:T(8,128)(2,1)S(1)}, bf16[64,2560]{1,0:T(8,128)(2,1)S(1)}, u32[]{:S(2)}, u32[]{:S(2)}) collective-permute-start(bf16[64,2560]{1,0:T(8,128)(2,1)S(1)} %slice.183), channel_id=1, source_target_pairs={{0,2},{1,3},{2,0},{3,1},{4,6},{5,7},{6,4},{7,5},{8,10},{9,11},{10,... | collective-permute-start | bytes 983048 | tf_op jit(solution)/shard_map/ppermute | solution.py:33
  84.6 16.7 %collective-permute-start.7 = (bf16[256,1024]{1,0:T(8,128)(2,1)S(1)}, bf16[256,1024]{1,0:T(8,128)(2,1)S(1)}, u32[]{:S(2)}, u32[]{:S(2)}) collective-permute-start(bf16[256,1024]{1,0:T(8,128)(2,1)S(1)} %through.4), channel_id=1, source_target_pairs={{8,0},{16,8},{24,16},{9,1},{17,9},{25,17},{10,2},{18,10},{26,18},{... | collective-permute-start | bytes 1572872 | tf_op jit(solution)/shard_map/ppermute | solution.py:29
  86.0 44.9 %collective-permute-start.23 = (bf16[384,1024]{1,0:T(8,128)(2,1)S(1)}, bf16[384,1024]{1,0:T(8,128)(2,1)S(1)}, u32[]{:S(2)}, u32[]{:S(2)}) collective-permute-start(bf16[384,1024]{1,0:T(8,128)(2,1)S(1)} %through.6), channel_id=1, source_target_pairs={{8,0},{16,8},{24,16},{9,1},{17,9},{25,17},{10,2},{18,10},{26,18},{... | collective-permute-start | bytes 2359304 | tf_op jit(solution)/shard_map/ppermute | solution.py:29
  90.4 39.0 %collective-permute-start.18 = (bf16[256,1024]{1,0:T(8,128)(2,1)S(1)}, bf16[256,1024]{1,0:T(8,128)(2,1)S(1)}, u32[]{:S(2)}, u32[]{:S(2)}) collective-permute-start(bf16[256,1024]{1,0:T(8,128)(2,1)S(1)} %through.5), channel_id=1, source_target_pairs={{8,0},{16,8},{24,16},{9,1},{17,9},{25,17},{10,2},{18,10},{26,18},{... | collective-permute-start | bytes 1572872 | tf_op jit(solution)/shard_map/ppermute | solution.py:29
  95.9 49.3 %collective-permute-start.33 = (bf16[384,1024]{1,0:T(8,128)(2,1)S(1)}, bf16[384,1024]{1,0:T(8,128)(2,1)S(1)}, u32[]{:S(2)}, u32[]{:S(2)}) collective-permute-start(bf16[384,1024]{1,0:T(8,128)(2,1)S(1)} %through.7), channel_id=1, source_target_pairs={{8,0},{16,8},{24,16},{9,1},{17,9},{25,17},{10,2},{18,10},{26,18},{... | collective-permute-start | bytes 2359304 | tf_op jit(solution)/shard_map/ppermute | solution.py:29
  97.5 33.4 %copy-start.5 = (bf16[1,4,128,2560]{3,2,1,0:T(8,128)(2,1)S(1)}, bf16[1,4,128,2560]{3,2,1,0:T(8,128)(2,1)}, u32[]{:S(2)}) copy-start(bf16[1,4,128,2560]{3,2,1,0:T(8,128)(2,1)} %param.13) | copy-start | bytes 7864324
  97.5 79.6 %collective-permute-start.16 = (bf16[2,2,32,320]{3,2,1,0:T(8,128)(2,1)S(1)}, bf16[2,2,32,320]{3,2,1,0:T(8,128)(2,1)S(1)}, u32[]{:S(2)}, u32[]{:S(2)}) collective-permute-start(bf16[2,2,32,320]{3,2,1,0:T(8,128)(2,1)S(1)} %get-tuple-element.75), channel_id=1, source_target_pairs={{0,2},{1,3},{2,0},{3,1},{4,6},{5,7},{6,4},{7,5},{8,10},{9,11},{10,... | collective-permute-start | bytes 245768 | tf_op jit(solution)/shard_map/ppermute | solution.py:33
  107.6 49.0 %collective-permute-start.10 = (bf16[2,128,640]{2,1,0:T(8,128)(2,1)S(1)}, bf16[2,128,640]{2,1,0:T(8,128)(2,1)S(1)}, u32[]{:S(2)}, u32[]{:S(2)}) collective-permute-start(bf16[2,128,640]{2,1,0:T(8,128)(2,1)S(1)} %get-tuple-element.41), channel_id=1, source_target_pairs={{0,2},{1,3},{2,0},{3,1},{4,6},{5,7},{6,4},{7,5},{8,10},{9,11},{10,... | collective-permute-start | bytes 983048 | tf_op jit(solution)/shard_map/ppermute | solution.py:33
  129.4 49.5 %collective-permute-start.12 = (bf16[2,128,640]{2,1,0:T(8,128)(2,1)S(1)}, bf16[2,128,640]{2,1,0:T(8,128)(2,1)S(1)}, u32[]{:S(2)}, u32[]{:S(2)}) collective-permute-start(bf16[2,128,640]{2,1,0:T(8,128)(2,1)S(1)} %get-tuple-element.43), channel_id=1, source_target_pairs={{0,4},{1,5},{2,6},{3,7},{4,0},{5,1},{6,2},{7,3},{8,12},{9,13},{10,... | collective-permute-start | bytes 983048 | tf_op jit(solution)/shard_map/ppermute | solution.py:33
  142.5 14.5 %collective-permute-start.24 = (bf16[2,256,640]{2,1,0:T(8,128)(2,1)S(1)}, bf16[2,256,640]{2,1,0:T(8,128)(2,1)S(1)}, u32[]{:S(2)}, u32[]{:S(2)}) collective-permute-start(bf16[2,256,640]{2,1,0:T(8,128)(2,1)S(1)} %get-tuple-element.47), channel_id=1, source_target_pairs={{0,2},{1,3},{2,0},{3,1},{4,6},{5,7},{6,4},{7,5},{8,10},{9,11},{10,... | collective-permute-start | bytes 1966088 | tf_op jit(solution)/shard_map/ppermute | solution.py:33
  145.3 17.7 %collective-permute-start.26 = (bf16[2,256,640]{2,1,0:T(8,128)(2,1)S(1)}, bf16[2,256,640]{2,1,0:T(8,128)(2,1)S(1)}, u32[]{:S(2)}, u32[]{:S(2)}) collective-permute-start(bf16[2,256,640]{2,1,0:T(8,128)(2,1)S(1)} %get-tuple-element.49), channel_id=1, source_target_pairs={{0,4},{1,5},{2,6},{3,7},{4,0},{5,1},{6,2},{7,3},{8,12},{9,13},{10,... | collective-permute-start | bytes 1966088 | tf_op jit(solution)/shard_map/ppermute | solution.py:33
  156.7 15.5 %collective-permute-start.34 = (bf16[2,256,640]{2,1,0:T(8,128)(2,1)S(1)}, bf16[2,256,640]{2,1,0:T(8,128)(2,1)S(1)}, u32[]{:S(2)}, u32[]{:S(2)}) collective-permute-start(bf16[2,256,640]{2,1,0:T(8,128)(2,1)S(1)} %get-tuple-element.53), channel_id=1, source_target_pairs={{0,2},{1,3},{2,0},{3,1},{4,6},{5,7},{6,4},{7,5},{8,10},{9,11},{10,... | collective-permute-start | bytes 1966088 | tf_op jit(solution)/shard_map/ppermute | solution.py:33
  157.1 19.9 %collective-permute-start.36 = (bf16[2,256,640]{2,1,0:T(8,128)(2,1)S(1)}, bf16[2,256,640]{2,1,0:T(8,128)(2,1)S(1)}, u32[]{:S(2)}, u32[]{:S(2)}) collective-permute-start(bf16[2,256,640]{2,1,0:T(8,128)(2,1)S(1)} %get-tuple-element.55), channel_id=1, source_target_pairs={{0,4},{1,5},{2,6},{3,7},{4,0},{5,1},{6,2},{7,3},{8,12},{9,13},{10,... | collective-permute-start | bytes 1966088 | tf_op jit(solution)/shard_map/ppermute | solution.py:33
  162.9 17.8 %collective-permute-start.11 = (bf16[128,640]{1,0:T(8,128)(2,1)S(1)}, bf16[128,640]{1,0:T(8,128)(2,1)S(1)}, u32[]{:S(2)}, u32[]{:S(2)}) collective-permute-start(bf16[128,640]{1,0:T(8,128)(2,1)S(1)} %fusion.12), channel_id=1, source_target_pairs={{0,4},{1,5},{2,6},{3,7},{4,0},{5,1},{6,2},{7,3},{8,12},{9,13},{10,... | collective-permute-start | bytes 491528 | tf_op jit(solution)/shard_map/ppermute | solution.py:33
  172.2 22.4 %collective-permute-start.25 = (bf16[256,640]{1,0:T(8,128)(2,1)S(1)}, bf16[256,640]{1,0:T(8,128)(2,1)S(1)}, u32[]{:S(2)}, u32[]{:S(2)}) collective-permute-start(bf16[256,640]{1,0:T(8,128)(2,1)S(1)} %fusion.5), channel_id=1, source_target_pairs={{0,4},{1,5},{2,6},{3,7},{4,0},{5,1},{6,2},{7,3},{8,12},{9,13},{10,... | collective-permute-start | bytes 983048 | tf_op jit(solution)/shard_map/ppermute | solution.py:33
  177.0 17.6 %collective-permute-start.27 = (bf16[256,640]{1,0:T(8,128)(2,1)S(1)}, bf16[256,640]{1,0:T(8,128)(2,1)S(1)}, u32[]{:S(2)}, u32[]{:S(2)}) collective-permute-start(bf16[256,640]{1,0:T(8,128)(2,1)S(1)} %fusion.6), channel_id=1, source_target_pairs={{0,2},{1,3},{2,0},{3,1},{4,6},{5,7},{6,4},{7,5},{8,10},{9,11},{10,... | collective-permute-start | bytes 983048 | tf_op jit(solution)/shard_map/ppermute | solution.py:33
  177.1 19.3 %collective-permute-start.35 = (bf16[256,640]{1,0:T(8,128)(2,1)S(1)}, bf16[256,640]{1,0:T(8,128)(2,1)S(1)}, u32[]{:S(2)}, u32[]{:S(2)}) collective-permute-start(bf16[256,640]{1,0:T(8,128)(2,1)S(1)} %fusion.7), channel_id=1, source_target_pairs={{0,4},{1,5},{2,6},{3,7},{4,0},{5,1},{6,2},{7,3},{8,12},{9,13},{10,... | collective-permute-start | bytes 983048 | tf_op jit(solution)/shard_map/ppermute | solution.py:33
  178.9 17.5 %collective-permute-start.37 = (bf16[256,640]{1,0:T(8,128)(2,1)S(1)}, bf16[256,640]{1,0:T(8,128)(2,1)S(1)}, u32[]{:S(2)}, u32[]{:S(2)}) collective-permute-start(bf16[256,640]{1,0:T(8,128)(2,1)S(1)} %fusion.8), channel_id=1, source_target_pairs={{0,2},{1,3},{2,0},{3,1},{4,6},{5,7},{6,4},{7,5},{8,10},{9,11},{10,... | collective-permute-start | bytes 983048 | tf_op jit(solution)/shard_map/ppermute | solution.py:33
  180.7 12.7 %collective-permute-start.13 = (bf16[128,640]{1,0:T(8,128)(2,1)S(1)}, bf16[128,640]{1,0:T(8,128)(2,1)S(1)}, u32[]{:S(2)}, u32[]{:S(2)}) collective-permute-start(bf16[128,640]{1,0:T(8,128)(2,1)S(1)} %fusion.13), channel_id=1, source_target_pairs={{0,2},{1,3},{2,0},{3,1},{4,6},{5,7},{6,4},{7,5},{8,10},{9,11},{10,... | collective-permute-start | bytes 491528 | tf_op jit(solution)/shard_map/ppermute | solution.py:33
  194.5 19.2 %collective-permute-start.14 = (bf16[320,512]{1,0:T(8,128)(2,1)S(1)}, bf16[320,512]{1,0:T(8,128)(2,1)S(1)}, u32[]{:S(2)}, u32[]{:S(2)}) collective-permute-start(bf16[320,512]{1,0:T(8,128)(2,1)S(1)} %get-tuple-element.45), channel_id=1, source_target_pairs={{0,1},{1,0},{2,3},{3,2},{4,5},{5,4},{6,7},{7,6},{8,9},{9,8},{10,11... | collective-permute-start | bytes 983048 | tf_op jit(solution)/shard_map/ppermute | solution.py:33
  195.8 12.7 %collective-permute-start.28 = (bf16[320,512]{1,0:T(8,128)(2,1)S(1)}, bf16[320,512]{1,0:T(8,128)(2,1)S(1)}, u32[]{:S(2)}, u32[]{:S(2)}) collective-permute-start(bf16[320,512]{1,0:T(8,128)(2,1)S(1)} %get-tuple-element.51), channel_id=1, source_target_pairs={{0,1},{1,0},{2,3},{3,2},{4,5},{5,4},{6,7},{7,6},{8,9},{9,8},{10,11... | collective-permute-start | bytes 983048 | tf_op jit(solution)/shard_map/ppermute | solution.py:33
  197.7 5.4 %collective-permute-start.38 = (bf16[320,512]{1,0:T(8,128)(2,1)S(1)}, bf16[320,512]{1,0:T(8,128)(2,1)S(1)}, u32[]{:S(2)}, u32[]{:S(2)}) collective-permute-start(bf16[320,512]{1,0:T(8,128)(2,1)S(1)} %get-tuple-element.57), channel_id=1, source_target_pairs={{0,1},{1,0},{2,3},{3,2},{4,5},{5,4},{6,7},{7,6},{8,9},{9,8},{10,11... | collective-permute-start | bytes 983048 | tf_op jit(solution)/shard_map/ppermute | solution.py:33
  197.9 5.2 %collective-permute-start.17 = (bf16[2,2,32,320]{3,2,1,0:T(8,128)(2,1)S(1)}, bf16[2,2,32,320]{3,2,1,0:T(8,128)(2,1)S(1)}, u32[]{:S(2)}, u32[]{:S(2)}) collective-permute-start(bf16[2,2,32,320]{3,2,1,0:T(8,128)(2,1)S(1)} %get-tuple-element.73), channel_id=1, source_target_pairs={{0,4},{1,5},{2,6},{3,7},{4,0},{5,1},{6,2},{7,3},{8,12},{9,13},{10,... | collective-permute-start | bytes 245768 | tf_op jit(solution)/shard_map/ppermute | solution.py:33
  216.9 1.4 collective-permute-start.42
  217.1 2.4 %collective-permute-start.39 = (bf16[4,32,2048]{2,1,0:T(8,128)(2,1)S(1)}, bf16[4,32,2048]{2,1,0:T(8,128)(2,1)S(1)}, u32[]{:S(2)}, u32[]{:S(2)}) collective-permute-start(bf16[4,32,2048]{2,1,0:T(8,128)(2,1)S(1)} %slice_bitcast_fusion), channel_id=1, source_target_pairs={{0,1},{1,0},{2,3},{3,2},{4,5},{5,4},{6,7},{7,6},{8,9},{9,8},{10,11... | collective-permute-start | bytes 1572872 | tf_op jit(solution)/shard_map/ppermute | solution.py:33
  218.4 4.7 %collective-permute-start.43 = (bf16[2,32,512]{2,1,0:T(8,128)(2,1)S(1)}, bf16[2,32,512]{2,1,0:T(8,128)(2,1)S(1)}, u32[]{:S(2)}, u32[]{:S(2)}) collective-permute-start(bf16[2,32,512]{2,1,0:T(8,128)(2,1)S(1)} %slice_bitcast_fusion.14), channel_id=1, source_target_pairs={{0,2},{1,3},{2,0},{3,1},{4,6},{5,7},{6,4},{7,5},{8,10},{9,11},{10,... | collective-permute-start | bytes 196616 | tf_op jit(solution)/shard_map/ppermute | solution.py:33
  219.6 8.7 %collective-permute-start.40 = (bf16[2,32,2048]{2,1,0:T(8,128)(2,1)S(1)}, bf16[2,32,2048]{2,1,0:T(8,128)(2,1)S(1)}, u32[]{:S(2)}, u32[]{:S(2)}) collective-permute-start(bf16[2,32,2048]{2,1,0:T(8,128)(2,1)S(1)} %slice_bitcast_fusion.2), channel_id=1, source_target_pairs={{0,2},{1,3},{2,0},{3,1},{4,6},{5,7},{6,4},{7,5},{8,10},{9,11},{10,... | collective-permute-start | bytes 786440 | tf_op jit(solution)/shard_map/ppermute | solution.py:33
  223.1 6.8 %collective-permute-start.44 = (bf16[32,512]{1,0:T(8,128)(2,1)S(1)}, bf16[32,512]{1,0:T(8,128)(2,1)S(1)}, u32[]{:S(2)}, u32[]{:S(2)}) collective-permute-start(bf16[32,512]{1,0:T(8,128)(2,1)S(1)} %slice_bitcast_fusion.16), channel_id=1, source_target_pairs={{0,4},{1,5},{2,6},{3,7},{4,0},{5,1},{6,2},{7,3},{8,12},{9,13},{10,... | collective-permute-start | bytes 98312 | tf_op jit(solution)/shard_map/ppermute | solution.py:33
  228.4 5.1 %collective-permute-start.41 = (bf16[32,2048]{1,0:T(8,128)(2,1)S(1)}, bf16[32,2048]{1,0:T(8,128)(2,1)S(1)}, u32[]{:S(2)}, u32[]{:S(2)}) collective-permute-start(bf16[32,2048]{1,0:T(8,128)(2,1)S(1)} %slice_bitcast_fusion.6), channel_id=1, source_target_pairs={{0,4},{1,5},{2,6},{3,7},{4,0},{5,1},{6,2},{7,3},{8,12},{9,13},{10,... | collective-permute-start | bytes 393224 | tf_op jit(solution)/shard_map/ppermute | solution.py:33
  (11 other events, 108.4 us)

commit v2 on v1

v2 whole, which is shorter than its diff:
```python
import functools

import jax
import jax.numpy as jnp
from jax import lax
from jax.experimental import pallas as pl
from jax.experimental.pallas import tpu as pltpu
from jax.sharding import PartitionSpec as P

LEAK_RATE = 0.5
LEARN_RATE = 0.002
FIRST_DECAY = 0.9
SECOND_DECAY = 0.95
EPSILON = 1e-08
WEIGHT_DECAY = 0.1
FIRST_CORRECTION = 1.0 - 0.9**10
SECOND_CORRECTION = 1.0 - 0.95**10

LANES = 128
PARTS = 8
CHIPS = 4
BF16 = jnp.bfloat16
F32 = jnp.float32


def passed_along(shard, axis, by):
    count = lax.axis_size(axis)
    pairs = [(i, i + by) for i in range(count) if 0 <= i + by < count]
    return lax.ppermute(shard, axis, pairs)


def swapped(shard, bit):
    return lax.ppermute(shard, "dp", [(i, i ^ bit) for i in range(PARTS)])


def over_core(shard):
    return swapped(shard, 1)


def over_x(shard):
    return swapped(shard, 2)


def over_y(shard):
    return swapped(shard, 4)


def tied(held, *earlier):
    return lax.optimization_barrier((held, *earlier))[0]


SMALL = pl.CostEstimate(flops=1, bytes_accessed=1, transcendentals=0)
VMEM = 60 << 20


def adam(params, first, second, gradient):
    fresh_first = FIRST_DECAY * first + (1.0 - FIRST_DECAY) * gradient
    fresh_second = SECOND_DECAY * second + (1.0 - SECOND_DECAY) * gradient * gradient
    direction = (
        fresh_first / FIRST_CORRECTION / (jnp.sqrt(fresh_second / SECOND_CORRECTION) + EPSILON)
    )
    fresh_params = params - LEARN_RATE * (direction + WEIGHT_DECAY * params)
    return fresh_params, fresh_first, fresh_second


def prepare_kernel(groups, where, *refs):
    grads, own, arriving = refs[0:2], refs[2:4], refs[4:6]
    membrane_t, grads_t, window_t = refs[6:]
    steps, tok_rows = grads[0].shape[0], grads[0].shape[1]
    rows = own[0].shape[1] // 2
    chip = pl.program_id(0)
    for side in range(2):
        window = own[side][...].T
        later = arriving[side][...].T
        carried = jnp.zeros(window.shape, F32)
        values = []
        for moment in reversed(range(steps)):
            now = grads[side][moment].astype(F32).T
            bit = jnp.bitwise_and(jnp.right_shift(window, moment), 1).astype(F32)
            carried = bit * now + LEAK_RATE * carried
            lanes = pl.ds((side * steps + moment) * tok_rows, tok_rows)
            membrane_t[:, lanes] = carried.astype(BF16)
            values.append((lanes, now.astype(BF16)))
        for core in range(2):

            @pl.when(where[1] == core)
            def _(core=core, later=later, values=values, side=side):
                for begin, width in groups:
                    at = begin if core == 0 else 2 * rows - begin - width
                    place = pl.ds(pl.multiple_of(CHIPS * begin + chip * width, width), width)
                    window_t[place, pl.ds(side * tok_rows, tok_rows)] = later[at : at + width]
                    for lanes, value in values:
                        grads_t[place, lanes] = value[at : at + width]


def prepare(where, grads, own, arriving, groups, rows):
    steps, tok_rows, features = grads[0].shape
    block = 2 * rows
    tokens = 2 * steps * tok_rows
    cut = CHIPS * rows
    outs = (
        jax.ShapeDtypeStruct((features, tokens), BF16),
        jax.ShapeDtypeStruct((cut, tokens), BF16),
        jax.ShapeDtypeStruct((cut, 2 * tok_rows), jnp.int32),
    )
    whole = [pl.BlockSpec(o.shape, lambda i, s: (0, 0)) for o in outs[1:]]
    return pl.pallas_call(
        functools.partial(prepare_kernel, groups),
        out_shape=outs,
        grid_spec=pltpu.PrefetchScalarGridSpec(
            num_scalar_prefetch=1,
            grid=(features // block,),
            in_specs=[pl.BlockSpec((steps, tok_rows, block), lambda i, s: (0, 0, i))] * 2
            + [pl.BlockSpec((tok_rows, block), lambda i, s: (0, i))] * 4,
            out_specs=[pl.BlockSpec((block, tokens), lambda i, s: (i, 0)), *whole],
        ),
        cost_estimate=SMALL,
        compiler_params=pltpu.CompilerParams(vmem_limit_bytes=VMEM),
        name="prepare",
    )(where, *grads, *own, *arriving)


def compact_block(s, relative, begin, width):
    return CHIPS * begin // width + jnp.bitwise_xor(s[0], relative)


def column_block(s, relative, begin, width, rows):
    chip = jnp.bitwise_xor(s[0], relative)
    at = jnp.where(s[1] == 0, begin, 2 * rows - begin - width)
    return (chip * (2 * rows) + at) // width


def through_kernel(count, pieces, where, *refs):
    weights, held = refs[:count], refs[count]
    grads = refs[count + 1 : count + 1 + len(pieces)]
    out, total = refs[count + 1 + len(pieces) :]
    step = pl.program_id(0)
    rows = jnp.concatenate([w[...] for w in weights], axis=0)
    half = held.shape[1] // 2
    for side in range(2):
        lanes = pl.ds(side * half, half)
        term = jnp.dot(rows, held[:, lanes], preferred_element_type=F32)

        @pl.when(step == 0)
        def _(lanes=lanes, term=term):
            total[:, lanes] = term

        @pl.when(step != 0)
        def _(lanes=lanes, term=term):
            at = 0
            for (_, _, width), grad in zip(pieces, grads):
                value = total[pl.ds(at, width), lanes] + term[at : at + width]
                out[pl.ds(at, width), lanes] = (value + grad[:, lanes].astype(F32)).astype(BF16)
                at += width


def through(where, pieces, weights, membrane_t, grads_t):
    features, tokens = membrane_t.shape
    count = sum(p[2] for p in pieces)
    chunk = features // 2
    out = jax.ShapeDtypeStruct((count, tokens), BF16)
    specs = [pl.BlockSpec((w.shape[0], chunk), lambda i, s: (0, i)) for w in weights]
    specs.append(pl.BlockSpec((chunk, tokens), lambda i, s: (i, 0)))
    for relative, begin, width in pieces:
        specs.append(
            pl.BlockSpec(
                (width, tokens),
                functools.partial(
                    lambda i, s, r, b, w: (compact_block(s, r, b, w), 0), r=relative, b=begin, w=width
                ),
            )
        )
    return pl.pallas_call(
        functools.partial(through_kernel, len(weights), pieces),
        out_shape=out,
        grid_spec=pltpu.PrefetchScalarGridSpec(
            num_scalar_prefetch=1,
            grid=(2,),
            in_specs=specs,
            out_specs=pl.BlockSpec((count, tokens), lambda i, s: (0, 0)),
            scratch_shapes=[pltpu.VMEM((count, tokens), F32)],
        ),
        cost_estimate=SMALL,
        compiler_params=pltpu.CompilerParams(vmem_limit_bytes=VMEM),
        name="through",
    )(where, *weights, membrane_t, *([grads_t] * len(pieces)))


def partial_kernel(sources, count, width, where, *refs):
    own, windows = refs[:CHIPS], refs[CHIPS : 2 * CHIPS]
    arrived = refs[2 * CHIPS : 2 * CHIPS + count]
    refs = refs[2 * CHIPS + count :]
    acts = refs[:4]
    x_keep, x_send, y_keep, y_send, held = refs[4:]
    step = pl.program_id(0)
    tokens = own[0].shape[1]
    rows = windows[0].shape[1] // 2
    moments = tokens // (2 * rows)

    @pl.when(step == 0)
    def _():
        for chip in range(CHIPS):
            held[pl.ds(chip * width, width), :tokens] = own[chip][...]
        for relative in range(CHIPS):
            chip = jnp.bitwise_xor(where[0], relative)
            place = pl.ds(pl.multiple_of(chip * width, width), width)
            array, begin = sources[relative]
            for side in range(2):
                window = windows[relative][:, side * rows : (side + 1) * rows]
                carried = jnp.zeros(window.shape, F32)
                for moment in reversed(range(moments)):
                    at = (side * moments + moment) * rows
                    now = arrived[array][pl.ds(begin, width), pl.ds(at, rows)].astype(F32)
                    bit = jnp.bitwise_and(jnp.right_shift(window, moment), 1).astype(F32)
                    carried = bit * now + LEAK_RATE * carried
                    held[place, pl.ds(tokens + at, rows)] = carried.astype(BF16)

    value = None
    for index, act in enumerate(acts):
        term = lax.dot_general(
            act[...],
            held[:, pl.ds(index * tokens // 2, tokens // 2)],
            (((0,), (1,)), ((), ())),
            preferred_element_type=F32,
        )
        value = term if value is None else value + term
    value = value.astype(BF16)
    first, last = value[:, : 2 * width], value[:, 2 * width :]

    @pl.when(jnp.logical_or(step == 0, step == 2))
    def _():
        x_send[0] = first

    @pl.when(jnp.logical_or(step == 1, step == 3))
    def _():
        x_keep[0] = first

    @pl.when(step < 2)
    def _():
        y_send[0] = last

    @pl.when(step >= 2)
    def _():
        y_keep[0] = last


def partials(where, begin, width, membrane_t, window_t, arrived, sources, acts, rows):
    tokens = membrane_t.shape[1]
    block = 2 * rows
    specs, operands = [], []
    for chip in range(CHIPS):

        def index(i, s, chip=chip):
            return (column_block(s, jnp.bitwise_xor(s[0], chip), begin, width, rows), 0)

        specs.append(pl.BlockSpec((width, tokens), index))
        operands.append(membrane_t)
    for relative in range(CHIPS):

        def index(i, s, relative=relative):
            return (compact_block(s, relative, begin, width), 0)

        specs.append(pl.BlockSpec((width, window_t.shape[1]), index))
        operands.append(window_t)
    for array in arrived:
        specs.append(pl.BlockSpec(array.shape, lambda i, s: (0, 0)))
        operands.append(array)
    for act in acts:
        specs.append(
            pl.BlockSpec((act.shape[0], block), lambda i, s: (0, jnp.bitwise_xor(s[0], 3 - i)))
        )
        operands.append(act)
    piece = jax.ShapeDtypeStruct((2, block, 2 * width), BF16)

    def out_spec(index):
        return pl.BlockSpec((1, block, 2 * width), lambda i, s: (index(i), 0, 0))

    return pl.pallas_call(
        functools.partial(partial_kernel, sources, len(arrived), width),
        out_shape=(piece,) * 4,
        grid_spec=pltpu.PrefetchScalarGridSpec(
            num_scalar_prefetch=1,
            grid=(CHIPS,),
            in_specs=specs,
            out_specs=[
                out_spec(lambda i: jnp.where(i < 3, 1, 0)),
                out_spec(lambda i: jnp.where(i < 2, 1, 0)),
                out_spec(lambda i: jnp.where(i < 3, 1, 0)),
                out_spec(lambda i: jnp.where(i < 1, 1, 0)),
            ],
            scratch_shapes=[pltpu.VMEM((CHIPS * width, 2 * tokens), BF16)],
        ),
        cost_estimate=SMALL,
        compiler_params=pltpu.CompilerParams(vmem_limit_bytes=28 << 20),
        name="partials",
    )(where, *operands)


def gather_up_kernel(width, where, xk, xr, xs, yk, yr, ys, mine, other):
    rows = mine.shape[0]
    parts = []
    for kept, received, summed in ((xk, xr, xs), (yk, yr, ys)):
        value = kept[0].astype(F32) + received[0].astype(F32) + summed[...].astype(F32)
        parts.append(value.astype(BF16))
    value = jnp.concatenate(parts, axis=1)
    if width < LANES:
        pieces = [value[:, chip * width : (chip + 1) * width] for chip in range(CHIPS)]
        blank = jnp.zeros((value.shape[0], LANES - width), BF16)
        low = jnp.concatenate([p for piece in pieces for p in (piece, blank)], axis=1)
        high = jnp.concatenate([p for piece in pieces for p in (blank, piece)], axis=1)
        value = jnp.where(where[1] == 0, low.astype(F32), high.astype(F32)).astype(BF16)

    @pl.when(where[1] == 0)
    def _():
        mine[...] = value[:rows]
        other[...] = value[rows:]

    @pl.when(where[1] != 0)
    def _():
        mine[...] = value[rows:]
        other[...] = value[:rows]


def gather_up(where, width, kept_x, got_x, sum_x, kept_y, got_y, sum_y, rows):
    first = pl.BlockSpec((1, 2 * rows, 2 * width), lambda i, s: (0, 0, 0))
    whole = pl.BlockSpec((2 * rows, 2 * width), lambda i, s: (0, 0))
    out = jax.ShapeDtypeStruct((rows, CHIPS * LANES), BF16)
    spec = pl.BlockSpec(out.shape, lambda i, s: (0, 0))
    return pl.pallas_call(
        functools.partial(gather_up_kernel, width),
        out_shape=(out, out),
        grid_spec=pltpu.PrefetchScalarGridSpec(
            num_scalar_prefetch=1,
            grid=(1,),
            in_specs=[first, first, whole, first, first, whole],
            out_specs=[spec, spec],
        ),
        cost_estimate=SMALL,
        compiler_params=pltpu.CompilerParams(vmem_limit_bytes=12 << 20),
        name="gather_up",
    )(where, kept_x, got_x, sum_x, kept_y, got_y, sum_y)


def update_kernel(whole, where, mine, theirs, params, first, second, acts, *refs):
    fresh_params, fresh_first, fresh_second, currents = refs[-4:]
    if whole:
        own = pl.program_id(1) == where[1]
        gradient = jnp.where(own, mine[...].astype(F32), theirs[...].astype(F32))
    else:
        gradient = mine[...].astype(F32) + theirs[...].astype(F32)
    new = adam(params[...], first[...], second[...], gradient)
    fresh_params[...], fresh_first[...], fresh_second[...] = new
    currents[...] = jnp.dot(
        acts[...], new[0].astype(BF16), preferred_element_type=F32
    ).astype(BF16)


def update(where, begin, width, mine, theirs, state, acts, held):
    params = state[0]
    rows, features = params.shape
    per_chip = 2 * rows // LANES
    whole = width == LANES
    cores = 2 if whole else 1
    tile_of_core = [begin // LANES, (2 * rows - begin - width) // LANES]

    def tile(i, j, s):
        inside = jnp.where(j == 0, tile_of_core[0], tile_of_core[1])
        return (0, per_chip * i + inside)

    block = pl.BlockSpec((rows, LANES), tile)
    grads = pl.BlockSpec((rows, LANES), lambda i, j, s: (0, i))
    current_shape = jax.ShapeDtypeStruct((acts.shape[0], CHIPS * cores * LANES), BF16)
    operands = [where, mine, theirs, *state, acts]
    specs = [grads, grads, block, block, block, pl.BlockSpec(acts.shape, lambda i, j, s: (0, 0))]
    aliases = {}
    if held is not None:
        for index, array in enumerate(held):
            aliases[len(operands)] = index
            operands.append(array)
            specs.append(pl.BlockSpec(memory_space=pl.ANY))
    shape = jax.ShapeDtypeStruct((rows, features), F32)
    *fresh, currents = pl.pallas_call(
        functools.partial(update_kernel, whole),
        out_shape=(shape, shape, shape, current_shape),
        grid_spec=pltpu.PrefetchScalarGridSpec(
            num_scalar_prefetch=1,
            grid=(CHIPS, cores),
            in_specs=specs,
            out_specs=[
                block,
                block,
                block,
                pl.BlockSpec((acts.shape[0], LANES), lambda i, j, s: (0, cores * i + j)),
            ],
        ),
        input_output_aliases=aliases,
        cost_estimate=pl.CostEstimate(
            flops=2 * acts.size * CHIPS * cores * LANES,
            bytes_accessed=24 * rows * CHIPS * cores * LANES,
            transcendentals=0,
        ),
        compiler_params=pltpu.CompilerParams(vmem_limit_bytes=8 << 20),
        name="update",
    )(*operands)
    return fresh, currents


def columns_to_owners(tokens, device):
    count, features = tokens.shape
    width = features // PARTS
    cut = tokens.reshape(count, PARTS, width).transpose(1, 0, 2)
    cut = cut.reshape(2, 2, 2, count, width)
    for axis, bit in ((0, 4), (1, 2), (2, 1)):
        cut = jnp.where(jnp.bitwise_and(device, bit) != 0, jnp.flip(cut, axis), cut)
    held = cut.transpose(2, 0, 1, 3, 4)
    held = jnp.stack([held[0], over_core(held[1])])
    held = held.transpose(2, 0, 1, 3, 4)
    held = jnp.stack([held[0], over_x(held[1])])
    held = held.transpose(3 - 1, 0, 1, 3, 4)
    held = jnp.stack([held[0], over_y(held[1])])
    return held.reshape(PARTS * count, width)


def summed_to_owners(terms):
    rows, columns = terms.shape
    held = terms.reshape(CHIPS, 2, rows // PARTS, columns)

    def add(kept, got):
        return (kept.astype(F32) + got.astype(F32)).astype(BF16)

    held = add(held[:, 0], over_core(held[:, 1]))
    held = held.reshape(2, 2, rows // PARTS, columns)
    held = add(held[:, 0], over_x(held[:, 1]))
    return add(held[0], over_y(held[1]))


def relay_shards(
    master,
    first_moment,
    second_moment,
    inputs_own,
    inputs_arriving,
    grads_own,
    windows_own,
    windows_arriving,
    next_inputs,
):
    params = master[0]
    rows, features = params.shape
    steps, tok_rows = grads_own.shape[1], grads_own.shape[2]
    tokens = steps * tok_rows
    device = lax.axis_index("dp")
    core = jnp.bitwise_and(device, 1)
    where = jnp.stack([device // 2, core]).astype(jnp.int32)

    widths = [LANES] * (rows // LANES) + ([rows % LANES] if rows % LANES else [])
    begins = [sum(widths[:i]) for i in range(len(widths))]
    groups = list(zip(begins, widths))

    held = []
    for begin, width in groups:
        at = jnp.where(core == 0, begin, rows - begin - width)
        source = params if not held else tied(params, held[0])
        held.append(lax.dynamic_slice_in_dim(source, at, width, 0).astype(BF16))

    def forward(by_x, by_y, *after):
        half = by_x.shape[0] // 2
        first, second = by_x[:half], by_y[half:]
        if after:
            first, second = tied(first, *after), tied(second, *after)
        return over_y(first), over_x(second)

    x0, y0 = over_x(held[0]), over_y(held[0])
    both = []
    for array in (grads_own, windows_own, windows_arriving):
        both.append((array[0], over_core(array[0])))
    piece = tied(held[1], both[0][1])
    x1, y1 = over_x(piece), over_y(piece)
    membrane_t, grads_t, window_t = prepare(where, *both, groups, rows)
    d0 = forward(x0, y0, membrane_t)

    (b0, w0), (b1, w1), (b2, w2) = groups

    def send(pieces, weights):
        sent = through(where, pieces, weights, membrane_t, grads_t)
        return sent, passed_along(sent, "section", -1)

    sent_a, got_a = send(
        [(0, b0, w0), (0, b1, w1), (1, b0, w0), (2, b0, w0)], [held[0], held[1], x0, y0]
    )
    piece = tied(held[2], x1, y1, sent_a)
    x2, y2 = over_x(piece), over_y(piece)
    acts = []
    for array in (inputs_own, inputs_arriving):
        flat = array[0].reshape(tokens, features)
        acts += [flat, over_core(tied(flat, x2, y2))]
    sent_b, got_b = send(
        [(3, b0, w0), (1, b1, w1), (2, b1, w1)], [*d0, x1, y1]
    )
    d1 = forward(x1, y1, sent_a)
    d2 = forward(x2, y2, sent_b)
    sent_c, got_c = send(
        [(3, b1, w1), (0, b2, w2), (1, b2, w2), (2, b2, w2), (3, b2, w2)],
        [*d1, held[2], tied(x2, got_a), y2, *d2],
    )

    def sum_up(g, arrived, sources, *after):
        begin, width = groups[g]
        if after:
            arrived = tied(arrived, *after)
        return partials(
            where, begin, width, membrane_t, window_t, arrived, sources, acts, rows
        )

    def first_stage(pieces):
        return over_x(pieces[1]), over_y(pieces[3])

    def second_stage(pieces, got):
        pass_y = (pieces[0][1].astype(F32) + got[0][1].astype(F32)).astype(BF16)
        pass_x = (pieces[2][1].astype(F32) + got[1][1].astype(F32)).astype(BF16)
        return over_y(pass_y), over_x(pass_x), (pass_y, pass_x)

    state = (params, first_moment[0], second_moment[0])

    def finish(g, pieces, got, sums, fresh, *after):
        begin, width = groups[g]
        sum_x = tied(sums[0], *after) if after else sums[0]
        mine, other = gather_up(
            where, width, pieces[0], got[0], sum_x, pieces[2], got[1], sums[1], rows
        )
        return update(where, begin, width, mine, over_core(other), state, acts_here, fresh)

    pieces0 = sum_up(
        0, (got_a, got_b), [(0, 0), (0, w0 + w1), (0, 2 * w0 + w1), (1, 0)], sent_c
    )
    got0 = first_stage(pieces0)
    acts_here = columns_to_owners(tied(next_inputs[0], sent_c), device)
    pieces1 = sum_up(
        1, (got_a, got_b, got_c), [(0, w0), (1, w0), (1, w0 + w1), (2, 0)], pieces0[0]
    )
    got1 = first_stage(pieces1)
    sums0 = second_stage(pieces0, got0)
    pieces2 = sum_up(
        2, (got_c,), [(0, w1 + r * w2) for r in range(CHIPS)], pieces1[0], *sums0[2]
    )
    got2 = first_stage(pieces2)
    sums1 = second_stage(pieces1, got1)
    fresh, current0 = finish(0, pieces0, got0, sums0, None, pieces2[0])
    sums2 = second_stage(pieces2, got2)
    fresh, current1 = finish(1, pieces1, got1, sums1, fresh)
    fresh, current2 = finish(2, pieces2, got2, sums2, fresh, current1)
    last = len(groups) - 1
    currents = [current0, current1, current2]

    early = summed_to_owners(jnp.concatenate(currents[:last], axis=1))
    late = summed_to_owners(currents[last])
    count = early.shape[0]
    tiles = [None] * (2 * rows // LANES)
    for g, (begin, width) in enumerate(groups):
        if g < last:
            size = CHIPS * 2 * LANES
            whole = early[:, g * size : (g + 1) * size].reshape(count, CHIPS, 2, LANES)
            tiles[begin // LANES] = whole[:, :, 0]
            tiles[(2 * rows - begin - width) // LANES] = whole[:, :, 1]
        else:
            tiles[begin // LANES] = late.reshape(count, CHIPS, LANES)
    next_currents = jnp.stack(tiles, axis=2).reshape(count, features)
    return (fresh[0][None], fresh[1][None], fresh[2][None], next_currents[None])


def membrane_grads(gradients, windows):
    carried = jnp.zeros(gradients.shape[1:], F32)
    results = []
    for moment in reversed(range(gradients.shape[0])):
        window = jnp.bitwise_and(jnp.right_shift(windows, moment), 1).astype(F32)
        carried = window * gradients[moment].astype(F32) + LEAK_RATE * carried
        results = [carried] + results
    return jnp.stack(results).astype(BF16)


def plain_shards(
    master,
    first_moment,
    second_moment,
    inputs_own,
    inputs_arriving,
    grads_own,
    windows_own,
    windows_arriving,
    next_inputs,
):
    params = master[0]
    timesteps, tok_rows, features = (grads_own.shape[1], grads_own.shape[2], grads_own.shape[3])
    flat_rows = timesteps * tok_rows
    membrane_own = membrane_grads(grads_own[0], windows_own[0]).reshape(flat_rows, features)
    weights = lax.all_gather(params.astype(BF16), "dp", axis=0, tiled=True)
    across = (((1,), (1,)), ((), ()))
    product = lax.dot_general(membrane_own, weights, across, preferred_element_type=F32)
    summed = grads_own[0].reshape(flat_rows, features).astype(F32) + product
    outgoing = summed.astype(BF16).reshape(timesteps, tok_rows, features)
    received = passed_along(outgoing, "section", -1)
    membrane_arriving = membrane_grads(received, windows_arriving[0]).reshape(flat_rows, features)
    contract = (((0,), (0,)), ((), ()))
    partial_value = lax.dot_general(
        inputs_own[0].reshape(flat_rows, features),
        membrane_own,
        contract,
        preferred_element_type=F32,
    ) + lax.dot_general(
        inputs_arriving[0].reshape(flat_rows, features),
        membrane_arriving,
        contract,
        preferred_element_type=F32,
    )
    gradient = lax.psum_scatter(
        partial_value.astype(BF16), "dp", scatter_dimension=0, tiled=True
    ).astype(F32)
    fresh_params, fresh_first, fresh_second = adam(
        params, first_moment[0], second_moment[0], gradient
    )
    gathered = lax.all_gather(fresh_params.astype(BF16), "dp", axis=0, tiled=True)
    currents = jnp.dot(next_inputs[0], gathered, preferred_element_type=F32)
    return (
        fresh_params[None],
        fresh_first[None],
        fresh_second[None],
        currents.astype(BF16)[None],
    )


def solution(mesh):
    rows = P("section", "dp", None)
    acts = P("section", None, "dp", None)
    return jax.shard_map(
        relay_shards if mesh.shape["dp"] == PARTS else plain_shards,
        mesh=mesh,
        in_specs=(rows, rows, rows, acts, acts, acts, rows, rows, rows),
        out_specs=(rows, rows, rows, rows),
        check_vma=False,
    )
```

time: 236 us -> 201 us (0.85)
  waiting for transfers between devices: 111 us -> 67.6 us
  Pallas kernels: 63.3 us -> 77.1 us
  starting transfers between devices: 43.3 us -> 39.3 us
    ppermute x41, waiting for transfers between devices: 83.6 us -> 56.5 us  [swapped(): return lax.ppermute(shard, 'dp', [(i, i ^ bit) for i in range(PARTS)])]
    ppermute x4 -> x3, waiting for transfers between devices: 27.3 us -> 11.1 us  [passed_along(): return lax.ppermute(shard, axis, pairs)]
    pallas_call x8 -> x7, Pallas kernels: 45.9 us -> 60.6 us  [the longest x3 27.8 us: partials(): pl.pallas_call(functools.partial(partial_kernel, sources, len(arrived), w...]
    unnamed x31 -> x39, local copies, waits for them, and re-layouts: 6.9 us -> 4.07 us
    ppermute x41, starting transfers between devices: 37.9 us -> 35.2 us  [swapped(): return lax.ppermute(shard, 'dp', [(i, i ^ bit) for i in range(PARTS)])]
    slice x6, local copies, waits for them, and re-layouts: 1.03 us -> 3.4 us  [forward(): first, second = (by_x[:half], by_y[half:])]
    ppermute x4 -> x3, starting transfers between devices: 5.35 us -> 4.02 us  [passed_along(): return lax.ppermute(shard, axis, pairs)]
  transfers between devices with their start and end apart: 45 -> 44, of which waited for: 19 -> 19; matrix products, arithmetic and copies ran while one was open for 3% -> 5% of each run, Pallas kernels for 26% -> 36%
where the time goes in v2:
time: 201 us; the launch traced here: 200 us
  Pallas kernels  77.1 us (38%)
  waiting for transfers between devices  67.6 us (34%)
  starting transfers between devices  39.3 us (20%)
  local copies, waits for them, and re-layouts  13.3 us (7%)
    ppermute x41, waiting for transfers between devices, swapped(): return lax.ppermute(shard, 'dp', [(i, i ^ bit) for i in range(PARTS)])  56.5 us
    ppermute x41, starting transfers between devices, swapped(): return lax.ppermute(shard, 'dp', [(i, i ^ bit) for i in range(PARTS)])  35.2 us
    pallas_call x3, Pallas kernels, partials(): pl.pallas_call(functools.partial(partial_kernel, sources, len(arrived), w...  27.8 us
    pallas_call x3, Pallas kernels, through(): pl.pallas_call(functools.partial(through_kernel, len(weights), pieces), o...  22.1 us
    pallas_call x3, Pallas kernels, update(): pl.pallas_call(functools.partial(update_kernel, whole), out_shape=(shape,...  13.7 us
    ppermute x3, waiting for transfers between devices, passed_along(): return lax.ppermute(shard, axis, pairs)  11.1 us
    pallas_call x1, Pallas kernels, prepare(): pl.pallas_call(functools.partial(prepare_kernel, groups), out_shape=outs,...  10.8 us
    unnamed x39, local copies, waits for them, and re-layouts  4.07 us
  transfers between devices with their start and end apart: 44, of which 19 were waited for; matrix products, arithmetic and copies ran while one was open for 5% of the time, Pallas kernels for 36%

profile of v2, /device:TPU:0, one launch (start us, length us, event | category | flops | bytes accessed | tf_op | source)
XLA Modules:
  0.0 200.2 jit_solution(16360673025401032894)
XLA Ops:
  1.7 1.4 fusion.1.refs_0_
  3.1 2.6 %collective-permute-start.4 = (bf16[128,2560]{1,0:T(8,128)(2,1)S(1)}, bf16[128,2560]{1,0:T(8,128)(2,1)}, u32[]{:S(2)}, u32[]{:S(2)}) collective-permute-start(bf16[128,2560]{1,0:T(8,128)(2,1)S(1)} %fusion.1.refs_0_), channel_id=1, source_target_pairs={{0,2},{1,3},{2,0},{3,1},{4,6},{5,7},{6,4},{7,5},{8,10},{9,11},{10,... | collective-permute-start | bytes 1966088 | tf_op jit(solution)/shard_map/ppermute | solution.py:33
  5.7 1.5 collective-permute-start.5
  7.2 1.4 dynamic-slice_convert_fusion.refs_1_
  9.2 1.6 collective-permute-start.7
  11.4 1.1 dynamic-slice_convert_fusion.2.refs_2_
  12.6 10.8 %prepare.1 = (bf16[2560,1024]{1,0:T(8,128)(2,1)}, bf16[1280,1024]{1,0:T(8,128)(2,1)}, s32[1280,256]{1,0:T(8,128)}) custom-call(s32[2]{0:T(128)} %pad_add_fusion.where, bf16[4,128,2560]{2,1,0:T(8,128)(2,1)} %bitcast.132, bf16[4,128,2560]{2,1,0:T(8,128)(2,1)} %collective-permute-done.refs_1_, s32[128,2560]{1,0:T(8,128)} %bitcast.136, ...), custom_call_target="tpu_custom_call" | custom-call | flops 1 | bytes 1 | tf_op jit(solution)/shard_map/prepare/pallas_call | solution.py:107
  23.4 8.0 %through.3 = bf16[512,1024]{1,0:T(8,128)(2,1)} custom-call(s32[2]{0:T(128)} %pad_add_fusion.where, bf16[128,2560]{1,0:T(8,128)(2,1)} %copy-done.6, bf16[128,2560]{1,0:T(8,128)(2,1)} %copy-done.7, bf16[128,2560]{1,0:T(8,128)(2,1)} %collective-permute-done.4.refs_2_, bf16[128,2560]{1,0:T(8,128)(2,1)} %collective-permute-done.5.refs_3_, ...), custom_call_target="tpu_custom_call" | custom-call | flops 1 | bytes 1 | tf_op jit(solution)/shard_map/through/pallas_call | solution.py:173
  31.4 3.7 %collective-permute-done.3.refs_2_ = bf16[128,2560]{1,0:T(8,128)(2,1)S(1)} collective-permute-done((bf16[128,2560]{1,0:T(8,128)(2,1)S(1)}, bf16[128,2560]{1,0:T(8,128)(2,1)S(1)}, u32[]{:S(2)}, u32[]{:S(2)}) %collective-permute-start.3) | collective-permute-done | bytes 655392 | tf_op jit(solution)/shard_map/ppermute | solution.py:33
  35.1 1.5 collective-permute-done.7.refs_3_
  36.5 1.5 collective-permute-start.11
  38.6 6.9 %collective-permute-done.11.refs_4_ = bf16[64,2560]{1,0:T(8,128)(2,1)S(1)} collective-permute-done((bf16[64,2560]{1,0:T(8,128)(2,1)S(1)}, bf16[64,2560]{1,0:T(8,128)(2,1)S(1)}, u32[]{:S(2)}, u32[]{:S(2)}) %collective-permute-start.11) | collective-permute-done | bytes 327712 | tf_op jit(solution)/shard_map/ppermute | solution.py:33
  45.5 1.2 collective-permute-done.9.refs_3_
  47.2 1.3 collective-permute-start.10
  48.5 1.0 slice.171
  49.5 1.0 slice.172
  51.8 8.4 %collective-permute-done.12.refs_0_ = bf16[64,2560]{1,0:T(8,128)(2,1)S(1)} collective-permute-done((bf16[64,2560]{1,0:T(8,128)(2,1)S(1)}, bf16[64,2560]{1,0:T(8,128)(2,1)S(1)}, u32[]{:S(2)}, u32[]{:S(2)}) %collective-permute-start.12) | collective-permute-done | bytes 327712 | tf_op jit(solution)/shard_map/ppermute | solution.py:33
  61.7 1.0 collective-permute-start.6
  62.7 7.0 %through.4 = bf16[384,1024]{1,0:T(8,128)(2,1)} custom-call(s32[2]{0:T(128)} %pad_add_fusion.where, bf16[64,2560]{1,0:T(8,128)(2,1)} %copy-done.13, bf16[64,2560]{1,0:T(8,128)(2,1)} %copy-done.14, bf16[128,2560]{1,0:T(8,128)(2,1)} %copy-done.8, bf16[128,2560]{1,0:T(8,128)(2,1)} %copy-done.9, ...), custom_call_target="tpu_custom_call" | custom-call | flops 1 | bytes 1 | tf_op jit(solution)/shard_map/through/pallas_call | solution.py:173
  71.9 1.5 collective-permute-start.14
  74.4 1.3 collective-permute-start.17
  78.1 7.0 %through.5 = bf16[384,1024]{1,0:T(8,128)(2,1)} custom-call(s32[2]{0:T(128)} %pad_add_fusion.where, bf16[64,2560]{1,0:T(8,128)(2,1)} %collective-permute-done.6.refs_0_, bf16[64,2560]{1,0:T(8,128)(2,1)} %collective-permute-done.8.refs_1_, bf16[64,2560]{1,0:T(8,128)(2,1)} %copy-done.10, bf16[64,2560]{1,0:T(8,128)(2,1)} %copy-done.12, ...), custom_call_target="tpu_custom_call" | custom-call | flops 1 | bytes 1 | tf_op jit(solution)/shard_map/through/pallas_call | solution.py:173
  85.1 1.5 collective-permute-start.16
  87.0 10.1 %collective-permute-done.17.refs_9_ = bf16[384,1024]{1,0:T(8,128)(2,1)} collective-permute-done((bf16[384,1024]{1,0:T(8,128)(2,1)}, bf16[384,1024]{1,0:T(8,128)(2,1)}, u32[]{:S(2)}, u32[]{:S(2)}) %collective-permute-start.17) | collective-permute-done | bytes 786464 | tf_op jit(solution)/shard_map/ppermute | solution.py:29
  97.1 2.5 %copy-done = bf16[2560,1024]{1,0:T(8,128)(2,1)S(1)} copy-done((bf16[2560,1024]{1,0:T(8,128)(2,1)S(1)}, bf16[2560,1024]{1,0:T(8,128)(2,1)}, u32[]{:S(2)}) %copy-start) | copy-done | bytes 5242904
  99.6 10.1 %partials.3 = (bf16[2,640,256]{2,1,0:T(8,128)(2,1)S(1)}, bf16[2,640,256]{2,1,0:T(8,128)(2,1)S(1)}, bf16[2,640,256]{2,1,0:T(8,128)(2,1)S(1)}, bf16[2,640,256]{2,1,0:T(8,128)(2,1)S(1)}) custom-call(s32[2]{0:T(128)S(1)} %copy-done.5, bf16[2560,1024]{1,0:T(8,128)(2,1)S(1)} %copy-done, bf16[2560,1024]{1,0:T(8,128)(2,1)S(1)} %copy-done, ...), custom_call_target="tpu_custom_call" | custom-call | flops 1 | bytes 1 | tf_op jit(solution)/shard_map/partials/pallas_call | solution.py:278
  111.9 10.1 %partials.4 = (bf16[2,640,256]{2,1,0:T(8,128)(2,1)S(1)}, bf16[2,640,256]{2,1,0:T(8,128)(2,1)S(1)}, bf16[2,640,256]{2,1,0:T(8,128)(2,1)S(1)}, bf16[2,640,256]{2,1,0:T(8,128)(2,1)S(1)}) custom-call(s32[2]{0:T(128)S(1)} %copy-done.5, bf16[2560,1024]{1,0:T(8,128)(2,1)S(1)} %copy-done, bf16[2560,1024]{1,0:T(8,128)(2,1)S(1)} %copy-done, ...), custom_call_target="tpu_custom_call" | custom-call | flops 1 | bytes 1 | tf_op jit(solution)/shard_map/partials/pallas_call | solution.py:278
  122.9 1.4 collective-permute-start.30
  125.1 1.3 collective-permute-start.32
  126.4 1.8 collective-permute-done.21.yr
  128.3 1.4 collective-permute-start.33
  129.6 12.6 %collective-permute-done.26.yr = bf16[2,640,256]{2,1,0:T(8,128)(2,1)S(1)} collective-permute-done((bf16[2,640,256]{2,1,0:T(8,128)(2,1)S(1)}, bf16[2,640,256]{2,1,0:T(8,128)(2,1)S(1)}, u32[]{:S(2)}, u32[]{:S(2)}) %collective-permute-start.26) | collective-permute-done | bytes 655392 | tf_op jit(solution)/shard_map/ppermute | solution.py:33
  142.3 1.4 collective-permute-start.27
  144.3 7.6 %partials.5 = (bf16[2,640,128]{2,1,0:T(8,128)(2,1)S(1)}, bf16[2,640,128]{2,1,0:T(8,128)(2,1)S(1)}, bf16[2,640,128]{2,1,0:T(8,128)(2,1)S(1)}, bf16[2,640,128]{2,1,0:T(8,128)(2,1)S(1)}) custom-call(s32[2]{0:T(128)S(1)} %copy-done.5, bf16[2560,1024]{1,0:T(8,128)(2,1)S(1)} %copy-done, bf16[2560,1024]{1,0:T(8,128)(2,1)S(1)} %copy-done, ...), custom_call_target="tpu_custom_call" | custom-call | flops 1 | bytes 1 | tf_op jit(solution)/shard_map/partials/pallas_call | solution.py:278
  151.9 1.2 collective-permute-start.22
  153.2 1.2 collective-permute-start.35
  154.4 1.0 collective-permute-start.31
  158.3 4.4 %collective-permute-done.22.xr = bf16[2,640,128]{2,1,0:T(8,128)(2,1)S(1)} collective-permute-done((bf16[2,640,128]{2,1,0:T(8,128)(2,1)S(1)}, bf16[2,640,128]{2,1,0:T(8,128)(2,1)S(1)}, u32[]{:S(2)}, u32[]{:S(2)}) %collective-permute-start.22) | collective-permute-done | bytes 327712 | tf_op jit(solution)/shard_map/ppermute | solution.py:33
  162.7 1.3 collective-permute-start.23
  164.1 1.4 collective-permute-start.36
  165.6 5.3 %update.3 = (f32[320,2560]{1,0:T(8,128)}, f32[320,2560]{1,0:T(8,128)}, f32[320,2560]{1,0:T(8,128)}, bf16[256,1024]{1,0:T(8,128)(2,1)S(1)}) custom-call(s32[2]{0:T(128)S(1)} %copy-done.5, bf16[320,512]{1,0:T(8,128)(2,1)S(1)} %get-tuple-element.93.mine, bf16[320,512]{1,0:T(8,128)(2,1)S(1)} %collective-permute-done.34.theirs, f32[320,2560]{1,0:T(8,128)S(1)} %bitcast.112, ...), custom_call_target="tpu_custom_call" | custom-call | flops 167772160 | bytes 7864320 | tf_op jit(solution)/shard_map/update/pallas_call | solution.py:382
  170.8 5.3 %update.4 = (f32[320,2560]{1,0:T(8,128)}, f32[320,2560]{1,0:T(8,128)}, f32[320,2560]{1,0:T(8,128)}, bf16[256,1024]{1,0:T(8,128)(2,1)S(1)}) custom-call(s32[2]{0:T(128)S(1)} %copy-done.5, bf16[320,512]{1,0:T(8,128)(2,1)S(1)} %get-tuple-element.89.mine, ...), custom_call_target="tpu_custom_call", output_to_operand_aliasing={{0}: (7, {}), {1}: (8, {}), {2}: (9, {})} | custom-call | flops 167772160 | bytes 7864320 | tf_op jit(solution)/shard_map/update/pallas_call | solution.py:382
  177.2 1.5 collective-permute-done.37.theirs
  178.7 3.2 %update.5 = (f32[320,2560]{1,0:T(8,128)}, f32[320,2560]{1,0:T(8,128)}, f32[320,2560]{1,0:T(8,128)}, bf16[256,512]{1,0:T(8,128)(2,1)S(1)}) custom-call(s32[2]{0:T(128)S(1)} %copy-done.5, bf16[320,512]{1,0:T(8,128)(2,1)S(1)} %get-tuple-element.102.mine, ...), custom_call_target="tpu_custom_call", output_to_operand_aliasing={{0}: (7, {}), {1}: (8, {}), {2}: (9, {})} | custom-call | flops 83886080 | bytes 3932160 | tf_op jit(solution)/shard_map/update/pallas_call | solution.py:382
  183.4 1.3 collective-permute-start.42
  185.7 2.4 %collective-permute-done.42 = bf16[2,32,512]{2,1,0:T(8,128)(2,1)S(1)} collective-permute-done((bf16[2,32,512]{2,1,0:T(8,128)(2,1)S(1)}, bf16[2,32,512]{2,1,0:T(8,128)(2,1)S(1)}, u32[]{:S(2)}, u32[]{:S(2)}) %collective-permute-start.42) | collective-permute-done | bytes 65568 | tf_op jit(solution)/shard_map/ppermute | solution.py:33
  188.9 4.4 %collective-permute-done.39 = bf16[2,32,2048]{2,1,0:T(8,128)(2,1)S(1)} collective-permute-done((bf16[2,32,2048]{2,1,0:T(8,128)(2,1)S(1)}, bf16[2,32,2048]{2,1,0:T(8,128)(2,1)S(1)}, u32[]{:S(2)}, u32[]{:S(2)}) %collective-permute-start.39) | collective-permute-done | bytes 262176 | tf_op jit(solution)/shard_map/ppermute | solution.py:33
  194.3 4.2 %collective-permute-done.40 = bf16[32,2048]{1,0:T(8,128)(2,1)S(1)} collective-permute-done((bf16[32,2048]{1,0:T(8,128)(2,1)S(1)}, bf16[32,2048]{1,0:T(8,128)(2,1)S(1)}, u32[]{:S(2)}, u32[]{:S(2)}) %collective-permute-start.40) | collective-permute-done | bytes 131104 | tf_op jit(solution)/shard_map/ppermute | solution.py:33
  (136 shorter events, 26.9 us)
Async XLA Ops:
  0.6 8.0 %collective-permute-start = (bf16[4,128,2560]{2,1,0:T(8,128)(2,1)}, bf16[4,128,2560]{2,1,0:T(8,128)(2,1)}, u32[]{:S(2)}, u32[]{:S(2)}) collective-permute-start(bf16[4,128,2560]{2,1,0:T(8,128)(2,1)} %bitcast.131), channel_id=1, source_target_pairs={{0,1},{1,0},{2,3},{3,2},{4,5},{5,4},{6,7},{7,6},{8,9},{9,8},{10,11... | collective-permute-start | bytes 7864328 | tf_op jit(solution)/shard_map/ppermute | solution.py:33
  1.1 8.1 %collective-permute-start.1 = (s32[128,2560]{1,0:T(8,128)}, s32[128,2560]{1,0:T(8,128)}, u32[]{:S(2)}, u32[]{:S(2)}) collective-permute-start(s32[128,2560]{1,0:T(8,128)} %bitcast.135), channel_id=1, source_target_pairs={{0,1},{1,0},{2,3},{3,2},{4,5},{5,4},{6,7},{7,6},{8,9},{9,8},{10,11... | collective-permute-start | bytes 3932168 | tf_op jit(solution)/shard_map/ppermute | solution.py:33
  1.2 11.4 %collective-permute-start.2 = (s32[128,2560]{1,0:T(8,128)}, s32[128,2560]{1,0:T(8,128)}, u32[]{:S(2)}, u32[]{:S(2)}) collective-permute-start(s32[128,2560]{1,0:T(8,128)} %bitcast.137), channel_id=1, source_target_pairs={{0,1},{1,0},{2,3},{3,2},{4,5},{5,4},{6,7},{7,6},{8,9},{9,8},{10,11... | collective-permute-start | bytes 3932168 | tf_op jit(solution)/shard_map/ppermute | solution.py:33
  3.1 20.3 %collective-permute-start.4 = (bf16[128,2560]{1,0:T(8,128)(2,1)S(1)}, bf16[128,2560]{1,0:T(8,128)(2,1)}, u32[]{:S(2)}, u32[]{:S(2)}) collective-permute-start(bf16[128,2560]{1,0:T(8,128)(2,1)S(1)} %fusion.1.refs_0_), channel_id=1, source_target_pairs={{0,2},{1,3},{2,0},{3,1},{4,6},{5,7},{6,4},{7,5},{8,10},{9,11},{10,... | collective-permute-start | bytes 1966088 | tf_op jit(solution)/shard_map/ppermute | solution.py:33
  5.7 17.7 %collective-permute-start.5 = (bf16[128,2560]{1,0:T(8,128)(2,1)S(1)}, bf16[128,2560]{1,0:T(8,128)(2,1)}, u32[]{:S(2)}, u32[]{:S(2)}) collective-permute-start(bf16[128,2560]{1,0:T(8,128)(2,1)S(1)} %fusion.1.refs_0_), channel_id=1, source_target_pairs={{0,4},{1,5},{2,6},{3,7},{4,0},{5,1},{6,2},{7,3},{8,12},{9,13},{10,... | collective-permute-start | bytes 1966088 | tf_op jit(solution)/shard_map/ppermute | solution.py:33
  8.6 26.4 %collective-permute-start.3 = (bf16[128,2560]{1,0:T(8,128)(2,1)S(1)}, bf16[128,2560]{1,0:T(8,128)(2,1)S(1)}, u32[]{:S(2)}, u32[]{:S(2)}) collective-permute-start(bf16[128,2560]{1,0:T(8,128)(2,1)S(1)} %dynamic-slice_convert_fusion.refs_1_), channel_id=1, source_target_pairs={{0,2},{1,3},{2,0},{3,1},{4,6},{5,7},{6,4},{7,5},{8,10},{9,11},{10,... | collective-permute-start | bytes 1966088 | tf_op jit(solution)/shard_map/ppermute | solution.py:33
  9.2 27.3 %collective-permute-start.7 = (bf16[128,2560]{1,0:T(8,128)(2,1)S(1)}, bf16[128,2560]{1,0:T(8,128)(2,1)S(1)}, u32[]{:S(2)}, u32[]{:S(2)}) collective-permute-start(bf16[128,2560]{1,0:T(8,128)(2,1)S(1)} %dynamic-slice_convert_fusion.refs_1_), channel_id=1, source_target_pairs={{0,4},{1,5},{2,6},{3,7},{4,0},{5,1},{6,2},{7,3},{8,12},{9,13},{10,... | collective-permute-start | bytes 1966088 | tf_op jit(solution)/shard_map/ppermute | solution.py:33
  12.6 25.5 %copy-start.10 = (bf16[64,2560]{1,0:T(8,128)(2,1)}, bf16[64,2560]{1,0:T(8,128)(2,1)S(1)}, u32[]{:S(2)}) copy-start(bf16[64,2560]{1,0:T(8,128)(2,1)S(1)} %dynamic-slice_convert_fusion.2.refs_2_) | copy-start | bytes 983044
  35.1 27.6 %copy-start.8 = (bf16[128,2560]{1,0:T(8,128)(2,1)}, bf16[128,2560]{1,0:T(8,128)(2,1)S(1)}, u32[]{:S(2)}) copy-start(bf16[128,2560]{1,0:T(8,128)(2,1)S(1)} %collective-permute-done.3.refs_2_) | copy-start | bytes 1966084
  36.5 26.2 %copy-start.9 = (bf16[128,2560]{1,0:T(8,128)(2,1)}, bf16[128,2560]{1,0:T(8,128)(2,1)S(1)}, u32[]{:S(2)}) copy-start(bf16[128,2560]{1,0:T(8,128)(2,1)S(1)} %collective-permute-done.7.refs_3_) | copy-start | bytes 1966084
  36.5 8.9 %collective-permute-start.11 = (bf16[64,2560]{1,0:T(8,128)(2,1)S(1)}, bf16[64,2560]{1,0:T(8,128)(2,1)S(1)}, u32[]{:S(2)}, u32[]{:S(2)}) collective-permute-start(bf16[64,2560]{1,0:T(8,128)(2,1)S(1)} %dynamic-slice_convert_fusion.2.refs_2_), channel_id=1, source_target_pairs={{0,4},{1,5},{2,6},{3,7},{4,0},{5,1},{6,2},{7,3},{8,12},{9,13},{10,... | collective-permute-start | bytes 983048 | tf_op jit(solution)/shard_map/ppermute | solution.py:33
  38.1 8.7 %collective-permute-start.9 = (bf16[64,2560]{1,0:T(8,128)(2,1)S(1)}, bf16[64,2560]{1,0:T(8,128)(2,1)S(1)}, u32[]{:S(2)}, u32[]{:S(2)}) collective-permute-start(bf16[64,2560]{1,0:T(8,128)(2,1)S(1)} %dynamic-slice_convert_fusion.2.refs_2_), channel_id=1, source_target_pairs={{0,2},{1,3},{2,0},{3,1},{4,6},{5,7},{6,4},{7,5},{8,10},{9,11},{10,... | collective-permute-start | bytes 983048 | tf_op jit(solution)/shard_map/ppermute | solution.py:33
  45.5 24.3 %copy-start.11 = (bf16[64,2560]{1,0:T(8,128)(2,1)}, bf16[64,2560]{1,0:T(8,128)(2,1)S(1)}, u32[]{:S(2)}) copy-start(bf16[64,2560]{1,0:T(8,128)(2,1)S(1)} %collective-permute-done.11.refs_4_) | copy-start | bytes 983044
  46.7 50.4 %collective-permute-start.19 = (bf16[512,2560]{1,0:T(8,128)(2,1)}, bf16[512,2560]{1,0:T(8,128)(2,1)}, u32[]{:S(2)}, u32[]{:S(2)}) collective-permute-start(bf16[512,2560]{1,0:T(8,128)(2,1)} %bitcast.8.refs_12_.refs_13_.refs_11_), channel_id=1, source_target_pairs={{0,1},{1,0},{2,3},{3,2},{4,5},{5,4},{6,7},{7,6},{8,9},{9,8},{10,11... | collective-permute-start | bytes 7864328 | tf_op jit(solution)/shard_map/ppermute | solution.py:33
  46.7 50.4 %collective-permute-start.18 = (bf16[512,2560]{1,0:T(8,128)(2,1)}, bf16[512,2560]{1,0:T(8,128)(2,1)}, u32[]{:S(2)}, u32[]{:S(2)}) collective-permute-start(bf16[512,2560]{1,0:T(8,128)(2,1)} %bitcast.7.refs_10_.refs_11_.refs_9_), channel_id=1, source_target_pairs={{0,1},{1,0},{2,3},{3,2},{4,5},{5,4},{6,7},{7,6},{8,9},{9,8},{10,11... | collective-permute-start | bytes 7864328 | tf_op jit(solution)/shard_map/ppermute | solution.py:33
  47.2 27.2 %collective-permute-start.10 = (bf16[512,1024]{1,0:T(8,128)(2,1)}, bf16[512,1024]{1,0:T(8,128)(2,1)S(1)}, u32[]{:S(2)}, u32[]{:S(2)}) collective-permute-start(bf16[512,1024]{1,0:T(8,128)(2,1)} %through.3), channel_id=1, source_target_pairs={{8,0},{16,8},{24,16},{9,1},{17,9},{25,17},{10,2},{18,10},{26,18},{... | collective-permute-start | bytes 3145736 | tf_op jit(solution)/shard_map/ppermute | solution.py:29
  50.5 9.7 %collective-permute-start.12 = (bf16[64,2560]{1,0:T(8,128)(2,1)S(1)}, bf16[64,2560]{1,0:T(8,128)(2,1)S(1)}, u32[]{:S(2)}, u32[]{:S(2)}) collective-permute-start(bf16[64,2560]{1,0:T(8,128)(2,1)S(1)} %slice.171), channel_id=1, source_target_pairs={{0,4},{1,5},{2,6},{3,7},{4,0},{5,1},{6,2},{7,3},{8,12},{9,13},{10,... | collective-permute-start | bytes 983048 | tf_op jit(solution)/shard_map/ppermute | solution.py:33
  51.1 9.8 %collective-permute-start.13 = (bf16[64,2560]{1,0:T(8,128)(2,1)S(1)}, bf16[64,2560]{1,0:T(8,128)(2,1)S(1)}, u32[]{:S(2)}, u32[]{:S(2)}) collective-permute-start(bf16[64,2560]{1,0:T(8,128)(2,1)S(1)} %slice.172), channel_id=1, source_target_pairs={{0,2},{1,3},{2,0},{3,1},{4,6},{5,7},{6,4},{7,5},{8,10},{9,11},{10,... | collective-permute-start | bytes 983048 | tf_op jit(solution)/shard_map/ppermute | solution.py:33
  60.2 10.9 %collective-permute-start.8 = (bf16[64,2560]{1,0:T(8,128)(2,1)S(1)}, bf16[64,2560]{1,0:T(8,128)(2,1)}, u32[]{:S(2)}, u32[]{:S(2)}) collective-permute-start(bf16[64,2560]{1,0:T(8,128)(2,1)S(1)} %slice.169), channel_id=1, source_target_pairs={{0,2},{1,3},{2,0},{3,1},{4,6},{5,7},{6,4},{7,5},{8,10},{9,11},{10,... | collective-permute-start | bytes 983048 | tf_op jit(solution)/shard_map/ppermute | solution.py:33
  61.7 10.2 %collective-permute-start.6 = (bf16[64,2560]{1,0:T(8,128)(2,1)S(1)}, bf16[64,2560]{1,0:T(8,128)(2,1)}, u32[]{:S(2)}, u32[]{:S(2)}) collective-permute-start(bf16[64,2560]{1,0:T(8,128)(2,1)S(1)} %slice.168), channel_id=1, source_target_pairs={{0,4},{1,5},{2,6},{3,7},{4,0},{5,1},{6,2},{7,3},{8,12},{9,13},{10,... | collective-permute-start | bytes 983048 | tf_op jit(solution)/shard_map/ppermute | solution.py:33
  71.1 5.5 %collective-permute-start.15 = (bf16[32,2560]{1,0:T(8,128)(2,1)}, bf16[32,2560]{1,0:T(8,128)(2,1)S(1)}, u32[]{:S(2)}, u32[]{:S(2)}) collective-permute-start(bf16[32,2560]{1,0:T(8,128)(2,1)} %slice.173), channel_id=1, source_target_pairs={{0,2},{1,3},{2,0},{3,1},{4,6},{5,7},{6,4},{7,5},{8,10},{9,11},{10,... | collective-permute-start | bytes 491528 | tf_op jit(solution)/shard_map/ppermute | solution.py:33
  71.9 5.5 %collective-permute-start.14 = (bf16[32,2560]{1,0:T(8,128)(2,1)}, bf16[32,2560]{1,0:T(8,128)(2,1)S(1)}, u32[]{:S(2)}, u32[]{:S(2)}) collective-permute-start(bf16[32,2560]{1,0:T(8,128)(2,1)} %slice.170), channel_id=1, source_target_pairs={{0,4},{1,5},{2,6},{3,7},{4,0},{5,1},{6,2},{7,3},{8,12},{9,13},{10,... | collective-permute-start | bytes 491528 | tf_op jit(solution)/shard_map/ppermute | solution.py:33
  74.4 22.7 %collective-permute-start.17 = (bf16[384,1024]{1,0:T(8,128)(2,1)}, bf16[384,1024]{1,0:T(8,128)(2,1)}, u32[]{:S(2)}, u32[]{:S(2)}) collective-permute-start(bf16[384,1024]{1,0:T(8,128)(2,1)} %through.4), channel_id=1, source_target_pairs={{8,0},{16,8},{24,16},{9,1},{17,9},{25,17},{10,2},{18,10},{26,18},{... | collective-permute-start | bytes 2359304 | tf_op jit(solution)/shard_map/ppermute | solution.py:29
  85.1 26.8 %collective-permute-start.16 = (bf16[384,1024]{1,0:T(8,128)(2,1)}, bf16[384,1024]{1,0:T(8,128)(2,1)S(1)}, u32[]{:S(2)}, u32[]{:S(2)}) collective-permute-start(bf16[384,1024]{1,0:T(8,128)(2,1)} %through.5), channel_id=1, source_target_pairs={{8,0},{16,8},{24,16},{9,1},{17,9},{25,17},{10,2},{18,10},{26,18},{... | collective-permute-start | bytes 2359304 | tf_op jit(solution)/shard_map/ppermute | solution.py:29
  109.7 15.3 %collective-permute-start.20 = (bf16[2,640,256]{2,1,0:T(8,128)(2,1)S(1)}, bf16[2,640,256]{2,1,0:T(8,128)(2,1)S(1)}, u32[]{:S(2)}, u32[]{:S(2)}) collective-permute-start(bf16[2,640,256]{2,1,0:T(8,128)(2,1)S(1)} %get-tuple-element.80), channel_id=1, source_target_pairs={{0,2},{1,3},{2,0},{3,1},{4,6},{5,7},{6,4},{7,5},{8,10},{9,11},{10,... | collective-permute-start | bytes 1966088 | tf_op jit(solution)/shard_map/ppermute | solution.py:33
  110.5 1.4 collective-permute-start.29
  110.6 17.6 %collective-permute-start.21 = (bf16[2,640,256]{2,1,0:T(8,128)(2,1)S(1)}, bf16[2,640,256]{2,1,0:T(8,128)(2,1)S(1)}, u32[]{:S(2)}, u32[]{:S(2)}) collective-permute-start(bf16[2,640,256]{2,1,0:T(8,128)(2,1)S(1)} %get-tuple-element.82), channel_id=1, source_target_pairs={{0,4},{1,5},{2,6},{3,7},{4,0},{5,1},{6,2},{7,3},{8,12},{9,13},{10,... | collective-permute-start | bytes 1966088 | tf_op jit(solution)/shard_map/ppermute | solution.py:33
  122.0 20.2 %collective-permute-start.26 = (bf16[2,640,256]{2,1,0:T(8,128)(2,1)S(1)}, bf16[2,640,256]{2,1,0:T(8,128)(2,1)S(1)}, u32[]{:S(2)}, u32[]{:S(2)}) collective-permute-start(bf16[2,640,256]{2,1,0:T(8,128)(2,1)S(1)} %get-tuple-element.88), channel_id=1, source_target_pairs={{0,4},{1,5},{2,6},{3,7},{4,0},{5,1},{6,2},{7,3},{8,12},{9,13},{10,... | collective-permute-start | bytes 1966088 | tf_op jit(solution)/shard_map/ppermute | solution.py:33
  122.9 29.0 %collective-permute-start.30 = (bf16[2,2,32,320]{3,2,1,0:T(8,128)(2,1)S(1)}, bf16[2,2,32,320]{3,2,1,0:T(8,128)(2,1)S(1)}, u32[]{:S(2)}, u32[]{:S(2)}) collective-permute-start(bf16[2,2,32,320]{3,2,1,0:T(8,128)(2,1)S(1)} %get-tuple-element.115), channel_id=1, source_target_pairs={{0,2},{1,3},{2,0},{3,1},{4,6},{5,7},{6,4},{7,5},{8,10},{9,11},{10,... | collective-permute-start | bytes 245768 | tf_op jit(solution)/shard_map/ppermute | solution.py:33
  124.3 19.4 %collective-permute-start.24 = (bf16[2,640,256]{2,1,0:T(8,128)(2,1)S(1)}, bf16[2,640,256]{2,1,0:T(8,128)(2,1)S(1)}, u32[]{:S(2)}, u32[]{:S(2)}) collective-permute-start(bf16[2,640,256]{2,1,0:T(8,128)(2,1)S(1)} %get-tuple-element.86), channel_id=1, source_target_pairs={{0,2},{1,3},{2,0},{3,1},{4,6},{5,7},{6,4},{7,5},{8,10},{9,11},{10,... | collective-permute-start | bytes 1966088 | tf_op jit(solution)/shard_map/ppermute | solution.py:33
  125.1 28.1 %collective-permute-start.32 = (bf16[640,256]{1,0:T(8,128)(2,1)S(1)}, bf16[640,256]{1,0:T(8,128)(2,1)S(1)}, u32[]{:S(2)}, u32[]{:S(2)}) collective-permute-start(bf16[640,256]{1,0:T(8,128)(2,1)S(1)} %fusion.3), channel_id=1, source_target_pairs={{0,4},{1,5},{2,6},{3,7},{4,0},{5,1},{6,2},{7,3},{8,12},{9,13},{10,... | collective-permute-start | bytes 983048 | tf_op jit(solution)/shard_map/ppermute | solution.py:33
  128.3 26.1 %collective-permute-start.33 = (bf16[640,256]{1,0:T(8,128)(2,1)S(1)}, bf16[640,256]{1,0:T(8,128)(2,1)S(1)}, u32[]{:S(2)}, u32[]{:S(2)}) collective-permute-start(bf16[640,256]{1,0:T(8,128)(2,1)S(1)} %fusion.4), channel_id=1, source_target_pairs={{0,2},{1,3},{2,0},{3,1},{4,6},{5,7},{6,4},{7,5},{8,10},{9,11},{10,... | collective-permute-start | bytes 983048 | tf_op jit(solution)/shard_map/ppermute | solution.py:33
  142.3 14.5 %collective-permute-start.27 = (bf16[640,256]{1,0:T(8,128)(2,1)S(1)}, bf16[640,256]{1,0:T(8,128)(2,1)S(1)}, u32[]{:S(2)}, u32[]{:S(2)}) collective-permute-start(bf16[640,256]{1,0:T(8,128)(2,1)S(1)} %fusion.6), channel_id=1, source_target_pairs={{0,2},{1,3},{2,0},{3,1},{4,6},{5,7},{6,4},{7,5},{8,10},{9,11},{10,... | collective-permute-start | bytes 983048 | tf_op jit(solution)/shard_map/ppermute | solution.py:33
  143.8 13.0 %collective-permute-start.25 = (bf16[640,256]{1,0:T(8,128)(2,1)S(1)}, bf16[640,256]{1,0:T(8,128)(2,1)S(1)}, u32[]{:S(2)}, u32[]{:S(2)}) collective-permute-start(bf16[640,256]{1,0:T(8,128)(2,1)S(1)} %fusion.5), channel_id=1, source_target_pairs={{0,4},{1,5},{2,6},{3,7},{4,0},{5,1},{6,2},{7,3},{8,12},{9,13},{10,... | collective-permute-start | bytes 983048 | tf_op jit(solution)/shard_map/ppermute | solution.py:33
  151.9 10.8 %collective-permute-start.22 = (bf16[2,640,128]{2,1,0:T(8,128)(2,1)S(1)}, bf16[2,640,128]{2,1,0:T(8,128)(2,1)S(1)}, u32[]{:S(2)}, u32[]{:S(2)}) collective-permute-start(bf16[2,640,128]{2,1,0:T(8,128)(2,1)S(1)} %get-tuple-element.85), channel_id=1, source_target_pairs={{0,2},{1,3},{2,0},{3,1},{4,6},{5,7},{6,4},{7,5},{8,10},{9,11},{10,... | collective-permute-start | bytes 983048 | tf_op jit(solution)/shard_map/ppermute | solution.py:33
  153.2 10.9 %collective-permute-start.35 = (bf16[2,640,128]{2,1,0:T(8,128)(2,1)S(1)}, bf16[2,640,128]{2,1,0:T(8,128)(2,1)S(1)}, u32[]{:S(2)}, u32[]{:S(2)}) collective-permute-start(bf16[2,640,128]{2,1,0:T(8,128)(2,1)S(1)} %get-tuple-element.101), channel_id=1, source_target_pairs={{0,4},{1,5},{2,6},{3,7},{4,0},{5,1},{6,2},{7,3},{8,12},{9,13},{10,... | collective-permute-start | bytes 983048 | tf_op jit(solution)/shard_map/ppermute | solution.py:33
  154.4 11.1 %collective-permute-start.31 = (bf16[2,2,32,320]{3,2,1,0:T(8,128)(2,1)S(1)}, bf16[2,2,32,320]{3,2,1,0:T(8,128)(2,1)S(1)}, u32[]{:S(2)}, u32[]{:S(2)}) collective-permute-start(bf16[2,2,32,320]{3,2,1,0:T(8,128)(2,1)S(1)} %get-tuple-element.113), channel_id=1, source_target_pairs={{0,4},{1,5},{2,6},{3,7},{4,0},{5,1},{6,2},{7,3},{8,12},{9,13},{10,... | collective-permute-start | bytes 245768 | tf_op jit(solution)/shard_map/ppermute | solution.py:33
  156.8 8.8 %collective-permute-start.34 = (bf16[320,512]{1,0:T(8,128)(2,1)S(1)}, bf16[320,512]{1,0:T(8,128)(2,1)S(1)}, u32[]{:S(2)}, u32[]{:S(2)}) collective-permute-start(bf16[320,512]{1,0:T(8,128)(2,1)S(1)} %get-tuple-element.94), channel_id=1, source_target_pairs={{0,1},{1,0},{2,3},{3,2},{4,5},{5,4},{6,7},{7,6},{8,9},{9,8},{10,11... | collective-permute-start | bytes 983048 | tf_op jit(solution)/shard_map/ppermute | solution.py:33
  157.7 13.1 %collective-permute-start.28 = (bf16[320,512]{1,0:T(8,128)(2,1)S(1)}, bf16[320,512]{1,0:T(8,128)(2,1)S(1)}, u32[]{:S(2)}, u32[]{:S(2)}) collective-permute-start(bf16[320,512]{1,0:T(8,128)(2,1)S(1)} %get-tuple-element.90), channel_id=1, source_target_pairs={{0,1},{1,0},{2,3},{3,2},{4,5},{5,4},{6,7},{7,6},{8,9},{9,8},{10,11... | collective-permute-start | bytes 983048 | tf_op jit(solution)/shard_map/ppermute | solution.py:33
  162.7 13.4 %collective-permute-start.23 = (bf16[640,128]{1,0:T(8,128)(2,1)S(1)}, bf16[640,128]{1,0:T(8,128)(2,1)S(1)}, u32[]{:S(2)}, u32[]{:S(2)}) collective-permute-start(bf16[640,128]{1,0:T(8,128)(2,1)S(1)} %fusion.10), channel_id=1, source_target_pairs={{0,4},{1,5},{2,6},{3,7},{4,0},{5,1},{6,2},{7,3},{8,12},{9,13},{10,... | collective-permute-start | bytes 491528 | tf_op jit(solution)/shard_map/ppermute | solution.py:33
  164.1 12.0 %collective-permute-start.36 = (bf16[640,128]{1,0:T(8,128)(2,1)S(1)}, bf16[640,128]{1,0:T(8,128)(2,1)S(1)}, u32[]{:S(2)}, u32[]{:S(2)}) collective-permute-start(bf16[640,128]{1,0:T(8,128)(2,1)S(1)} %fusion.11), channel_id=1, source_target_pairs={{0,2},{1,3},{2,0},{3,1},{4,6},{5,7},{6,4},{7,5},{8,10},{9,11},{10,... | collective-permute-start | bytes 491528 | tf_op jit(solution)/shard_map/ppermute | solution.py:33
  177.0 1.7 collective-permute-start.37
  181.9 1.4 collective-permute-start.41
  182.1 2.5 %collective-permute-start.38 = (bf16[4,32,2048]{2,1,0:T(8,128)(2,1)S(1)}, bf16[4,32,2048]{2,1,0:T(8,128)(2,1)S(1)}, u32[]{:S(2)}, u32[]{:S(2)}) collective-permute-start(bf16[4,32,2048]{2,1,0:T(8,128)(2,1)S(1)} %slice_bitcast_fusion), channel_id=1, source_target_pairs={{0,1},{1,0},{2,3},{3,2},{4,5},{5,4},{6,7},{7,6},{8,9},{9,8},{10,11... | collective-permute-start | bytes 1572872 | tf_op jit(solution)/shard_map/ppermute | solution.py:33
  183.4 4.7 %collective-permute-start.42 = (bf16[2,32,512]{2,1,0:T(8,128)(2,1)S(1)}, bf16[2,32,512]{2,1,0:T(8,128)(2,1)S(1)}, u32[]{:S(2)}, u32[]{:S(2)}) collective-permute-start(bf16[2,32,512]{2,1,0:T(8,128)(2,1)S(1)} %slice_bitcast_fusion.14), channel_id=1, source_target_pairs={{0,2},{1,3},{2,0},{3,1},{4,6},{5,7},{6,4},{7,5},{8,10},{9,11},{10,... | collective-permute-start | bytes 196616 | tf_op jit(solution)/shard_map/ppermute | solution.py:33
  184.8 8.5 %collective-permute-start.39 = (bf16[2,32,2048]{2,1,0:T(8,128)(2,1)S(1)}, bf16[2,32,2048]{2,1,0:T(8,128)(2,1)S(1)}, u32[]{:S(2)}, u32[]{:S(2)}) collective-permute-start(bf16[2,32,2048]{2,1,0:T(8,128)(2,1)S(1)} %slice_bitcast_fusion.2), channel_id=1, source_target_pairs={{0,2},{1,3},{2,0},{3,1},{4,6},{5,7},{6,4},{7,5},{8,10},{9,11},{10,... | collective-permute-start | bytes 786440 | tf_op jit(solution)/shard_map/ppermute | solution.py:33
  188.1 6.1 %collective-permute-start.43 = (bf16[32,512]{1,0:T(8,128)(2,1)S(1)}, bf16[32,512]{1,0:T(8,128)(2,1)S(1)}, u32[]{:S(2)}, u32[]{:S(2)}) collective-permute-start(bf16[32,512]{1,0:T(8,128)(2,1)S(1)} %slice_bitcast_fusion.16), channel_id=1, source_target_pairs={{0,4},{1,5},{2,6},{3,7},{4,0},{5,1},{6,2},{7,3},{8,12},{9,13},{10,... | collective-permute-start | bytes 98312 | tf_op jit(solution)/shard_map/ppermute | solution.py:33
  193.4 5.0 %collective-permute-start.40 = (bf16[32,2048]{1,0:T(8,128)(2,1)S(1)}, bf16[32,2048]{1,0:T(8,128)(2,1)S(1)}, u32[]{:S(2)}, u32[]{:S(2)}) collective-permute-start(bf16[32,2048]{1,0:T(8,128)(2,1)S(1)} %slice_bitcast_fusion.6), channel_id=1, source_target_pairs={{0,4},{1,5},{2,6},{3,7},{4,0},{5,1},{6,2},{7,3},{8,12},{9,13},{10,... | collective-permute-start | bytes 393224 | tf_op jit(solution)/shard_map/ppermute | solution.py:33
  (14 other events, 161.5 us)

commit v3 on v2

--- a/solution.py
+++ b/solution.py
@@ -49,7 +49,7 @@
     return lax.optimization_barrier((held, *earlier))[0]
 
 
-SMALL = pl.CostEstimate(flops=1, bytes_accessed=1, transcendentals=0)
+SMALL = pl.CostEstimate(flops=10**10, bytes_accessed=10**7, transcendentals=0)
 VMEM = 60 << 20
 
 
@@ -465,16 +465,15 @@
 
     def forward(by_x, by_y, *after):
         half = by_x.shape[0] // 2
-        first, second = by_x[:half], by_y[half:]
         if after:
-            first, second = tied(first, *after), tied(second, *after)
-        return over_y(first), over_x(second)
+            by_x, by_y = tied((by_x, by_y), *after)
+        return over_y(by_x[:half]), over_x(by_y[half:])
 
     x0, y0 = over_x(held[0]), over_y(held[0])
     both = []
     for array in (grads_own, windows_own, windows_arriving):
         both.append((array[0], over_core(array[0])))
-    piece = tied(held[1], both[0][1])
+    piece = tied(held[1], both[0][1], both[1][1], both[2][1])
     x1, y1 = over_x(piece), over_y(piece)
     membrane_t, grads_t, window_t = prepare(where, *both, groups, rows)
     d0 = forward(x0, y0, membrane_t)
@@ -490,15 +489,15 @@
     )
     piece = tied(held[2], x1, y1, sent_a)
     x2, y2 = over_x(piece), over_y(piece)
+    sent_b, got_b = send(
+        [(3, b0, w0), (1, b1, w1), (2, b1, w1)], [*d0, tied(x1, sent_a), y1]
+    )
     acts = []
     for array in (inputs_own, inputs_arriving):
         flat = array[0].reshape(tokens, features)
-        acts += [flat, over_core(tied(flat, x2, y2))]
-    sent_b, got_b = send(
-        [(3, b0, w0), (1, b1, w1), (2, b1, w1)], [*d0, x1, y1]
-    )
+        acts += [flat, over_core(tied(flat, got_a))]
     d1 = forward(x1, y1, sent_a)
-    d2 = forward(x2, y2, sent_b)
+    d2 = forward(x2, y2, sent_b, *d1)
     sent_c, got_c = send(
         [(3, b1, w1), (0, b2, w2), (1, b2, w2), (2, b2, w2), (3, b2, w2)],
         [*d1, held[2], tied(x2, got_a), y2, *d2],
@@ -512,12 +511,15 @@
             where, begin, width, membrane_t, window_t, arrived, sources, acts, rows
         )
 
-    def first_stage(pieces):
-        return over_x(pieces[1]), over_y(pieces[3])
-
-    def second_stage(pieces, got):
+    def first_stage(pieces, *after):
+        to_x, to_y = tied((pieces[1], pieces[3]), *after) if after else (pieces[1], pieces[3])
+        return over_x(to_x), over_y(to_y)
+
+    def second_stage(pieces, got, *after):
         pass_y = (pieces[0][1].astype(F32) + got[0][1].astype(F32)).astype(BF16)
         pass_x = (pieces[2][1].astype(F32) + got[1][1].astype(F32)).astype(BF16)
+        if after:
+            pass_y, pass_x = tied((pass_y, pass_x), *after)
         return over_y(pass_y), over_x(pass_x), (pass_y, pass_x)
 
     state = (params, first_moment[0], second_moment[0])
@@ -538,14 +540,14 @@
     pieces1 = sum_up(
         1, (got_a, got_b, got_c), [(0, w0), (1, w0), (1, w0 + w1), (2, 0)], pieces0[0]
     )
-    got1 = first_stage(pieces1)
     sums0 = second_stage(pieces0, got0)
+    got1 = first_stage(pieces1, *sums0[2])
     pieces2 = sum_up(
         2, (got_c,), [(0, w1 + r * w2) for r in range(CHIPS)], pieces1[0], *sums0[2]
     )
     got2 = first_stage(pieces2)
-    sums1 = second_stage(pieces1, got1)
     fresh, current0 = finish(0, pieces0, got0, sums0, None, pieces2[0])
+    sums1 = second_stage(pieces1, got1, pieces2[0], current0)
     sums2 = second_stage(pieces2, got2)
     fresh, current1 = finish(1, pieces1, got1, sums1, fresh)
     fresh, current2 = finish(2, pieces2, got2, sums2, fresh, current1)

time: 201 us -> 187 us (0.930)
  waiting for transfers between devices: 67.6 us -> 54.5 us
  starting transfers between devices: 39.3 us -> 41.4 us
    ppermute x41, waiting for transfers between devices: 56.5 us -> 47.8 us  [swapped(): return lax.ppermute(shard, 'dp', [(i, i ^ bit) for i in range(PARTS)])]
    ppermute x3, waiting for transfers between devices: 11.1 us -> 6.73 us  [passed_along(): return lax.ppermute(shard, axis, pairs)]
    ppermute x41, starting transfers between devices: 35.2 us -> 37.3 us  [swapped(): return lax.ppermute(shard, 'dp', [(i, i ^ bit) for i in range(PARTS)])]
  transfers between devices with their start and end apart: 44 -> 44, of which waited for: 19 -> 21; matrix products, arithmetic and copies ran while one was open for 5% -> 4% of each run, Pallas kernels for 36% -> 39%
where the time goes in v3:
time: 187 us; the launch traced here: 186 us
  Pallas kernels  75.8 us (41%)
  waiting for transfers between devices  54.5 us (29%)
  starting transfers between devices  41.4 us (22%)
  local copies, waits for them, and re-layouts  11.5 us (6%)
    ppermute x41, waiting for transfers between devices, swapped(): return lax.ppermute(shard, 'dp', [(i, i ^ bit) for i in range(PARTS)])  47.8 us
    ppermute x41, starting transfers between devices, swapped(): return lax.ppermute(shard, 'dp', [(i, i ^ bit) for i in range(PARTS)])  37.3 us
    pallas_call x3, Pallas kernels, partials(): pl.pallas_call(functools.partial(partial_kernel, sources, len(arrived), w...  26.5 us
    pallas_call x3, Pallas kernels, through(): pl.pallas_call(functools.partial(through_kernel, len(weights), pieces), o...  22 us
    pallas_call x3, Pallas kernels, update(): pl.pallas_call(functools.partial(update_kernel, whole), out_shape=(shape,...  13.7 us
    pallas_call x1, Pallas kernels, prepare(): pl.pallas_call(functools.partial(prepare_kernel, groups), out_shape=outs,...  10.8 us
    ppermute x3, waiting for transfers between devices, passed_along(): return lax.ppermute(shard, axis, pairs)  6.73 us
    ppermute x3, starting transfers between devices, passed_along(): return lax.ppermute(shard, axis, pairs)  4.15 us
  transfers between devices with their start and end apart: 44, of which 21 were waited for; matrix products, arithmetic and copies ran while one was open for 4% of the time, Pallas kernels for 39%

profile of v3, /device:TPU:0, one launch (start us, length us, event | category | flops | bytes accessed | tf_op | source)
XLA Modules:
  0.0 186.2 jit_solution(2132353672282381647)
XLA Ops:
  1.7 1.4 fusion.1.refs_0_
  3.1 2.6 %collective-permute-start.5 = (bf16[128,2560]{1,0:T(8,128)(2,1)S(1)}, bf16[128,2560]{1,0:T(8,128)(2,1)S(1)}, u32[]{:S(2)}, u32[]{:S(2)}) collective-permute-start(bf16[128,2560]{1,0:T(8,128)(2,1)S(1)} %fusion.1.refs_0_), channel_id=1, source_target_pairs={{0,2},{1,3},{2,0},{3,1},{4,6},{5,7},{6,4},{7,5},{8,10},{9,11},{10,... | collective-permute-start | bytes 1966088 | tf_op jit(solution)/shard_map/ppermute | solution.py:33
  5.7 1.5 collective-permute-start.6
  7.9 1.4 dynamic-slice_convert_fusion.refs_1_
  9.8 2.9 %collective-permute-start.3 = (bf16[128,2560]{1,0:T(8,128)(2,1)S(1)}, bf16[128,2560]{1,0:T(8,128)(2,1)}, u32[]{:S(2)}, u32[]{:S(2)}) collective-permute-start(bf16[128,2560]{1,0:T(8,128)(2,1)S(1)} %dynamic-slice_convert_fusion.refs_1_), channel_id=1, source_target_pairs={{0,2},{1,3},{2,0},{3,1},{4,6},{5,7},{6,4},{7,5},{8,10},{9,11},{10,... | collective-permute-start | bytes 1966088 | tf_op jit(solution)/shard_map/ppermute | solution.py:33
  12.6 1.5 collective-permute-start.4
  14.2 10.8 %prepare.1 = (bf16[2560,1024]{1,0:T(8,128)(2,1)}, bf16[1280,1024]{1,0:T(8,128)(2,1)}, s32[1280,256]{1,0:T(8,128)}) custom-call(s32[2]{0:T(128)} %pad_add_fusion.where, bf16[4,128,2560]{2,1,0:T(8,128)(2,1)} %bitcast.142, bf16[4,128,2560]{2,1,0:T(8,128)(2,1)} %collective-permute-done.refs_1_, s32[128,2560]{1,0:T(8,128)} %bitcast.144, ...), custom_call_target="tpu_custom_call" | custom-call | flops 10000000000 | bytes 10000000 | tf_op jit(solution)/shard_map/prepare/pallas_call | solution.py:107
  26.0 8.0 %through.3 = bf16[512,1024]{1,0:T(8,128)(2,1)} custom-call(s32[2]{0:T(128)} %pad_add_fusion.where, bf16[128,2560]{1,0:T(8,128)(2,1)} %copy-done.6, bf16[128,2560]{1,0:T(8,128)(2,1)} %copy-done.7, bf16[128,2560]{1,0:T(8,128)(2,1)} %copy-done.9, bf16[128,2560]{1,0:T(8,128)(2,1)} %copy-done.10, ...), custom_call_target="tpu_custom_call" | custom-call | flops 10000000000 | bytes 10000000 | tf_op jit(solution)/shard_map/through/pallas_call | solution.py:173
  34.0 1.3 collective-permute-start.10
  35.3 1.1 dynamic-slice_convert_fusion.2.refs_2_
  37.4 1.5 collective-permute-start.11
  41.7 2.7 %collective-permute-done.12.refs_0_ = bf16[64,2560]{1,0:T(8,128)(2,1)} collective-permute-done((bf16[64,2560]{1,0:T(8,128)(2,1)S(1)}, bf16[64,2560]{1,0:T(8,128)(2,1)}, u32[]{:S(2)}, u32[]{:S(2)}) %collective-permute-start.12) | collective-permute-done | bytes 327712 | tf_op jit(solution)/shard_map/ppermute | solution.py:33
  44.4 1.5 collective-permute-start.7
  46.5 7.0 %through.4 = bf16[384,1024]{1,0:T(8,128)(2,1)} custom-call(s32[2]{0:T(128)} %pad_add_fusion.where, bf16[64,2560]{1,0:T(8,128)(2,1)} %collective-permute-done.12.refs_0_, bf16[64,2560]{1,0:T(8,128)(2,1)} %collective-permute-done.13.refs_1_, bf16[128,2560]{1,0:T(8,128)(2,1)} %collective-permute-done.3.refs_2_, ...), custom_call_target="tpu_custom_call" | custom-call | flops 10000000000 | bytes 10000000 | tf_op jit(solution)/shard_map/through/pallas_call | solution.py:173
  53.5 4.1 %collective-permute-done.7.refs_0_ = bf16[64,2560]{1,0:T(8,128)(2,1)S(1)} collective-permute-done((bf16[64,2560]{1,0:T(8,128)(2,1)S(1)}, bf16[64,2560]{1,0:T(8,128)(2,1)S(1)}, u32[]{:S(2)}, u32[]{:S(2)}) %collective-permute-start.7) | collective-permute-done | bytes 327712 | tf_op jit(solution)/shard_map/ppermute | solution.py:33
  57.6 1.6 collective-permute-start.14
  61.3 1.4 collective-permute-start.17
  63.1 1.5 collective-permute-done.15.refs_6_
  65.3 7.0 %through.5 = bf16[384,1024]{1,0:T(8,128)(2,1)} custom-call(s32[2]{0:T(128)} %pad_add_fusion.where, bf16[64,2560]{1,0:T(8,128)(2,1)} %copy-done.14, bf16[64,2560]{1,0:T(8,128)(2,1)} %copy-done.15, bf16[64,2560]{1,0:T(8,128)(2,1)} %copy-done.8, bf16[64,2560]{1,0:T(8,128)(2,1)} %copy-done.13, bf16[64,2560]{1,0:T(8,128)(2,1)} %copy-done.12, ...), custom_call_target="tpu_custom_call" | custom-call | flops 10000000000 | bytes 10000000 | tf_op jit(solution)/shard_map/through/pallas_call | solution.py:173
  72.8 1.3 collective-permute-done.29
  74.8 1.5 collective-permute-start.16
  76.2 2.9 %collective-permute-done.30 = bf16[2,2,32,320]{3,2,1,0:T(8,128)(2,1)S(1)} collective-permute-done((bf16[2,2,32,320]{3,2,1,0:T(8,128)(2,1)S(1)}, bf16[2,2,32,320]{3,2,1,0:T(8,128)(2,1)S(1)}, u32[]{:S(2)}, u32[]{:S(2)}) %collective-permute-start.30) | collective-permute-done | bytes 81952 | tf_op jit(solution)/shard_map/ppermute | solution.py:33
  79.1 4.8 %collective-permute-done.17.refs_9_ = bf16[384,1024]{1,0:T(8,128)(2,1)S(1)} collective-permute-done((bf16[384,1024]{1,0:T(8,128)(2,1)}, bf16[384,1024]{1,0:T(8,128)(2,1)S(1)}, u32[]{:S(2)}, u32[]{:S(2)}) %collective-permute-start.17) | collective-permute-done | bytes 786464 | tf_op jit(solution)/shard_map/ppermute | solution.py:29
  83.9 2.5 %copy-done = bf16[2560,1024]{1,0:T(8,128)(2,1)S(1)} copy-done((bf16[2560,1024]{1,0:T(8,128)(2,1)S(1)}, bf16[2560,1024]{1,0:T(8,128)(2,1)}, u32[]{:S(2)}) %copy-start) | copy-done | bytes 5242904
  86.4 9.6 %partials.3 = (bf16[2,640,256]{2,1,0:T(8,128)(2,1)S(1)}, bf16[2,640,256]{2,1,0:T(8,128)(2,1)S(1)}, bf16[2,640,256]{2,1,0:T(8,128)(2,1)S(1)}, bf16[2,640,256]{2,1,0:T(8,128)(2,1)S(1)}) custom-call(s32[2]{0:T(128)S(1)} %copy-done.5, bf16[2560,1024]{1,0:T(8,128)(2,1)S(1)} %copy-done, bf16[2560,1024]{1,0:T(8,128)(2,1)S(1)} %copy-done, ...), custom_call_target="tpu_custom_call" | custom-call | flops 10000000000 | bytes 10000000 | tf_op jit(solution)/shard_map/partials/pallas_call | solution.py:278
  96.0 1.2 collective-permute-start.21
  97.2 1.5 collective-permute-start.20
  98.7 1.1 collective-permute-done.16.refs_10_.refs_8_
  99.8 9.6 %partials.4 = (bf16[2,640,256]{2,1,0:T(8,128)(2,1)S(1)}, bf16[2,640,256]{2,1,0:T(8,128)(2,1)S(1)}, bf16[2,640,256]{2,1,0:T(8,128)(2,1)S(1)}, bf16[2,640,256]{2,1,0:T(8,128)(2,1)S(1)}) custom-call(s32[2]{0:T(128)S(1)} %copy-done.5, bf16[2560,1024]{1,0:T(8,128)(2,1)S(1)} %copy-done, bf16[2560,1024]{1,0:T(8,128)(2,1)S(1)} %copy-done, ...), custom_call_target="tpu_custom_call" | custom-call | flops 10000000000 | bytes 10000000 | tf_op jit(solution)/shard_map/partials/pallas_call | solution.py:278
  109.4 2.4 %collective-permute-done.20.xr = bf16[2,640,256]{2,1,0:T(8,128)(2,1)S(1)} collective-permute-done((bf16[2,640,256]{2,1,0:T(8,128)(2,1)S(1)}, bf16[2,640,256]{2,1,0:T(8,128)(2,1)S(1)}, u32[]{:S(2)}, u32[]{:S(2)}) %collective-permute-start.20) | collective-permute-done | bytes 655392 | tf_op jit(solution)/shard_map/ppermute | solution.py:33
  113.0 1.2 collective-permute-start.27
  114.2 1.5 collective-permute-start.25
  116.2 7.3 %partials.5 = (bf16[2,640,128]{2,1,0:T(8,128)(2,1)S(1)}, bf16[2,640,128]{2,1,0:T(8,128)(2,1)S(1)}, bf16[2,640,128]{2,1,0:T(8,128)(2,1)S(1)}, bf16[2,640,128]{2,1,0:T(8,128)(2,1)S(1)}) custom-call(s32[2]{0:T(128)S(1)} %copy-done.5, bf16[2560,1024]{1,0:T(8,128)(2,1)S(1)} %copy-done, bf16[2560,1024]{1,0:T(8,128)(2,1)S(1)} %copy-done, ...), custom_call_target="tpu_custom_call" | custom-call | flops 10000000000 | bytes 10000000 | tf_op jit(solution)/shard_map/partials/pallas_call | solution.py:278
  124.8 1.2 collective-permute-start.31
  126.0 8.8 %collective-permute-done.31 = bf16[2,2,32,320]{3,2,1,0:T(8,128)(2,1)S(1)} collective-permute-done((bf16[2,2,32,320]{3,2,1,0:T(8,128)(2,1)S(1)}, bf16[2,2,32,320]{3,2,1,0:T(8,128)(2,1)S(1)}, u32[]{:S(2)}, u32[]{:S(2)}) %collective-permute-start.31) | collective-permute-done | bytes 81952 | tf_op jit(solution)/shard_map/ppermute | solution.py:33
  134.9 1.6 collective-permute-start.22
  136.4 5.3 %update.3 = (f32[320,2560]{1,0:T(8,128)}, f32[320,2560]{1,0:T(8,128)}, f32[320,2560]{1,0:T(8,128)}, bf16[256,1024]{1,0:T(8,128)(2,1)S(1)}) custom-call(s32[2]{0:T(128)S(1)} %copy-done.5, bf16[320,512]{1,0:T(8,128)(2,1)S(1)} %get-tuple-element.98.mine, bf16[320,512]{1,0:T(8,128)(2,1)S(1)} %collective-permute-done.28.theirs, f32[320,2560]{1,0:T(8,128)S(1)} %bitcast.112, ...), custom_call_target="tpu_custom_call" | custom-call | flops 167772160 | bytes 7864320 | tf_op jit(solution)/shard_map/update/pallas_call | solution.py:382
  143.4 1.1 collective-permute-start.35
  145.5 7.1 %collective-permute-done.32.xs = bf16[640,256]{1,0:T(8,128)(2,1)S(1)} collective-permute-done((bf16[640,256]{1,0:T(8,128)(2,1)S(1)}, bf16[640,256]{1,0:T(8,128)(2,1)S(1)}, u32[]{:S(2)}, u32[]{:S(2)}) %collective-permute-start.32) | collective-permute-done | bytes 327712 | tf_op jit(solution)/shard_map/ppermute | solution.py:33
  153.7 2.5 %collective-permute-done.35.yr = bf16[2,640,128]{2,1,0:T(8,128)(2,1)S(1)} collective-permute-done((bf16[2,640,128]{2,1,0:T(8,128)(2,1)S(1)}, bf16[2,640,128]{2,1,0:T(8,128)(2,1)S(1)}, u32[]{:S(2)}, u32[]{:S(2)}) %collective-permute-start.35) | collective-permute-done | bytes 327712 | tf_op jit(solution)/shard_map/ppermute | solution.py:33
  156.9 5.3 %update.4 = (f32[320,2560]{1,0:T(8,128)}, f32[320,2560]{1,0:T(8,128)}, f32[320,2560]{1,0:T(8,128)}, bf16[256,1024]{1,0:T(8,128)(2,1)S(1)}) custom-call(s32[2]{0:T(128)S(1)} %copy-done.5, bf16[320,512]{1,0:T(8,128)(2,1)S(1)} %get-tuple-element.104.mine, ...), custom_call_target="tpu_custom_call", output_to_operand_aliasing={{0}: (7, {}), {1}: (8, {}), {2}: (9, {})} | custom-call | flops 167772160 | bytes 7864320 | tf_op jit(solution)/shard_map/update/pallas_call | solution.py:382
  163.2 1.5 collective-permute-done.37.theirs
  164.7 3.2 %update.5 = (f32[320,2560]{1,0:T(8,128)}, f32[320,2560]{1,0:T(8,128)}, f32[320,2560]{1,0:T(8,128)}, bf16[256,512]{1,0:T(8,128)(2,1)S(1)}) custom-call(s32[2]{0:T(128)S(1)} %copy-done.5, bf16[320,512]{1,0:T(8,128)(2,1)S(1)} %get-tuple-element.113.mine, ...), custom_call_target="tpu_custom_call", output_to_operand_aliasing={{0}: (7, {}), {1}: (8, {}), {2}: (9, {})} | custom-call | flops 83886080 | bytes 3932160 | tf_op jit(solution)/shard_map/update/pallas_call | solution.py:382
  169.4 1.6 collective-permute-start.42
  171.9 2.0 %collective-permute-done.42 = bf16[2,32,512]{2,1,0:T(8,128)(2,1)S(1)} collective-permute-done((bf16[2,32,512]{2,1,0:T(8,128)(2,1)S(1)}, bf16[2,32,512]{2,1,0:T(8,128)(2,1)S(1)}, u32[]{:S(2)}, u32[]{:S(2)}) %collective-permute-start.42) | collective-permute-done | bytes 65568 | tf_op jit(solution)/shard_map/ppermute | solution.py:33
  174.9 4.5 %collective-permute-done.39 = bf16[2,32,2048]{2,1,0:T(8,128)(2,1)S(1)} collective-permute-done((bf16[2,32,2048]{2,1,0:T(8,128)(2,1)S(1)}, bf16[2,32,2048]{2,1,0:T(8,128)(2,1)S(1)}, u32[]{:S(2)}, u32[]{:S(2)}) %collective-permute-start.39) | collective-permute-done | bytes 262176 | tf_op jit(solution)/shard_map/ppermute | solution.py:33
  179.4 1.3 collective-permute-start.40
  180.7 3.7 %collective-permute-done.40 = bf16[32,2048]{1,0:T(8,128)(2,1)S(1)} collective-permute-done((bf16[32,2048]{1,0:T(8,128)(2,1)S(1)}, bf16[32,2048]{1,0:T(8,128)(2,1)S(1)}, u32[]{:S(2)}, u32[]{:S(2)}) %collective-permute-start.40) | collective-permute-done | bytes 131104 | tf_op jit(solution)/shard_map/ppermute | solution.py:33
  (136 shorter events, 25.3 us)
Async XLA Ops:
  0.6 9.1 %collective-permute-start = (bf16[4,128,2560]{2,1,0:T(8,128)(2,1)}, bf16[4,128,2560]{2,1,0:T(8,128)(2,1)}, u32[]{:S(2)}, u32[]{:S(2)}) collective-permute-start(bf16[4,128,2560]{2,1,0:T(8,128)(2,1)} %bitcast.141), channel_id=1, source_target_pairs={{0,1},{1,0},{2,3},{3,2},{4,5},{5,4},{6,7},{7,6},{8,9},{9,8},{10,11... | collective-permute-start | bytes 7864328 | tf_op jit(solution)/shard_map/ppermute | solution.py:33
  1.1 8.1 %collective-permute-start.1 = (s32[128,2560]{1,0:T(8,128)}, s32[128,2560]{1,0:T(8,128)}, u32[]{:S(2)}, u32[]{:S(2)}) collective-permute-start(s32[128,2560]{1,0:T(8,128)} %bitcast.143), channel_id=1, source_target_pairs={{0,1},{1,0},{2,3},{3,2},{4,5},{5,4},{6,7},{7,6},{8,9},{9,8},{10,11... | collective-permute-start | bytes 3932168 | tf_op jit(solution)/shard_map/ppermute | solution.py:33
  1.2 8.5 %collective-permute-start.2 = (s32[128,2560]{1,0:T(8,128)}, s32[128,2560]{1,0:T(8,128)}, u32[]{:S(2)}, u32[]{:S(2)}) collective-permute-start(s32[128,2560]{1,0:T(8,128)} %bitcast.145), channel_id=1, source_target_pairs={{0,1},{1,0},{2,3},{3,2},{4,5},{5,4},{6,7},{7,6},{8,9},{9,8},{10,11... | collective-permute-start | bytes 3932168 | tf_op jit(solution)/shard_map/ppermute | solution.py:33
  3.0 21.9 %copy-start.6 = (bf16[128,2560]{1,0:T(8,128)(2,1)}, bf16[128,2560]{1,0:T(8,128)(2,1)S(1)}, u32[]{:S(2)}) copy-start(bf16[128,2560]{1,0:T(8,128)(2,1)S(1)} %fusion.1.refs_0_) | copy-start | bytes 1966084
  3.1 21.9 %collective-permute-start.5 = (bf16[128,2560]{1,0:T(8,128)(2,1)S(1)}, bf16[128,2560]{1,0:T(8,128)(2,1)S(1)}, u32[]{:S(2)}, u32[]{:S(2)}) collective-permute-start(bf16[128,2560]{1,0:T(8,128)(2,1)S(1)} %fusion.1.refs_0_), channel_id=1, source_target_pairs={{0,2},{1,3},{2,0},{3,1},{4,6},{5,7},{6,4},{7,5},{8,10},{9,11},{10,... | collective-permute-start | bytes 1966088 | tf_op jit(solution)/shard_map/ppermute | solution.py:33
  5.7 19.3 %collective-permute-start.6 = (bf16[128,2560]{1,0:T(8,128)(2,1)S(1)}, bf16[128,2560]{1,0:T(8,128)(2,1)S(1)}, u32[]{:S(2)}, u32[]{:S(2)}) collective-permute-start(bf16[128,2560]{1,0:T(8,128)(2,1)S(1)} %fusion.1.refs_0_), channel_id=1, source_target_pairs={{0,4},{1,5},{2,6},{3,7},{4,0},{5,1},{6,2},{7,3},{8,12},{9,13},{10,... | collective-permute-start | bytes 1966088 | tf_op jit(solution)/shard_map/ppermute | solution.py:33
  9.3 15.7 %copy-start.7 = (bf16[128,2560]{1,0:T(8,128)(2,1)}, bf16[128,2560]{1,0:T(8,128)(2,1)S(1)}, u32[]{:S(2)}) copy-start(bf16[128,2560]{1,0:T(8,128)(2,1)S(1)} %dynamic-slice_convert_fusion.refs_1_) | copy-start | bytes 1966084
  9.8 26.7 %collective-permute-start.3 = (bf16[128,2560]{1,0:T(8,128)(2,1)S(1)}, bf16[128,2560]{1,0:T(8,128)(2,1)}, u32[]{:S(2)}, u32[]{:S(2)}) collective-permute-start(bf16[128,2560]{1,0:T(8,128)(2,1)S(1)} %dynamic-slice_convert_fusion.refs_1_), channel_id=1, source_target_pairs={{0,2},{1,3},{2,0},{3,1},{4,6},{5,7},{6,4},{7,5},{8,10},{9,11},{10,... | collective-permute-start | bytes 1966088 | tf_op jit(solution)/shard_map/ppermute | solution.py:33
  12.6 24.8 %collective-permute-start.4 = (bf16[128,2560]{1,0:T(8,128)(2,1)S(1)}, bf16[128,2560]{1,0:T(8,128)(2,1)}, u32[]{:S(2)}, u32[]{:S(2)}) collective-permute-start(bf16[128,2560]{1,0:T(8,128)(2,1)S(1)} %dynamic-slice_convert_fusion.refs_1_), channel_id=1, source_target_pairs={{0,4},{1,5},{2,6},{3,7},{4,0},{5,1},{6,2},{7,3},{8,12},{9,13},{10,... | collective-permute-start | bytes 1966088 | tf_op jit(solution)/shard_map/ppermute | solution.py:33
  25.0 19.4 %collective-permute-start.12 = (bf16[64,2560]{1,0:T(8,128)(2,1)S(1)}, bf16[64,2560]{1,0:T(8,128)(2,1)}, u32[]{:S(2)}, u32[]{:S(2)}) collective-permute-start(bf16[64,2560]{1,0:T(8,128)(2,1)S(1)} %slice.128), channel_id=1, source_target_pairs={{0,4},{1,5},{2,6},{3,7},{4,0},{5,1},{6,2},{7,3},{8,12},{9,13},{10,... | collective-permute-start | bytes 983048 | tf_op jit(solution)/shard_map/ppermute | solution.py:33
  25.6 20.4 %collective-permute-start.13 = (bf16[64,2560]{1,0:T(8,128)(2,1)S(1)}, bf16[64,2560]{1,0:T(8,128)(2,1)}, u32[]{:S(2)}, u32[]{:S(2)}) collective-permute-start(bf16[64,2560]{1,0:T(8,128)(2,1)S(1)} %slice.129), channel_id=1, source_target_pairs={{0,2},{1,3},{2,0},{3,1},{4,6},{5,7},{6,4},{7,5},{8,10},{9,11},{10,... | collective-permute-start | bytes 983048 | tf_op jit(solution)/shard_map/ppermute | solution.py:33
  34.0 26.7 %collective-permute-start.10 = (bf16[512,1024]{1,0:T(8,128)(2,1)}, bf16[512,1024]{1,0:T(8,128)(2,1)S(1)}, u32[]{:S(2)}, u32[]{:S(2)}) collective-permute-start(bf16[512,1024]{1,0:T(8,128)(2,1)} %through.3), channel_id=1, source_target_pairs={{8,0},{16,8},{24,16},{9,1},{17,9},{25,17},{10,2},{18,10},{26,18},{... | collective-permute-start | bytes 3145736 | tf_op jit(solution)/shard_map/ppermute | solution.py:29
  36.4 17.1 %copy-start.8 = (bf16[64,2560]{1,0:T(8,128)(2,1)}, bf16[64,2560]{1,0:T(8,128)(2,1)S(1)}, u32[]{:S(2)}) copy-start(bf16[64,2560]{1,0:T(8,128)(2,1)S(1)} %dynamic-slice_convert_fusion.2.refs_2_) | copy-start | bytes 983044
  37.4 16.1 %collective-permute-start.11 = (bf16[64,2560]{1,0:T(8,128)(2,1)S(1)}, bf16[64,2560]{1,0:T(8,128)(2,1)S(1)}, u32[]{:S(2)}, u32[]{:S(2)}) collective-permute-start(bf16[64,2560]{1,0:T(8,128)(2,1)S(1)} %dynamic-slice_convert_fusion.2.refs_2_), channel_id=1, source_target_pairs={{0,4},{1,5},{2,6},{3,7},{4,0},{5,1},{6,2},{7,3},{8,12},{9,13},{10,... | collective-permute-start | bytes 983048 | tf_op jit(solution)/shard_map/ppermute | solution.py:33
  38.9 14.6 %collective-permute-start.9 = (bf16[64,2560]{1,0:T(8,128)(2,1)S(1)}, bf16[64,2560]{1,0:T(8,128)(2,1)S(1)}, u32[]{:S(2)}, u32[]{:S(2)}) collective-permute-start(bf16[64,2560]{1,0:T(8,128)(2,1)S(1)} %dynamic-slice_convert_fusion.2.refs_2_), channel_id=1, source_target_pairs={{0,2},{1,3},{2,0},{3,1},{4,6},{5,7},{6,4},{7,5},{8,10},{9,11},{10,... | collective-permute-start | bytes 983048 | tf_op jit(solution)/shard_map/ppermute | solution.py:33
  44.4 13.2 %collective-permute-start.7 = (bf16[64,2560]{1,0:T(8,128)(2,1)S(1)}, bf16[64,2560]{1,0:T(8,128)(2,1)S(1)}, u32[]{:S(2)}, u32[]{:S(2)}) collective-permute-start(bf16[64,2560]{1,0:T(8,128)(2,1)S(1)} %slice.126), channel_id=1, source_target_pairs={{0,4},{1,5},{2,6},{3,7},{4,0},{5,1},{6,2},{7,3},{8,12},{9,13},{10,... | collective-permute-start | bytes 983048 | tf_op jit(solution)/shard_map/ppermute | solution.py:33
  46.0 11.6 %collective-permute-start.8 = (bf16[64,2560]{1,0:T(8,128)(2,1)S(1)}, bf16[64,2560]{1,0:T(8,128)(2,1)S(1)}, u32[]{:S(2)}, u32[]{:S(2)}) collective-permute-start(bf16[64,2560]{1,0:T(8,128)(2,1)S(1)} %slice.127), channel_id=1, source_target_pairs={{0,2},{1,3},{2,0},{3,1},{4,6},{5,7},{6,4},{7,5},{8,10},{9,11},{10,... | collective-permute-start | bytes 983048 | tf_op jit(solution)/shard_map/ppermute | solution.py:33
  57.6 5.5 %collective-permute-start.14 = (bf16[32,2560]{1,0:T(8,128)(2,1)S(1)}, bf16[32,2560]{1,0:T(8,128)(2,1)S(1)}, u32[]{:S(2)}, u32[]{:S(2)}) collective-permute-start(bf16[32,2560]{1,0:T(8,128)(2,1)S(1)} %slice.130), channel_id=1, source_target_pairs={{0,4},{1,5},{2,6},{3,7},{4,0},{5,1},{6,2},{7,3},{8,12},{9,13},{10,... | collective-permute-start | bytes 491528 | tf_op jit(solution)/shard_map/ppermute | solution.py:33
  59.2 5.4 %collective-permute-start.15 = (bf16[32,2560]{1,0:T(8,128)(2,1)S(1)}, bf16[32,2560]{1,0:T(8,128)(2,1)S(1)}, u32[]{:S(2)}, u32[]{:S(2)}) collective-permute-start(bf16[32,2560]{1,0:T(8,128)(2,1)S(1)} %slice.131), channel_id=1, source_target_pairs={{0,2},{1,3},{2,0},{3,1},{4,6},{5,7},{6,4},{7,5},{8,10},{9,11},{10,... | collective-permute-start | bytes 491528 | tf_op jit(solution)/shard_map/ppermute | solution.py:33
  60.7 23.1 %collective-permute-start.18 = (bf16[512,2560]{1,0:T(8,128)(2,1)}, bf16[512,2560]{1,0:T(8,128)(2,1)}, u32[]{:S(2)}, u32[]{:S(2)}) collective-permute-start(bf16[512,2560]{1,0:T(8,128)(2,1)} %bitcast.7.refs_10_.refs_11_.refs_9_), channel_id=1, source_target_pairs={{0,1},{1,0},{2,3},{3,2},{4,5},{5,4},{6,7},{7,6},{8,9},{9,8},{10,11... | collective-permute-start | bytes 7864328 | tf_op jit(solution)/shard_map/ppermute | solution.py:33
  60.7 23.1 %collective-permute-start.19 = (bf16[512,2560]{1,0:T(8,128)(2,1)}, bf16[512,2560]{1,0:T(8,128)(2,1)}, u32[]{:S(2)}, u32[]{:S(2)}) collective-permute-start(bf16[512,2560]{1,0:T(8,128)(2,1)} %bitcast.8.refs_12_.refs_13_.refs_11_), channel_id=1, source_target_pairs={{0,1},{1,0},{2,3},{3,2},{4,5},{5,4},{6,7},{7,6},{8,9},{9,8},{10,11... | collective-permute-start | bytes 7864328 | tf_op jit(solution)/shard_map/ppermute | solution.py:33
  61.3 22.6 %collective-permute-start.17 = (bf16[384,1024]{1,0:T(8,128)(2,1)}, bf16[384,1024]{1,0:T(8,128)(2,1)S(1)}, u32[]{:S(2)}, u32[]{:S(2)}) collective-permute-start(bf16[384,1024]{1,0:T(8,128)(2,1)} %through.4), channel_id=1, source_target_pairs={{8,0},{16,8},{24,16},{9,1},{17,9},{25,17},{10,2},{18,10},{26,18},{... | collective-permute-start | bytes 2359304 | tf_op jit(solution)/shard_map/ppermute | solution.py:29
  72.7 1.4 collective-permute-start.29
  74.2 4.9 %collective-permute-start.30 = (bf16[2,2,32,320]{3,2,1,0:T(8,128)(2,1)S(1)}, bf16[2,2,32,320]{3,2,1,0:T(8,128)(2,1)S(1)}, u32[]{:S(2)}, u32[]{:S(2)}) collective-permute-start(bf16[2,2,32,320]{3,2,1,0:T(8,128)(2,1)S(1)} %get-tuple-element.125), channel_id=1, source_target_pairs={{0,2},{1,3},{2,0},{3,1},{4,6},{5,7},{6,4},{7,5},{8,10},{9,11},{10,... | collective-permute-start | bytes 245768 | tf_op jit(solution)/shard_map/ppermute | solution.py:33
  74.8 25.0 %collective-permute-start.16 = (bf16[384,1024]{1,0:T(8,128)(2,1)}, bf16[384,1024]{1,0:T(8,128)(2,1)S(1)}, u32[]{:S(2)}, u32[]{:S(2)}) collective-permute-start(bf16[384,1024]{1,0:T(8,128)(2,1)} %through.5), channel_id=1, source_target_pairs={{8,0},{16,8},{24,16},{9,1},{17,9},{25,17},{10,2},{18,10},{26,18},{... | collective-permute-start | bytes 2359304 | tf_op jit(solution)/shard_map/ppermute | solution.py:29
  96.0 16.9 %collective-permute-start.21 = (bf16[2,640,256]{2,1,0:T(8,128)(2,1)S(1)}, bf16[2,640,256]{2,1,0:T(8,128)(2,1)S(1)}, u32[]{:S(2)}, u32[]{:S(2)}) collective-permute-start(bf16[2,640,256]{2,1,0:T(8,128)(2,1)S(1)} %get-tuple-element.88), channel_id=1, source_target_pairs={{0,4},{1,5},{2,6},{3,7},{4,0},{5,1},{6,2},{7,3},{8,12},{9,13},{10,... | collective-permute-start | bytes 1966088 | tf_op jit(solution)/shard_map/ppermute | solution.py:33
  97.2 14.6 %collective-permute-start.20 = (bf16[2,640,256]{2,1,0:T(8,128)(2,1)S(1)}, bf16[2,640,256]{2,1,0:T(8,128)(2,1)S(1)}, u32[]{:S(2)}, u32[]{:S(2)}) collective-permute-start(bf16[2,640,256]{2,1,0:T(8,128)(2,1)S(1)} %get-tuple-element.86), channel_id=1, source_target_pairs={{0,2},{1,3},{2,0},{3,1},{4,6},{5,7},{6,4},{7,5},{8,10},{9,11},{10,... | collective-permute-start | bytes 1966088 | tf_op jit(solution)/shard_map/ppermute | solution.py:33
  111.9 11.6 %collective-permute-start.26 = (bf16[640,256]{1,0:T(8,128)(2,1)S(1)}, bf16[640,256]{1,0:T(8,128)(2,1)S(1)}, u32[]{:S(2)}, u32[]{:S(2)}) collective-permute-start(bf16[640,256]{1,0:T(8,128)(2,1)S(1)} %fusion.3), channel_id=1, source_target_pairs={{0,4},{1,5},{2,6},{3,7},{4,0},{5,1},{6,2},{7,3},{8,12},{9,13},{10,... | collective-permute-start | bytes 983048 | tf_op jit(solution)/shard_map/ppermute | solution.py:33
  113.0 10.7 %collective-permute-start.27 = (bf16[640,256]{1,0:T(8,128)(2,1)S(1)}, bf16[640,256]{1,0:T(8,128)(2,1)S(1)}, u32[]{:S(2)}, u32[]{:S(2)}) collective-permute-start(bf16[640,256]{1,0:T(8,128)(2,1)S(1)} %fusion.4), channel_id=1, source_target_pairs={{0,2},{1,3},{2,0},{3,1},{4,6},{5,7},{6,4},{7,5},{8,10},{9,11},{10,... | collective-permute-start | bytes 983048 | tf_op jit(solution)/shard_map/ppermute | solution.py:33
  114.2 27.6 %collective-permute-start.25 = (bf16[2,640,256]{2,1,0:T(8,128)(2,1)S(1)}, bf16[2,640,256]{2,1,0:T(8,128)(2,1)S(1)}, u32[]{:S(2)}, u32[]{:S(2)}) collective-permute-start(bf16[2,640,256]{2,1,0:T(8,128)(2,1)S(1)} %get-tuple-element.96), channel_id=1, source_target_pairs={{0,4},{1,5},{2,6},{3,7},{4,0},{5,1},{6,2},{7,3},{8,12},{9,13},{10,... | collective-permute-start | bytes 1966088 | tf_op jit(solution)/shard_map/ppermute | solution.py:33
  115.7 26.0 %collective-permute-start.24 = (bf16[2,640,256]{2,1,0:T(8,128)(2,1)S(1)}, bf16[2,640,256]{2,1,0:T(8,128)(2,1)S(1)}, u32[]{:S(2)}, u32[]{:S(2)}) collective-permute-start(bf16[2,640,256]{2,1,0:T(8,128)(2,1)S(1)} %get-tuple-element.94), channel_id=1, source_target_pairs={{0,2},{1,3},{2,0},{3,1},{4,6},{5,7},{6,4},{7,5},{8,10},{9,11},{10,... | collective-permute-start | bytes 1966088 | tf_op jit(solution)/shard_map/ppermute | solution.py:33
  123.5 12.9 %copy-start.2 = (f32[1,320,2560]{2,1,0:T(8,128)S(1)}, f32[1,320,2560]{2,1,0:T(8,128)}, u32[]{:S(2)}) copy-start(f32[1,320,2560]{2,1,0:T(8,128)} %param.9) | copy-start | bytes 9830404
  124.6 11.8 %collective-permute-start.28 = (bf16[320,512]{1,0:T(8,128)(2,1)S(1)}, bf16[320,512]{1,0:T(8,128)(2,1)S(1)}, u32[]{:S(2)}, u32[]{:S(2)}) collective-permute-start(bf16[320,512]{1,0:T(8,128)(2,1)S(1)} %get-tuple-element.99), channel_id=1, source_target_pairs={{0,1},{1,0},{2,3},{3,2},{4,5},{5,4},{6,7},{7,6},{8,9},{9,8},{10,11... | collective-permute-start | bytes 983048 | tf_op jit(solution)/shard_map/ppermute | solution.py:33
  124.8 10.1 %collective-permute-start.31 = (bf16[2,2,32,320]{3,2,1,0:T(8,128)(2,1)S(1)}, bf16[2,2,32,320]{3,2,1,0:T(8,128)(2,1)S(1)}, u32[]{:S(2)}, u32[]{:S(2)}) collective-permute-start(bf16[2,2,32,320]{3,2,1,0:T(8,128)(2,1)S(1)} %get-tuple-element.123), channel_id=1, source_target_pairs={{0,4},{1,5},{2,6},{3,7},{4,0},{5,1},{6,2},{7,3},{8,12},{9,13},{10,... | collective-permute-start | bytes 245768 | tf_op jit(solution)/shard_map/ppermute | solution.py:33
  134.9 9.7 %collective-permute-start.22 = (bf16[2,640,128]{2,1,0:T(8,128)(2,1)S(1)}, bf16[2,640,128]{2,1,0:T(8,128)(2,1)S(1)}, u32[]{:S(2)}, u32[]{:S(2)}) collective-permute-start(bf16[2,640,128]{2,1,0:T(8,128)(2,1)S(1)} %get-tuple-element.91), channel_id=1, source_target_pairs={{0,2},{1,3},{2,0},{3,1},{4,6},{5,7},{6,4},{7,5},{8,10},{9,11},{10,... | collective-permute-start | bytes 983048 | tf_op jit(solution)/shard_map/ppermute | solution.py:33
  141.9 10.7 %collective-permute-start.32 = (bf16[640,256]{1,0:T(8,128)(2,1)S(1)}, bf16[640,256]{1,0:T(8,128)(2,1)S(1)}, u32[]{:S(2)}, u32[]{:S(2)}) collective-permute-start(bf16[640,256]{1,0:T(8,128)(2,1)S(1)} %fusion.5), channel_id=1, source_target_pairs={{0,4},{1,5},{2,6},{3,7},{4,0},{5,1},{6,2},{7,3},{8,12},{9,13},{10,... | collective-permute-start | bytes 983048 | tf_op jit(solution)/shard_map/ppermute | solution.py:33
  142.9 9.8 %collective-permute-start.33 = (bf16[640,256]{1,0:T(8,128)(2,1)S(1)}, bf16[640,256]{1,0:T(8,128)(2,1)S(1)}, u32[]{:S(2)}, u32[]{:S(2)}) collective-permute-start(bf16[640,256]{1,0:T(8,128)(2,1)S(1)} %fusion.6), channel_id=1, source_target_pairs={{0,2},{1,3},{2,0},{3,1},{4,6},{5,7},{6,4},{7,5},{8,10},{9,11},{10,... | collective-permute-start | bytes 983048 | tf_op jit(solution)/shard_map/ppermute | solution.py:33
  143.4 12.8 %collective-permute-start.35 = (bf16[2,640,128]{2,1,0:T(8,128)(2,1)S(1)}, bf16[2,640,128]{2,1,0:T(8,128)(2,1)S(1)}, u32[]{:S(2)}, u32[]{:S(2)}) collective-permute-start(bf16[2,640,128]{2,1,0:T(8,128)(2,1)S(1)} %get-tuple-element.112), channel_id=1, source_target_pairs={{0,4},{1,5},{2,6},{3,7},{4,0},{5,1},{6,2},{7,3},{8,12},{9,13},{10,... | collective-permute-start | bytes 983048 | tf_op jit(solution)/shard_map/ppermute | solution.py:33
  144.6 17.5 %collective-permute-start.23 = (bf16[640,128]{1,0:T(8,128)(2,1)S(1)}, bf16[640,128]{1,0:T(8,128)(2,1)S(1)}, u32[]{:S(2)}, u32[]{:S(2)}) collective-permute-start(bf16[640,128]{1,0:T(8,128)(2,1)S(1)} %fusion.10), channel_id=1, source_target_pairs={{0,4},{1,5},{2,6},{3,7},{4,0},{5,1},{6,2},{7,3},{8,12},{9,13},{10,... | collective-permute-start | bytes 491528 | tf_op jit(solution)/shard_map/ppermute | solution.py:33
  153.6 3.3 %collective-permute-start.34 = (bf16[320,512]{1,0:T(8,128)(2,1)S(1)}, bf16[320,512]{1,0:T(8,128)(2,1)S(1)}, u32[]{:S(2)}, u32[]{:S(2)}) collective-permute-start(bf16[320,512]{1,0:T(8,128)(2,1)S(1)} %get-tuple-element.105), channel_id=1, source_target_pairs={{0,1},{1,0},{2,3},{3,2},{4,5},{5,4},{6,7},{7,6},{8,9},{9,8},{10,11... | collective-permute-start | bytes 983048 | tf_op jit(solution)/shard_map/ppermute | solution.py:33
  156.3 5.9 %collective-permute-start.36 = (bf16[640,128]{1,0:T(8,128)(2,1)S(1)}, bf16[640,128]{1,0:T(8,128)(2,1)S(1)}, u32[]{:S(2)}, u32[]{:S(2)}) collective-permute-start(bf16[640,128]{1,0:T(8,128)(2,1)S(1)} %fusion.11), channel_id=1, source_target_pairs={{0,2},{1,3},{2,0},{3,1},{4,6},{5,7},{6,4},{7,5},{8,10},{9,11},{10,... | collective-permute-start | bytes 491528 | tf_op jit(solution)/shard_map/ppermute | solution.py:33
  163.0 1.7 collective-permute-start.37
  167.9 1.4 collective-permute-start.41
  168.2 2.8 %collective-permute-start.38 = (bf16[4,32,2048]{2,1,0:T(8,128)(2,1)S(1)}, bf16[4,32,2048]{2,1,0:T(8,128)(2,1)S(1)}, u32[]{:S(2)}, u32[]{:S(2)}) collective-permute-start(bf16[4,32,2048]{2,1,0:T(8,128)(2,1)S(1)} %slice_bitcast_fusion), channel_id=1, source_target_pairs={{0,1},{1,0},{2,3},{3,2},{4,5},{5,4},{6,7},{7,6},{8,9},{9,8},{10,11... | collective-permute-start | bytes 1572872 | tf_op jit(solution)/shard_map/ppermute | solution.py:33
  169.4 4.5 %collective-permute-start.42 = (bf16[2,32,512]{2,1,0:T(8,128)(2,1)S(1)}, bf16[2,32,512]{2,1,0:T(8,128)(2,1)S(1)}, u32[]{:S(2)}, u32[]{:S(2)}) collective-permute-start(bf16[2,32,512]{2,1,0:T(8,128)(2,1)S(1)} %slice_bitcast_fusion.14), channel_id=1, source_target_pairs={{0,2},{1,3},{2,0},{3,1},{4,6},{5,7},{6,4},{7,5},{8,10},{9,11},{10,... | collective-permute-start | bytes 196616 | tf_op jit(solution)/shard_map/ppermute | solution.py:33
  171.1 8.2 %collective-permute-start.39 = (bf16[2,32,2048]{2,1,0:T(8,128)(2,1)S(1)}, bf16[2,32,2048]{2,1,0:T(8,128)(2,1)S(1)}, u32[]{:S(2)}, u32[]{:S(2)}) collective-permute-start(bf16[2,32,2048]{2,1,0:T(8,128)(2,1)S(1)} %slice_bitcast_fusion.2), channel_id=1, source_target_pairs={{0,2},{1,3},{2,0},{3,1},{4,6},{5,7},{6,4},{7,5},{8,10},{9,11},{10,... | collective-permute-start | bytes 786440 | tf_op jit(solution)/shard_map/ppermute | solution.py:33
  173.9 6.8 %collective-permute-start.43 = (bf16[32,512]{1,0:T(8,128)(2,1)S(1)}, bf16[32,512]{1,0:T(8,128)(2,1)S(1)}, u32[]{:S(2)}, u32[]{:S(2)}) collective-permute-start(bf16[32,512]{1,0:T(8,128)(2,1)S(1)} %slice_bitcast_fusion.16), channel_id=1, source_target_pairs={{0,4},{1,5},{2,6},{3,7},{4,0},{5,1},{6,2},{7,3},{8,12},{9,13},{10,... | collective-permute-start | bytes 98312 | tf_op jit(solution)/shard_map/ppermute | solution.py:33
  179.4 5.0 %collective-permute-start.40 = (bf16[32,2048]{1,0:T(8,128)(2,1)S(1)}, bf16[32,2048]{1,0:T(8,128)(2,1)S(1)}, u32[]{:S(2)}, u32[]{:S(2)}) collective-permute-start(bf16[32,2048]{1,0:T(8,128)(2,1)S(1)} %slice_bitcast_fusion.6), channel_id=1, source_target_pairs={{0,4},{1,5},{2,6},{3,7},{4,0},{5,1},{6,2},{7,3},{8,12},{9,13},{10,... | collective-permute-start | bytes 393224 | tf_op jit(solution)/shard_map/ppermute | solution.py:33
  (14 other events, 92.1 us)

commit v4 on v3

--- a/solution.py
+++ b/solution.py
@@ -43,6 +43,10 @@
 
 def over_y(shard):
     return swapped(shard, 4)
+
+
+def over_both(shard):
+    return swapped(shard, 6)
 
 
 def tied(held, *earlier):
@@ -429,9 +433,9 @@
         return (kept.astype(F32) + got.astype(F32)).astype(BF16)
 
     held = add(held[:, 0], over_core(held[:, 1]))
-    held = held.reshape(2, 2, rows // PARTS, columns)
-    held = add(held[:, 0], over_x(held[:, 1]))
-    return add(held[0], over_y(held[1]))
+    near = held[0].astype(F32) + over_x(held[1]).astype(F32)
+    far = over_y(held[2]).astype(F32) + over_both(held[3]).astype(F32)
+    return (near + far).astype(BF16)
 
 
 def relay_shards(

time: 187 us -> 185 us (0.989)
  waiting for transfers between devices: 54.5 us -> 50.1 us
  starting transfers between devices: 41.4 us -> 44 us
    ppermute x41 -> x43, waiting for transfers between devices: 47.8 us -> 43.3 us  [swapped(): return lax.ppermute(shard, 'dp', [(i, i ^ bit) for i in range(PARTS)])]
    ppermute x41 -> x43, starting transfers between devices: 37.3 us -> 39.8 us  [swapped(): return lax.ppermute(shard, 'dp', [(i, i ^ bit) for i in range(PARTS)])]
  transfers between devices with their start and end apart: 44 -> 46, of which waited for: 21 -> 21; matrix products, arithmetic and copies ran while one was open for 4% -> 4% of each run, Pallas kernels for 39% -> 39%
where the time goes in v4:
time: 185 us; the launch traced here: 184 us
  Pallas kernels  75.8 us (41%)
  waiting for transfers between devices  50.1 us (27%)
  starting transfers between devices  44 us (24%)
  local copies, waits for them, and re-layouts  11.5 us (6%)
    ppermute x43, waiting for transfers between devices, swapped(): return lax.ppermute(shard, 'dp', [(i, i ^ bit) for i in range(PARTS)])  43.3 us
    ppermute x43, starting transfers between devices, swapped(): return lax.ppermute(shard, 'dp', [(i, i ^ bit) for i in range(PARTS)])  39.8 us
    pallas_call x3, Pallas kernels, partials(): pl.pallas_call(functools.partial(partial_kernel, sources, len(arrived), w...  26.5 us
    pallas_call x3, Pallas kernels, through(): pl.pallas_call(functools.partial(through_kernel, len(weights), pieces), o...  22 us
    pallas_call x3, Pallas kernels, update(): pl.pallas_call(functools.partial(update_kernel, whole), out_shape=(shape,...  13.7 us
    pallas_call x1, Pallas kernels, prepare(): pl.pallas_call(functools.partial(prepare_kernel, groups), out_shape=outs,...  10.8 us
    ppermute x3, waiting for transfers between devices, passed_along(): return lax.ppermute(shard, axis, pairs)  6.73 us
    ppermute x3, starting transfers between devices, passed_along(): return lax.ppermute(shard, axis, pairs)  4.15 us
  transfers between devices with their start and end apart: 46, of which 21 were waited for; matrix products, arithmetic and copies ran while one was open for 4% of the time, Pallas kernels for 39%

profile of v4, /device:TPU:0, one launch (start us, length us, event | category | flops | bytes accessed | tf_op | source)
XLA Modules:
  0.0 184.2 jit_solution(5880416990745648646)
XLA Ops:
  1.7 1.4 fusion.1.refs_0_
  3.1 2.6 %collective-permute-start.5 = (bf16[128,2560]{1,0:T(8,128)(2,1)S(1)}, bf16[128,2560]{1,0:T(8,128)(2,1)S(1)}, u32[]{:S(2)}, u32[]{:S(2)}) collective-permute-start(bf16[128,2560]{1,0:T(8,128)(2,1)S(1)} %fusion.1.refs_0_), channel_id=1, source_target_pairs={{0,2},{1,3},{2,0},{3,1},{4,6},{5,7},{6,4},{7,5},{8,10},{9,11},{10,... | collective-permute-start | bytes 1966088 | tf_op jit(solution)/shard_map/ppermute | solution.py:33
  5.7 1.5 collective-permute-start.6
  7.9 1.4 dynamic-slice_convert_fusion.refs_1_
  9.8 2.9 %collective-permute-start.3 = (bf16[128,2560]{1,0:T(8,128)(2,1)S(1)}, bf16[128,2560]{1,0:T(8,128)(2,1)}, u32[]{:S(2)}, u32[]{:S(2)}) collective-permute-start(bf16[128,2560]{1,0:T(8,128)(2,1)S(1)} %dynamic-slice_convert_fusion.refs_1_), channel_id=1, source_target_pairs={{0,2},{1,3},{2,0},{3,1},{4,6},{5,7},{6,4},{7,5},{8,10},{9,11},{10,... | collective-permute-start | bytes 1966088 | tf_op jit(solution)/shard_map/ppermute | solution.py:33
  12.6 1.5 collective-permute-start.4
  14.2 10.8 %prepare.1 = (bf16[2560,1024]{1,0:T(8,128)(2,1)}, bf16[1280,1024]{1,0:T(8,128)(2,1)}, s32[1280,256]{1,0:T(8,128)}) custom-call(s32[2]{0:T(128)} %pad_add_fusion.where, bf16[4,128,2560]{2,1,0:T(8,128)(2,1)} %bitcast.126, bf16[4,128,2560]{2,1,0:T(8,128)(2,1)} %collective-permute-done.refs_1_, s32[128,2560]{1,0:T(8,128)} %bitcast.128, ...), custom_call_target="tpu_custom_call" | custom-call | flops 10000000000 | bytes 10000000 | tf_op jit(solution)/shard_map/prepare/pallas_call | solution.py:111
  26.0 8.0 %through.3 = bf16[512,1024]{1,0:T(8,128)(2,1)} custom-call(s32[2]{0:T(128)} %pad_add_fusion.where, bf16[128,2560]{1,0:T(8,128)(2,1)} %copy-done.6, bf16[128,2560]{1,0:T(8,128)(2,1)} %copy-done.7, bf16[128,2560]{1,0:T(8,128)(2,1)} %copy-done.9, bf16[128,2560]{1,0:T(8,128)(2,1)} %copy-done.10, ...), custom_call_target="tpu_custom_call" | custom-call | flops 10000000000 | bytes 10000000 | tf_op jit(solution)/shard_map/through/pallas_call | solution.py:177
  34.0 1.3 collective-permute-start.10
  35.3 1.1 dynamic-slice_convert_fusion.2.refs_2_
  37.4 1.5 collective-permute-start.11
  41.7 2.7 %collective-permute-done.12.refs_0_ = bf16[64,2560]{1,0:T(8,128)(2,1)} collective-permute-done((bf16[64,2560]{1,0:T(8,128)(2,1)S(1)}, bf16[64,2560]{1,0:T(8,128)(2,1)}, u32[]{:S(2)}, u32[]{:S(2)}) %collective-permute-start.12) | collective-permute-done | bytes 327712 | tf_op jit(solution)/shard_map/ppermute | solution.py:33
  44.4 1.5 collective-permute-start.7
  46.5 7.0 %through.4 = bf16[384,1024]{1,0:T(8,128)(2,1)} custom-call(s32[2]{0:T(128)} %pad_add_fusion.where, bf16[64,2560]{1,0:T(8,128)(2,1)} %collective-permute-done.12.refs_0_, bf16[64,2560]{1,0:T(8,128)(2,1)} %collective-permute-done.13.refs_1_, bf16[128,2560]{1,0:T(8,128)(2,1)} %collective-permute-done.3.refs_2_, ...), custom_call_target="tpu_custom_call" | custom-call | flops 10000000000 | bytes 10000000 | tf_op jit(solution)/shard_map/through/pallas_call | solution.py:177
  53.5 4.1 %collective-permute-done.7.refs_0_ = bf16[64,2560]{1,0:T(8,128)(2,1)S(1)} collective-permute-done((bf16[64,2560]{1,0:T(8,128)(2,1)S(1)}, bf16[64,2560]{1,0:T(8,128)(2,1)S(1)}, u32[]{:S(2)}, u32[]{:S(2)}) %collective-permute-start.7) | collective-permute-done | bytes 327712 | tf_op jit(solution)/shard_map/ppermute | solution.py:33
  57.6 1.6 collective-permute-start.14
  61.2 1.4 collective-permute-start.17
  63.1 1.5 collective-permute-done.15.refs_6_
  65.3 7.0 %through.5 = bf16[384,1024]{1,0:T(8,128)(2,1)} custom-call(s32[2]{0:T(128)} %pad_add_fusion.where, bf16[64,2560]{1,0:T(8,128)(2,1)} %copy-done.14, bf16[64,2560]{1,0:T(8,128)(2,1)} %copy-done.15, bf16[64,2560]{1,0:T(8,128)(2,1)} %copy-done.8, bf16[64,2560]{1,0:T(8,128)(2,1)} %copy-done.13, bf16[64,2560]{1,0:T(8,128)(2,1)} %copy-done.12, ...), custom_call_target="tpu_custom_call" | custom-call | flops 10000000000 | bytes 10000000 | tf_op jit(solution)/shard_map/through/pallas_call | solution.py:177
  72.8 1.3 collective-permute-done.29
  74.8 1.5 collective-permute-start.16
  76.2 2.9 %collective-permute-done.30 = bf16[2,2,32,320]{3,2,1,0:T(8,128)(2,1)S(1)} collective-permute-done((bf16[2,2,32,320]{3,2,1,0:T(8,128)(2,1)S(1)}, bf16[2,2,32,320]{3,2,1,0:T(8,128)(2,1)S(1)}, u32[]{:S(2)}, u32[]{:S(2)}) %collective-permute-start.30) | collective-permute-done | bytes 81952 | tf_op jit(solution)/shard_map/ppermute | solution.py:33
  79.1 4.8 %collective-permute-done.17.refs_9_ = bf16[384,1024]{1,0:T(8,128)(2,1)S(1)} collective-permute-done((bf16[384,1024]{1,0:T(8,128)(2,1)}, bf16[384,1024]{1,0:T(8,128)(2,1)S(1)}, u32[]{:S(2)}, u32[]{:S(2)}) %collective-permute-start.17) | collective-permute-done | bytes 786464 | tf_op jit(solution)/shard_map/ppermute | solution.py:29
  83.9 2.5 %copy-done = bf16[2560,1024]{1,0:T(8,128)(2,1)S(1)} copy-done((bf16[2560,1024]{1,0:T(8,128)(2,1)S(1)}, bf16[2560,1024]{1,0:T(8,128)(2,1)}, u32[]{:S(2)}) %copy-start) | copy-done | bytes 5242904
  86.4 9.6 %partials.3 = (bf16[2,640,256]{2,1,0:T(8,128)(2,1)S(1)}, bf16[2,640,256]{2,1,0:T(8,128)(2,1)S(1)}, bf16[2,640,256]{2,1,0:T(8,128)(2,1)S(1)}, bf16[2,640,256]{2,1,0:T(8,128)(2,1)S(1)}) custom-call(s32[2]{0:T(128)S(1)} %copy-done.5, bf16[2560,1024]{1,0:T(8,128)(2,1)S(1)} %copy-done, bf16[2560,1024]{1,0:T(8,128)(2,1)S(1)} %copy-done, ...), custom_call_target="tpu_custom_call" | custom-call | flops 10000000000 | bytes 10000000 | tf_op jit(solution)/shard_map/partials/pallas_call | solution.py:282
  96.0 1.2 collective-permute-start.21
  97.2 1.5 collective-permute-start.20
  99.8 9.6 %partials.4 = (bf16[2,640,256]{2,1,0:T(8,128)(2,1)S(1)}, bf16[2,640,256]{2,1,0:T(8,128)(2,1)S(1)}, bf16[2,640,256]{2,1,0:T(8,128)(2,1)S(1)}, bf16[2,640,256]{2,1,0:T(8,128)(2,1)S(1)}) custom-call(s32[2]{0:T(128)S(1)} %copy-done.5, bf16[2560,1024]{1,0:T(8,128)(2,1)S(1)} %copy-done, bf16[2560,1024]{1,0:T(8,128)(2,1)S(1)} %copy-done, ...), custom_call_target="tpu_custom_call" | custom-call | flops 10000000000 | bytes 10000000 | tf_op jit(solution)/shard_map/partials/pallas_call | solution.py:282
  109.4 2.4 %collective-permute-done.20.xr = bf16[2,640,256]{2,1,0:T(8,128)(2,1)S(1)} collective-permute-done((bf16[2,640,256]{2,1,0:T(8,128)(2,1)S(1)}, bf16[2,640,256]{2,1,0:T(8,128)(2,1)S(1)}, u32[]{:S(2)}, u32[]{:S(2)}) %collective-permute-start.20) | collective-permute-done | bytes 655392 | tf_op jit(solution)/shard_map/ppermute | solution.py:33
  112.9 1.2 collective-permute-start.27
  114.2 1.5 collective-permute-start.25
  116.2 7.3 %partials.5 = (bf16[2,640,128]{2,1,0:T(8,128)(2,1)S(1)}, bf16[2,640,128]{2,1,0:T(8,128)(2,1)S(1)}, bf16[2,640,128]{2,1,0:T(8,128)(2,1)S(1)}, bf16[2,640,128]{2,1,0:T(8,128)(2,1)S(1)}) custom-call(s32[2]{0:T(128)S(1)} %copy-done.5, bf16[2560,1024]{1,0:T(8,128)(2,1)S(1)} %copy-done, bf16[2560,1024]{1,0:T(8,128)(2,1)S(1)} %copy-done, ...), custom_call_target="tpu_custom_call" | custom-call | flops 10000000000 | bytes 10000000 | tf_op jit(solution)/shard_map/partials/pallas_call | solution.py:282
  124.7 1.2 collective-permute-start.31
  126.0 8.8 %collective-permute-done.31 = bf16[2,2,32,320]{3,2,1,0:T(8,128)(2,1)S(1)} collective-permute-done((bf16[2,2,32,320]{3,2,1,0:T(8,128)(2,1)S(1)}, bf16[2,2,32,320]{3,2,1,0:T(8,128)(2,1)S(1)}, u32[]{:S(2)}, u32[]{:S(2)}) %collective-permute-start.31) | collective-permute-done | bytes 81952 | tf_op jit(solution)/shard_map/ppermute | solution.py:33
  134.9 1.6 collective-permute-start.22
  136.4 5.3 %update.3 = (f32[320,2560]{1,0:T(8,128)}, f32[320,2560]{1,0:T(8,128)}, f32[320,2560]{1,0:T(8,128)}, bf16[256,1024]{1,0:T(8,128)(2,1)S(1)}) custom-call(s32[2]{0:T(128)S(1)} %copy-done.5, bf16[320,512]{1,0:T(8,128)(2,1)S(1)} %get-tuple-element.98.mine, bf16[320,512]{1,0:T(8,128)(2,1)S(1)} %collective-permute-done.28.theirs, f32[320,2560]{1,0:T(8,128)S(1)} %bitcast.100, ...), custom_call_target="tpu_custom_call" | custom-call | flops 167772160 | bytes 7864320 | tf_op jit(solution)/shard_map/update/pallas_call | solution.py:386
  143.4 1.1 collective-permute-start.35
  145.5 7.1 %collective-permute-done.32.xs = bf16[640,256]{1,0:T(8,128)(2,1)S(1)} collective-permute-done((bf16[640,256]{1,0:T(8,128)(2,1)S(1)}, bf16[640,256]{1,0:T(8,128)(2,1)S(1)}, u32[]{:S(2)}, u32[]{:S(2)}) %collective-permute-start.32) | collective-permute-done | bytes 327712 | tf_op jit(solution)/shard_map/ppermute | solution.py:33
  153.7 2.5 %collective-permute-done.35.yr = bf16[2,640,128]{2,1,0:T(8,128)(2,1)S(1)} collective-permute-done((bf16[2,640,128]{2,1,0:T(8,128)(2,1)S(1)}, bf16[2,640,128]{2,1,0:T(8,128)(2,1)S(1)}, u32[]{:S(2)}, u32[]{:S(2)}) %collective-permute-start.35) | collective-permute-done | bytes 327712 | tf_op jit(solution)/shard_map/ppermute | solution.py:33
  156.9 5.3 %update.4 = (f32[320,2560]{1,0:T(8,128)}, f32[320,2560]{1,0:T(8,128)}, f32[320,2560]{1,0:T(8,128)}, bf16[256,1024]{1,0:T(8,128)(2,1)S(1)}) custom-call(s32[2]{0:T(128)S(1)} %copy-done.5, bf16[320,512]{1,0:T(8,128)(2,1)S(1)} %get-tuple-element.104.mine, ...), custom_call_target="tpu_custom_call", output_to_operand_aliasing={{0}: (7, {}), {1}: (8, {}), {2}: (9, {})} | custom-call | flops 167772160 | bytes 7864320 | tf_op jit(solution)/shard_map/update/pallas_call | solution.py:386
  163.2 1.5 collective-permute-done.37.theirs
  164.7 3.2 %update.5 = (f32[320,2560]{1,0:T(8,128)}, f32[320,2560]{1,0:T(8,128)}, f32[320,2560]{1,0:T(8,128)}, bf16[256,512]{1,0:T(8,128)(2,1)S(1)}) custom-call(s32[2]{0:T(128)S(1)} %copy-done.5, bf16[320,512]{1,0:T(8,128)(2,1)S(1)} %get-tuple-element.113.mine, ...), custom_call_target="tpu_custom_call", output_to_operand_aliasing={{0}: (7, {}), {1}: (8, {}), {2}: (9, {})} | custom-call | flops 83886080 | bytes 3932160 | tf_op jit(solution)/shard_map/update/pallas_call | solution.py:386
  169.4 1.6 collective-permute-start.43
  170.9 1.3 collective-permute-start.44
  173.1 1.6 collective-permute-start.39
  174.7 1.3 collective-permute-start.40
  177.5 1.5 collective-permute-done.39
  179.0 3.4 %collective-permute-done.40 = bf16[32,2048]{1,0:T(8,128)(2,1)S(1)} collective-permute-done((bf16[32,2048]{1,0:T(8,128)(2,1)S(1)}, bf16[32,2048]{1,0:T(8,128)(2,1)S(1)}, u32[]{:S(2)}, u32[]{:S(2)}) %collective-permute-start.40) | collective-permute-done | bytes 131104 | tf_op jit(solution)/shard_map/ppermute | solution.py:33
  (136 shorter events, 26.9 us)
Async XLA Ops:
  0.6 9.1 %collective-permute-start = (bf16[4,128,2560]{2,1,0:T(8,128)(2,1)}, bf16[4,128,2560]{2,1,0:T(8,128)(2,1)}, u32[]{:S(2)}, u32[]{:S(2)}) collective-permute-start(bf16[4,128,2560]{2,1,0:T(8,128)(2,1)} %bitcast.125), channel_id=1, source_target_pairs={{0,1},{1,0},{2,3},{3,2},{4,5},{5,4},{6,7},{7,6},{8,9},{9,8},{10,11... | collective-permute-start | bytes 7864328 | tf_op jit(solution)/shard_map/ppermute | solution.py:33
  1.1 8.1 %collective-permute-start.1 = (s32[128,2560]{1,0:T(8,128)}, s32[128,2560]{1,0:T(8,128)}, u32[]{:S(2)}, u32[]{:S(2)}) collective-permute-start(s32[128,2560]{1,0:T(8,128)} %bitcast.127), channel_id=1, source_target_pairs={{0,1},{1,0},{2,3},{3,2},{4,5},{5,4},{6,7},{7,6},{8,9},{9,8},{10,11... | collective-permute-start | bytes 3932168 | tf_op jit(solution)/shard_map/ppermute | solution.py:33
  1.2 8.5 %collective-permute-start.2 = (s32[128,2560]{1,0:T(8,128)}, s32[128,2560]{1,0:T(8,128)}, u32[]{:S(2)}, u32[]{:S(2)}) collective-permute-start(s32[128,2560]{1,0:T(8,128)} %bitcast.129), channel_id=1, source_target_pairs={{0,1},{1,0},{2,3},{3,2},{4,5},{5,4},{6,7},{7,6},{8,9},{9,8},{10,11... | collective-permute-start | bytes 3932168 | tf_op jit(solution)/shard_map/ppermute | solution.py:33
  3.0 21.9 %copy-start.6 = (bf16[128,2560]{1,0:T(8,128)(2,1)}, bf16[128,2560]{1,0:T(8,128)(2,1)S(1)}, u32[]{:S(2)}) copy-start(bf16[128,2560]{1,0:T(8,128)(2,1)S(1)} %fusion.1.refs_0_) | copy-start | bytes 1966084
  3.1 21.9 %collective-permute-start.5 = (bf16[128,2560]{1,0:T(8,128)(2,1)S(1)}, bf16[128,2560]{1,0:T(8,128)(2,1)S(1)}, u32[]{:S(2)}, u32[]{:S(2)}) collective-permute-start(bf16[128,2560]{1,0:T(8,128)(2,1)S(1)} %fusion.1.refs_0_), channel_id=1, source_target_pairs={{0,2},{1,3},{2,0},{3,1},{4,6},{5,7},{6,4},{7,5},{8,10},{9,11},{10,... | collective-permute-start | bytes 1966088 | tf_op jit(solution)/shard_map/ppermute | solution.py:33
  5.7 19.3 %collective-permute-start.6 = (bf16[128,2560]{1,0:T(8,128)(2,1)S(1)}, bf16[128,2560]{1,0:T(8,128)(2,1)S(1)}, u32[]{:S(2)}, u32[]{:S(2)}) collective-permute-start(bf16[128,2560]{1,0:T(8,128)(2,1)S(1)} %fusion.1.refs_0_), channel_id=1, source_target_pairs={{0,4},{1,5},{2,6},{3,7},{4,0},{5,1},{6,2},{7,3},{8,12},{9,13},{10,... | collective-permute-start | bytes 1966088 | tf_op jit(solution)/shard_map/ppermute | solution.py:33
  9.8 26.6 %collective-permute-start.3 = (bf16[128,2560]{1,0:T(8,128)(2,1)S(1)}, bf16[128,2560]{1,0:T(8,128)(2,1)}, u32[]{:S(2)}, u32[]{:S(2)}) collective-permute-start(bf16[128,2560]{1,0:T(8,128)(2,1)S(1)} %dynamic-slice_convert_fusion.refs_1_), channel_id=1, source_target_pairs={{0,2},{1,3},{2,0},{3,1},{4,6},{5,7},{6,4},{7,5},{8,10},{9,11},{10,... | collective-permute-start | bytes 1966088 | tf_op jit(solution)/shard_map/ppermute | solution.py:33
  12.6 24.8 %collective-permute-start.4 = (bf16[128,2560]{1,0:T(8,128)(2,1)S(1)}, bf16[128,2560]{1,0:T(8,128)(2,1)}, u32[]{:S(2)}, u32[]{:S(2)}) collective-permute-start(bf16[128,2560]{1,0:T(8,128)(2,1)S(1)} %dynamic-slice_convert_fusion.refs_1_), channel_id=1, source_target_pairs={{0,4},{1,5},{2,6},{3,7},{4,0},{5,1},{6,2},{7,3},{8,12},{9,13},{10,... | collective-permute-start | bytes 1966088 | tf_op jit(solution)/shard_map/ppermute | solution.py:33
  25.0 19.4 %collective-permute-start.12 = (bf16[64,2560]{1,0:T(8,128)(2,1)S(1)}, bf16[64,2560]{1,0:T(8,128)(2,1)}, u32[]{:S(2)}, u32[]{:S(2)}) collective-permute-start(bf16[64,2560]{1,0:T(8,128)(2,1)S(1)} %slice.128), channel_id=1, source_target_pairs={{0,4},{1,5},{2,6},{3,7},{4,0},{5,1},{6,2},{7,3},{8,12},{9,13},{10,... | collective-permute-start | bytes 983048 | tf_op jit(solution)/shard_map/ppermute | solution.py:33
  25.6 20.4 %collective-permute-start.13 = (bf16[64,2560]{1,0:T(8,128)(2,1)S(1)}, bf16[64,2560]{1,0:T(8,128)(2,1)}, u32[]{:S(2)}, u32[]{:S(2)}) collective-permute-start(bf16[64,2560]{1,0:T(8,128)(2,1)S(1)} %slice.129), channel_id=1, source_target_pairs={{0,2},{1,3},{2,0},{3,1},{4,6},{5,7},{6,4},{7,5},{8,10},{9,11},{10,... | collective-permute-start | bytes 983048 | tf_op jit(solution)/shard_map/ppermute | solution.py:33
  34.0 26.7 %collective-permute-start.10 = (bf16[512,1024]{1,0:T(8,128)(2,1)}, bf16[512,1024]{1,0:T(8,128)(2,1)S(1)}, u32[]{:S(2)}, u32[]{:S(2)}) collective-permute-start(bf16[512,1024]{1,0:T(8,128)(2,1)} %through.3), channel_id=1, source_target_pairs={{8,0},{16,8},{24,16},{9,1},{17,9},{25,17},{10,2},{18,10},{26,18},{... | collective-permute-start | bytes 3145736 | tf_op jit(solution)/shard_map/ppermute | solution.py:29
  36.4 17.1 %copy-start.8 = (bf16[64,2560]{1,0:T(8,128)(2,1)}, bf16[64,2560]{1,0:T(8,128)(2,1)S(1)}, u32[]{:S(2)}) copy-start(bf16[64,2560]{1,0:T(8,128)(2,1)S(1)} %dynamic-slice_convert_fusion.2.refs_2_) | copy-start | bytes 983044
  37.4 16.1 %collective-permute-start.11 = (bf16[64,2560]{1,0:T(8,128)(2,1)S(1)}, bf16[64,2560]{1,0:T(8,128)(2,1)S(1)}, u32[]{:S(2)}, u32[]{:S(2)}) collective-permute-start(bf16[64,2560]{1,0:T(8,128)(2,1)S(1)} %dynamic-slice_convert_fusion.2.refs_2_), channel_id=1, source_target_pairs={{0,4},{1,5},{2,6},{3,7},{4,0},{5,1},{6,2},{7,3},{8,12},{9,13},{10,... | collective-permute-start | bytes 983048 | tf_op jit(solution)/shard_map/ppermute | solution.py:33
  38.9 14.6 %collective-permute-start.9 = (bf16[64,2560]{1,0:T(8,128)(2,1)S(1)}, bf16[64,2560]{1,0:T(8,128)(2,1)S(1)}, u32[]{:S(2)}, u32[]{:S(2)}) collective-permute-start(bf16[64,2560]{1,0:T(8,128)(2,1)S(1)} %dynamic-slice_convert_fusion.2.refs_2_), channel_id=1, source_target_pairs={{0,2},{1,3},{2,0},{3,1},{4,6},{5,7},{6,4},{7,5},{8,10},{9,11},{10,... | collective-permute-start | bytes 983048 | tf_op jit(solution)/shard_map/ppermute | solution.py:33
  44.4 13.2 %collective-permute-start.7 = (bf16[64,2560]{1,0:T(8,128)(2,1)S(1)}, bf16[64,2560]{1,0:T(8,128)(2,1)S(1)}, u32[]{:S(2)}, u32[]{:S(2)}) collective-permute-start(bf16[64,2560]{1,0:T(8,128)(2,1)S(1)} %slice.126), channel_id=1, source_target_pairs={{0,4},{1,5},{2,6},{3,7},{4,0},{5,1},{6,2},{7,3},{8,12},{9,13},{10,... | collective-permute-start | bytes 983048 | tf_op jit(solution)/shard_map/ppermute | solution.py:33
  46.0 11.6 %collective-permute-start.8 = (bf16[64,2560]{1,0:T(8,128)(2,1)S(1)}, bf16[64,2560]{1,0:T(8,128)(2,1)S(1)}, u32[]{:S(2)}, u32[]{:S(2)}) collective-permute-start(bf16[64,2560]{1,0:T(8,128)(2,1)S(1)} %slice.127), channel_id=1, source_target_pairs={{0,2},{1,3},{2,0},{3,1},{4,6},{5,7},{6,4},{7,5},{8,10},{9,11},{10,... | collective-permute-start | bytes 983048 | tf_op jit(solution)/shard_map/ppermute | solution.py:33
  57.6 5.5 %collective-permute-start.14 = (bf16[32,2560]{1,0:T(8,128)(2,1)S(1)}, bf16[32,2560]{1,0:T(8,128)(2,1)S(1)}, u32[]{:S(2)}, u32[]{:S(2)}) collective-permute-start(bf16[32,2560]{1,0:T(8,128)(2,1)S(1)} %slice.130), channel_id=1, source_target_pairs={{0,4},{1,5},{2,6},{3,7},{4,0},{5,1},{6,2},{7,3},{8,12},{9,13},{10,... | collective-permute-start | bytes 491528 | tf_op jit(solution)/shard_map/ppermute | solution.py:33
  59.2 5.4 %collective-permute-start.15 = (bf16[32,2560]{1,0:T(8,128)(2,1)S(1)}, bf16[32,2560]{1,0:T(8,128)(2,1)S(1)}, u32[]{:S(2)}, u32[]{:S(2)}) collective-permute-start(bf16[32,2560]{1,0:T(8,128)(2,1)S(1)} %slice.131), channel_id=1, source_target_pairs={{0,2},{1,3},{2,0},{3,1},{4,6},{5,7},{6,4},{7,5},{8,10},{9,11},{10,... | collective-permute-start | bytes 491528 | tf_op jit(solution)/shard_map/ppermute | solution.py:33
  60.7 23.1 %collective-permute-start.18 = (bf16[512,2560]{1,0:T(8,128)(2,1)}, bf16[512,2560]{1,0:T(8,128)(2,1)}, u32[]{:S(2)}, u32[]{:S(2)}) collective-permute-start(bf16[512,2560]{1,0:T(8,128)(2,1)} %bitcast.7.refs_10_.refs_11_.refs_9_), channel_id=1, source_target_pairs={{0,1},{1,0},{2,3},{3,2},{4,5},{5,4},{6,7},{7,6},{8,9},{9,8},{10,11... | collective-permute-start | bytes 7864328 | tf_op jit(solution)/shard_map/ppermute | solution.py:33
  60.7 23.1 %collective-permute-start.19 = (bf16[512,2560]{1,0:T(8,128)(2,1)}, bf16[512,2560]{1,0:T(8,128)(2,1)}, u32[]{:S(2)}, u32[]{:S(2)}) collective-permute-start(bf16[512,2560]{1,0:T(8,128)(2,1)} %bitcast.8.refs_12_.refs_13_.refs_11_), channel_id=1, source_target_pairs={{0,1},{1,0},{2,3},{3,2},{4,5},{5,4},{6,7},{7,6},{8,9},{9,8},{10,11... | collective-permute-start | bytes 7864328 | tf_op jit(solution)/shard_map/ppermute | solution.py:33
  61.2 22.6 %collective-permute-start.17 = (bf16[384,1024]{1,0:T(8,128)(2,1)}, bf16[384,1024]{1,0:T(8,128)(2,1)S(1)}, u32[]{:S(2)}, u32[]{:S(2)}) collective-permute-start(bf16[384,1024]{1,0:T(8,128)(2,1)} %through.4), channel_id=1, source_target_pairs={{8,0},{16,8},{24,16},{9,1},{17,9},{25,17},{10,2},{18,10},{26,18},{... | collective-permute-start | bytes 2359304 | tf_op jit(solution)/shard_map/ppermute | solution.py:29
  72.7 1.4 collective-permute-start.29
  74.2 4.9 %collective-permute-start.30 = (bf16[2,2,32,320]{3,2,1,0:T(8,128)(2,1)S(1)}, bf16[2,2,32,320]{3,2,1,0:T(8,128)(2,1)S(1)}, u32[]{:S(2)}, u32[]{:S(2)}) collective-permute-start(bf16[2,2,32,320]{3,2,1,0:T(8,128)(2,1)S(1)} %get-tuple-element.128), channel_id=1, source_target_pairs={{0,2},{1,3},{2,0},{3,1},{4,6},{5,7},{6,4},{7,5},{8,10},{9,11},{10,... | collective-permute-start | bytes 245768 | tf_op jit(solution)/shard_map/ppermute | solution.py:33
  74.8 25.0 %collective-permute-start.16 = (bf16[384,1024]{1,0:T(8,128)(2,1)}, bf16[384,1024]{1,0:T(8,128)(2,1)S(1)}, u32[]{:S(2)}, u32[]{:S(2)}) collective-permute-start(bf16[384,1024]{1,0:T(8,128)(2,1)} %through.5), channel_id=1, source_target_pairs={{8,0},{16,8},{24,16},{9,1},{17,9},{25,17},{10,2},{18,10},{26,18},{... | collective-permute-start | bytes 2359304 | tf_op jit(solution)/shard_map/ppermute | solution.py:29
  96.0 16.9 %collective-permute-start.21 = (bf16[2,640,256]{2,1,0:T(8,128)(2,1)S(1)}, bf16[2,640,256]{2,1,0:T(8,128)(2,1)S(1)}, u32[]{:S(2)}, u32[]{:S(2)}) collective-permute-start(bf16[2,640,256]{2,1,0:T(8,128)(2,1)S(1)} %get-tuple-element.88), channel_id=1, source_target_pairs={{0,4},{1,5},{2,6},{3,7},{4,0},{5,1},{6,2},{7,3},{8,12},{9,13},{10,... | collective-permute-start | bytes 1966088 | tf_op jit(solution)/shard_map/ppermute | solution.py:33
  97.2 14.6 %collective-permute-start.20 = (bf16[2,640,256]{2,1,0:T(8,128)(2,1)S(1)}, bf16[2,640,256]{2,1,0:T(8,128)(2,1)S(1)}, u32[]{:S(2)}, u32[]{:S(2)}) collective-permute-start(bf16[2,640,256]{2,1,0:T(8,128)(2,1)S(1)} %get-tuple-element.86), channel_id=1, source_target_pairs={{0,2},{1,3},{2,0},{3,1},{4,6},{5,7},{6,4},{7,5},{8,10},{9,11},{10,... | collective-permute-start | bytes 1966088 | tf_op jit(solution)/shard_map/ppermute | solution.py:33
  111.9 11.6 %collective-permute-start.26 = (bf16[640,256]{1,0:T(8,128)(2,1)S(1)}, bf16[640,256]{1,0:T(8,128)(2,1)S(1)}, u32[]{:S(2)}, u32[]{:S(2)}) collective-permute-start(bf16[640,256]{1,0:T(8,128)(2,1)S(1)} %fusion.2), channel_id=1, source_target_pairs={{0,4},{1,5},{2,6},{3,7},{4,0},{5,1},{6,2},{7,3},{8,12},{9,13},{10,... | collective-permute-start | bytes 983048 | tf_op jit(solution)/shard_map/ppermute | solution.py:33
  112.9 10.7 %collective-permute-start.27 = (bf16[640,256]{1,0:T(8,128)(2,1)S(1)}, bf16[640,256]{1,0:T(8,128)(2,1)S(1)}, u32[]{:S(2)}, u32[]{:S(2)}) collective-permute-start(bf16[640,256]{1,0:T(8,128)(2,1)S(1)} %fusion.3), channel_id=1, source_target_pairs={{0,2},{1,3},{2,0},{3,1},{4,6},{5,7},{6,4},{7,5},{8,10},{9,11},{10,... | collective-permute-start | bytes 983048 | tf_op jit(solution)/shard_map/ppermute | solution.py:33
  114.2 27.6 %collective-permute-start.25 = (bf16[2,640,256]{2,1,0:T(8,128)(2,1)S(1)}, bf16[2,640,256]{2,1,0:T(8,128)(2,1)S(1)}, u32[]{:S(2)}, u32[]{:S(2)}) collective-permute-start(bf16[2,640,256]{2,1,0:T(8,128)(2,1)S(1)} %get-tuple-element.96), channel_id=1, source_target_pairs={{0,4},{1,5},{2,6},{3,7},{4,0},{5,1},{6,2},{7,3},{8,12},{9,13},{10,... | collective-permute-start | bytes 1966088 | tf_op jit(solution)/shard_map/ppermute | solution.py:33
  115.7 26.0 %collective-permute-start.24 = (bf16[2,640,256]{2,1,0:T(8,128)(2,1)S(1)}, bf16[2,640,256]{2,1,0:T(8,128)(2,1)S(1)}, u32[]{:S(2)}, u32[]{:S(2)}) collective-permute-start(bf16[2,640,256]{2,1,0:T(8,128)(2,1)S(1)} %get-tuple-element.94), channel_id=1, source_target_pairs={{0,2},{1,3},{2,0},{3,1},{4,6},{5,7},{6,4},{7,5},{8,10},{9,11},{10,... | collective-permute-start | bytes 1966088 | tf_op jit(solution)/shard_map/ppermute | solution.py:33
  124.6 11.8 %collective-permute-start.28 = (bf16[320,512]{1,0:T(8,128)(2,1)S(1)}, bf16[320,512]{1,0:T(8,128)(2,1)S(1)}, u32[]{:S(2)}, u32[]{:S(2)}) collective-permute-start(bf16[320,512]{1,0:T(8,128)(2,1)S(1)} %get-tuple-element.99), channel_id=1, source_target_pairs={{0,1},{1,0},{2,3},{3,2},{4,5},{5,4},{6,7},{7,6},{8,9},{9,8},{10,11... | collective-permute-start | bytes 983048 | tf_op jit(solution)/shard_map/ppermute | solution.py:33
  124.7 10.1 %collective-permute-start.31 = (bf16[2,2,32,320]{3,2,1,0:T(8,128)(2,1)S(1)}, bf16[2,2,32,320]{3,2,1,0:T(8,128)(2,1)S(1)}, u32[]{:S(2)}, u32[]{:S(2)}) collective-permute-start(bf16[2,2,32,320]{3,2,1,0:T(8,128)(2,1)S(1)} %get-tuple-element.126), channel_id=1, source_target_pairs={{0,4},{1,5},{2,6},{3,7},{4,0},{5,1},{6,2},{7,3},{8,12},{9,13},{10,... | collective-permute-start | bytes 245768 | tf_op jit(solution)/shard_map/ppermute | solution.py:33
  134.9 9.7 %collective-permute-start.22 = (bf16[2,640,128]{2,1,0:T(8,128)(2,1)S(1)}, bf16[2,640,128]{2,1,0:T(8,128)(2,1)S(1)}, u32[]{:S(2)}, u32[]{:S(2)}) collective-permute-start(bf16[2,640,128]{2,1,0:T(8,128)(2,1)S(1)} %get-tuple-element.91), channel_id=1, source_target_pairs={{0,2},{1,3},{2,0},{3,1},{4,6},{5,7},{6,4},{7,5},{8,10},{9,11},{10,... | collective-permute-start | bytes 983048 | tf_op jit(solution)/shard_map/ppermute | solution.py:33
  141.9 10.7 %collective-permute-start.32 = (bf16[640,256]{1,0:T(8,128)(2,1)S(1)}, bf16[640,256]{1,0:T(8,128)(2,1)S(1)}, u32[]{:S(2)}, u32[]{:S(2)}) collective-permute-start(bf16[640,256]{1,0:T(8,128)(2,1)S(1)} %fusion.4), channel_id=1, source_target_pairs={{0,4},{1,5},{2,6},{3,7},{4,0},{5,1},{6,2},{7,3},{8,12},{9,13},{10,... | collective-permute-start | bytes 983048 | tf_op jit(solution)/shard_map/ppermute | solution.py:33
  142.9 9.8 %collective-permute-start.33 = (bf16[640,256]{1,0:T(8,128)(2,1)S(1)}, bf16[640,256]{1,0:T(8,128)(2,1)S(1)}, u32[]{:S(2)}, u32[]{:S(2)}) collective-permute-start(bf16[640,256]{1,0:T(8,128)(2,1)S(1)} %fusion.5), channel_id=1, source_target_pairs={{0,2},{1,3},{2,0},{3,1},{4,6},{5,7},{6,4},{7,5},{8,10},{9,11},{10,... | collective-permute-start | bytes 983048 | tf_op jit(solution)/shard_map/ppermute | solution.py:33
  143.4 12.8 %collective-permute-start.35 = (bf16[2,640,128]{2,1,0:T(8,128)(2,1)S(1)}, bf16[2,640,128]{2,1,0:T(8,128)(2,1)S(1)}, u32[]{:S(2)}, u32[]{:S(2)}) collective-permute-start(bf16[2,640,128]{2,1,0:T(8,128)(2,1)S(1)} %get-tuple-element.112), channel_id=1, source_target_pairs={{0,4},{1,5},{2,6},{3,7},{4,0},{5,1},{6,2},{7,3},{8,12},{9,13},{10,... | collective-permute-start | bytes 983048 | tf_op jit(solution)/shard_map/ppermute | solution.py:33
  144.6 17.5 %collective-permute-start.23 = (bf16[640,128]{1,0:T(8,128)(2,1)S(1)}, bf16[640,128]{1,0:T(8,128)(2,1)S(1)}, u32[]{:S(2)}, u32[]{:S(2)}) collective-permute-start(bf16[640,128]{1,0:T(8,128)(2,1)S(1)} %fusion.10), channel_id=1, source_target_pairs={{0,4},{1,5},{2,6},{3,7},{4,0},{5,1},{6,2},{7,3},{8,12},{9,13},{10,... | collective-permute-start | bytes 491528 | tf_op jit(solution)/shard_map/ppermute | solution.py:33
  153.6 3.3 %collective-permute-start.34 = (bf16[320,512]{1,0:T(8,128)(2,1)S(1)}, bf16[320,512]{1,0:T(8,128)(2,1)S(1)}, u32[]{:S(2)}, u32[]{:S(2)}) collective-permute-start(bf16[320,512]{1,0:T(8,128)(2,1)S(1)} %get-tuple-element.105), channel_id=1, source_target_pairs={{0,1},{1,0},{2,3},{3,2},{4,5},{5,4},{6,7},{7,6},{8,9},{9,8},{10,11... | collective-permute-start | bytes 983048 | tf_op jit(solution)/shard_map/ppermute | solution.py:33
  156.3 5.9 %collective-permute-start.36 = (bf16[640,128]{1,0:T(8,128)(2,1)S(1)}, bf16[640,128]{1,0:T(8,128)(2,1)S(1)}, u32[]{:S(2)}, u32[]{:S(2)}) collective-permute-start(bf16[640,128]{1,0:T(8,128)(2,1)S(1)} %fusion.11), channel_id=1, source_target_pairs={{0,2},{1,3},{2,0},{3,1},{4,6},{5,7},{6,4},{7,5},{8,10},{9,11},{10,... | collective-permute-start | bytes 491528 | tf_op jit(solution)/shard_map/ppermute | solution.py:33
  163.0 1.7 collective-permute-start.37
  167.9 1.4 collective-permute-start.42
  168.2 4.8 %collective-permute-start.38 = (bf16[4,32,2048]{2,1,0:T(8,128)(2,1)S(1)}, bf16[4,32,2048]{2,1,0:T(8,128)(2,1)S(1)}, u32[]{:S(2)}, u32[]{:S(2)}) collective-permute-start(bf16[4,32,2048]{2,1,0:T(8,128)(2,1)S(1)} %slice_bitcast_fusion), channel_id=1, source_target_pairs={{0,1},{1,0},{2,3},{3,2},{4,5},{5,4},{6,7},{7,6},{8,9},{9,8},{10,11... | collective-permute-start | bytes 1572872 | tf_op jit(solution)/shard_map/ppermute | solution.py:33
  169.4 6.6 %collective-permute-start.43 = (bf16[32,512]{1,0:T(8,128)(2,1)S(1)}, bf16[32,512]{1,0:T(8,128)(2,1)S(1)}, u32[]{:S(2)}, u32[]{:S(2)}) collective-permute-start(bf16[32,512]{1,0:T(8,128)(2,1)S(1)} %get-tuple-element.131), channel_id=1, source_target_pairs={{0,2},{1,3},{2,0},{3,1},{4,6},{5,7},{6,4},{7,5},{8,10},{9,11},{10,... | collective-permute-start | bytes 98312 | tf_op jit(solution)/shard_map/ppermute | solution.py:33
  170.9 5.7 %collective-permute-start.44 = (bf16[32,512]{1,0:T(8,128)(2,1)S(1)}, bf16[32,512]{1,0:T(8,128)(2,1)S(1)}, u32[]{:S(2)}, u32[]{:S(2)}) collective-permute-start(bf16[32,512]{1,0:T(8,128)(2,1)S(1)} %get-tuple-element.133), channel_id=1, source_target_pairs={{0,4},{1,5},{2,6},{3,7},{4,0},{5,1},{6,2},{7,3},{8,12},{9,13},{10,... | collective-permute-start | bytes 98312 | tf_op jit(solution)/shard_map/ppermute | solution.py:33
  172.2 5.3 %collective-permute-start.45 = (bf16[32,512]{1,0:T(8,128)(2,1)S(1)}, bf16[32,512]{1,0:T(8,128)(2,1)S(1)}, u32[]{:S(2)}, u32[]{:S(2)}) collective-permute-start(bf16[32,512]{1,0:T(8,128)(2,1)S(1)} %get-tuple-element.132), channel_id=1, source_target_pairs={{0,6},{1,7},{2,4},{3,5},{4,2},{5,3},{6,0},{7,1},{8,14},{9,15},{10,... | collective-permute-start | bytes 98312 | tf_op jit(solution)/shard_map/ppermute | solution.py:33
  173.1 5.9 %collective-permute-start.39 = (bf16[32,2048]{1,0:T(8,128)(2,1)S(1)}, bf16[32,2048]{1,0:T(8,128)(2,1)S(1)}, u32[]{:S(2)}, u32[]{:S(2)}) collective-permute-start(bf16[32,2048]{1,0:T(8,128)(2,1)S(1)} %get-tuple-element.122), channel_id=1, source_target_pairs={{0,2},{1,3},{2,0},{3,1},{4,6},{5,7},{6,4},{7,5},{8,10},{9,11},{10,... | collective-permute-start | bytes 393224 | tf_op jit(solution)/shard_map/ppermute | solution.py:33
  174.7 7.8 %collective-permute-start.40 = (bf16[32,2048]{1,0:T(8,128)(2,1)S(1)}, bf16[32,2048]{1,0:T(8,128)(2,1)S(1)}, u32[]{:S(2)}, u32[]{:S(2)}) collective-permute-start(bf16[32,2048]{1,0:T(8,128)(2,1)S(1)} %get-tuple-element.124), channel_id=1, source_target_pairs={{0,4},{1,5},{2,6},{3,7},{4,0},{5,1},{6,2},{7,3},{8,12},{9,13},{10,... | collective-permute-start | bytes 393224 | tf_op jit(solution)/shard_map/ppermute | solution.py:33
  175.9 6.5 %collective-permute-start.41 = (bf16[32,2048]{1,0:T(8,128)(2,1)S(1)}, bf16[32,2048]{1,0:T(8,128)(2,1)S(1)}, u32[]{:S(2)}, u32[]{:S(2)}) collective-permute-start(bf16[32,2048]{1,0:T(8,128)(2,1)S(1)} %get-tuple-element.123), channel_id=1, source_target_pairs={{0,6},{1,7},{2,4},{3,5},{4,2},{5,3},{6,0},{7,1},{8,14},{9,15},{10,... | collective-permute-start | bytes 393224 | tf_op jit(solution)/shard_map/ppermute | solution.py:33
  (16 other events, 120.7 us)
